TPU v7x, 128 devices: a whole 4x4x4 slice. The times are simulated.
128 devices in a mesh: section: 4 (over z_hi, core), space: 32 (over z_lo, y, x).
Axes of the slice: x: 4, y: 4, z: 4 (z_hi: 2, z_lo: 2; z = z_hi * 2 + z_lo), core: 2. Of those that a mesh axis runs over, the one named last changes fastest.
Arguments:
- carried: float32 [2, 3, 2, 4, 64, 512], P(None, None, None, None, 'space'), may hold values from -6 to 6
- source_field: float32 [2, 3, 2, 4, 64, 512], P(None, None, None, None, 'space'), may hold values from -6 to 6
- source_slice: int32 [4], replicated, may hold values from 0 to 3, as said below
- space_links: float32 [4, 3, 2, 3, 3, 64, 512], P('section', None, None, None, None, 'space'), may hold values from -2.5 to 2.5
- time_links: float32 [4, 2, 3, 3, 64, 512], P('section', None, None, None, 'space'), may hold values from -2.5 to 2.5
- magnetic: float32 [4, 3, 2, 3, 3, 64, 512], P('section', None, None, None, None, 'space'), may hold values from -4 to 4
Outputs:
- smeared: float32 [4, 2, 3, 2, 4, 64, 512], P('section', None, None, None, None, 'space')
Inputs may be any that keep to these rules, and one draw needn't show every extreme that they name: `source_slice`: every group number from 0 to 3 occurs among the columns.
All inputs are finite; a program needn't handle non-finite values.
Results may differ from a plain program's by a relative error of at most 0.00002.
Values sent between devices are 32-bit elements; how exact they have to be, the bound alone decides.
No kernel may reach another device: no remote copies, remote signals or barrier semaphores. Data moves between devices by JAX's collectives and lax.ppermute only.
A program may use at most 128 MiB of HBM per device.

v0:
```python
import jax
import jax.numpy as jnp
from jax import lax
from jax.experimental import pallas as pl
from jax.experimental.pallas import tpu as pltpu
from jax.sharding import PartitionSpec as P


LZ = 16
KINETIC = 1.0 / 6.0
QUARTIC = 1.0 / 216.0
SPIN_WEIGHT = 1.0 / 6.0
SMEAR_WEIGHT = 0.1
AXES = ("section", "space")
VMEM = pltpu.VMEM
PATH = (
    (1, 0), (0, 0), (0, 1), (1, 1), (1, 2), (0, 2), (0, 3), (1, 3),
    (2, 3), (3, 3), (3, 2), (2, 2), (2, 1), (3, 1), (3, 0), (2, 0),
)
BLOCKS = len(PATH)


def place(half, ring, block, core):
    x, y = PATH[block % BLOCKS]
    return (2 * half + core) * 32 + ring * 16 + y * 4 + x


def natural(half, turn, pair):
    return (2 * half + turn) * 32 + pair


def every():
    return [
        (half, ring, block, core)
        for half in range(2)
        for ring in range(2)
        for block in range(BLOCKS)
        for core in range(2)
    ]


def across():
    return [
        (place(h, r, m, c), place(h, r, m + 1, 0) if c else place(h, r, m - 1, 1))
        for h, r, m, c in every()
    ]


def sibling():
    return [(place(h, r, m, c), place(h, r, m, 1 - c)) for h, r, m, c in every()]


def onward():
    return [(place(h, r, m, c), place(1 - h, r, m, c)) for h, r, m, c in every()]


def spread(way):
    return [
        (natural(h, r ^ way, 2 * m + c), place(h, r, m, c)) for h, r, m, c in every()
    ]


def collect(way):
    return [(there, here) for here, there in spread(way)]


def rows_of(shape):
    return lax.broadcasted_iota(jnp.int32, shape, len(shape) - 2)


def lanes_of(shape):
    return lax.broadcasted_iota(jnp.int32, shape, len(shape) - 1)


def roll(value, by, axis):
    return pltpu.roll(value, by, value.ndim + axis)


def swap_planes(value):
    first = rows_of(value.shape) % 2 == 0
    return jnp.where(first, roll(value, 7, -2), roll(value, 1, -2))


def y_forward(value):
    moved = roll(value, 112, -1)
    return jnp.where(lanes_of(value.shape) < 112, moved, roll(moved, 6, -2))


def y_backward(value):
    moved = roll(value, 16, -1)
    return jnp.where(lanes_of(value.shape) >= 16, moved, roll(moved, 2, -2))


def z_forward(value):
    inside = lanes_of(value.shape) % LZ < LZ - 1
    return jnp.where(inside, roll(value, 127, -1), roll(value, LZ - 1, -1))


def z_backward(value):
    inside = lanes_of(value.shape) % LZ > 0
    return jnp.where(inside, roll(value, 1, -1), roll(value, 129 - LZ, -1))


def add(one, other):
    return [a + b for a, b in zip(one, other)]


def scaled(factor, field):
    return [factor * a for a in field]


def link_at(ref, base):
    def entry(row, column):
        return ref[base + 3 * row + column], ref[base + 9 + 3 * row + column]

    return entry


def product(entry, field, dagger, total=None):
    real, imag = [], []
    for out in range(3):
        sum_real = None if total is None else total[out]
        sum_imag = None if total is None else total[3 + out]
        for inner in range(3):
            link_real, link_imag = entry(inner, out) if dagger else entry(out, inner)
            field_real, field_imag = field[inner], field[3 + inner]
            cross_real, cross_imag = link_imag * field_imag, link_imag * field_real
            part_real, part_imag = link_real * field_real, link_real * field_imag
            if dagger:
                part_real, part_imag = part_real + cross_real, part_imag - cross_imag
            else:
                part_real, part_imag = part_real - cross_real, part_imag + cross_imag
            sum_real = part_real if sum_real is None else sum_real + part_real
            sum_imag = part_imag if sum_imag is None else sum_imag + part_imag
        real.append(sum_real)
        imag.append(sum_imag)
    return real + imag


INNER, ALONG_Y, ALONG_Z = 0, 18, 36


def within(links, field):
    total = scaled(-6.0, field)
    total = product(link_at(links, ALONG_Y), [y_forward(a) for a in field], False, total)
    back = product(link_at(links, ALONG_Y), field, True)
    total = add(total, [y_backward(a) for a in back])
    total = product(link_at(links, ALONG_Z), [z_forward(a) for a in field], False, total)
    back = product(link_at(links, ALONG_Z), field, True)
    total = add(total, [z_backward(a) for a in back])
    return product(link_at(links, INNER), [swap_planes(a) for a in field], False, total)


LADDER, LEVEL, TIME = 0, 18, 27


def level_entry(ref):
    def entry(row, column):
        if row == column:
            return ref[LEVEL + row], None
        slot = min(row, column) + max(row, column) - 1
        imag = ref[LEVEL + 6 + slot]
        return ref[LEVEL + 3 + slot], imag if row < column else -imag

    return entry


def hermitian_product(entry, field):
    real, imag = [], []
    for out in range(3):
        sum_real = sum_imag = None
        for inner in range(3):
            link_real, link_imag = entry(out, inner)
            part_real, part_imag = link_real * field[inner], link_real * field[3 + inner]
            if link_imag is not None:
                part_real = part_real - link_imag * field[3 + inner]
                part_imag = part_imag + link_imag * field[inner]
            sum_real = part_real if sum_real is None else sum_real + part_real
            sum_imag = part_imag if sum_imag is None else sum_imag + part_imag
        real.append(sum_real)
        imag.append(sum_imag)
    return real + imag


def spin_term(others, field):
    up, down = [a[0] for a in field], [a[1] for a in field]
    ladder, level = link_at(others, LADDER), level_entry(others)
    upper = add(hermitian_product(level, up), product(ladder, down, False))
    lower = product(ladder, up, True)
    lower = [a - b for a, b in zip(lower, hermitian_product(level, down))]
    return [jnp.stack([a, b]) for a, b in zip(upper, lower)]


def load(ref, column):
    return [ref[column, part] for part in range(6)]


def store(ref, column, field):
    for part in range(6):
        ref[column, part] = field[part]


def prepare(field, links, own_side, partial_ref, across_ref, sibling_ref, column):
    partial = within(links, field)
    store(partial_ref, column, partial)
    for part in range(6):
        turned = swap_planes(partial[part])
        across_ref[column, part] = jnp.where(own_side, field[part], turned)
        sibling_ref[column, part] = jnp.where(own_side, turned, field[part])


def two_laplacians(field, partial, from_across, from_sibling, links, outer, own_side):
    beyond = [
        swap_planes(jnp.where(own_side, s, a)) for a, s in zip(from_across, from_sibling)
    ]
    rim = [jnp.where(own_side, a, s) for a, s in zip(from_across, from_sibling)]
    single = product(link_at(outer, 0), beyond, False, partial)
    rim = product(link_at(outer, 0), field, True, rim)
    double = product(link_at(outer, 0), rim, False, within(links, single))
    return single, double


def kernel_call(body, inputs, outputs, pinned=True):
    if pinned:
        inputs = [pltpu.with_memory_space_constraint(value, VMEM) for value in inputs]
    spec = pl.BlockSpec(memory_space=VMEM)
    shapes = [VMEM(shape, jnp.float32) for shape in outputs]
    return pl.pallas_call(
        body,
        in_specs=[spec] * len(inputs),
        out_specs=[spec] * len(outputs),
        out_shape=shapes,
        compiler_params=pltpu.CompilerParams(vmem_limit_bytes=32 * 1024 * 1024),
    )(*inputs)


FIELD = (2, 6, 2, 8, 128)
SIDE, RING, HALF = 0, 1, 2


def first_message(carried, space, marks, message):
    core = marks[RING] > 0
    message[pl.ds(0, 54)] = space[...]
    for column in range(2):
        for part in range(6):
            for spin in range(2):
                picked = jnp.where(core, carried[part, spin, 2 + column], carried[part, spin, column])
                message[54 + column * 12 + part * 2 + spin] = picked


def second_message(source, magnetic, time, marks, message):
    core = marks[RING] > 0

    def raw(axis, imag, row, column):
        return magnetic[axis * 18 + imag * 9 + row * 3 + column]

    def real(axis, row, column):
        return 0.5 * (raw(axis, 0, row, column) + raw(axis, 0, column, row))

    def imag(axis, row, column):
        return 0.5 * (raw(axis, 1, row, column) - raw(axis, 1, column, row))

    for row in range(3):
        for column in range(3):
            at = LADDER + 3 * row + column
            message[at] = real(0, row, column) + imag(1, row, column)
            message[at + 9] = imag(0, row, column) - real(1, row, column)
        message[LEVEL + row] = real(2, row, row)
    for slot, (row, column) in enumerate(((0, 1), (0, 2), (1, 2))):
        message[LEVEL + 3 + slot] = real(2, row, column)
        message[LEVEL + 6 + slot] = imag(2, row, column)
    message[pl.ds(TIME, 18)] = time[...]
    for column in range(2):
        for part in range(6):
            for spin in range(2):
                picked = jnp.where(core, source[part, spin, 2 + column], source[part, spin, column])
                message[45 + column * 12 + part * 2 + spin] = picked


def arrange(got0, got1, marks, field, links_a, links_b, plain_a, plain_b, partial, to_across, to_sibling):
    ring = marks[RING] > 0
    own_side = marks[SIDE] > 0
    first = rows_of((8, 128)) % 2 == 0
    for turn, links, plain in ((0, links_a, plain_a), (1, links_b, plain_b)):
        for at in range(18, 54):
            one, other = (got0[at], got1[at]) if turn == 0 else (got1[at], got0[at])
            links[at] = jnp.where(ring, other, one)
        for at in range(18):
            one, other = (got0[at], got1[at]) if turn == 0 else (got1[at], got0[at])
            plain[at] = jnp.where(ring, other, one)
        for row in range(3):
            for column in range(3):
                at, turned = 3 * row + column, 3 * column + row
                links[at] = jnp.where(first, plain[at], swap_planes(plain[turned]))
                links[at + 9] = jnp.where(first, plain[at + 9], -swap_planes(plain[turned + 9]))
        for at in range(9):
            edge = jnp.where(first, swap_planes(plain[at + 9]), plain[at])
            to_across[24 + 9 * turn + at] = edge
            to_sibling[24 + 9 * turn + at] = edge

    def one_column(column, carry):
        values = [got0[pl.ds(54 + column * 12 + part * 2, 2)] for part in range(6)]
        store(field, column, values)
        total = within(links_a, values)
        store(partial, column, total)
        for part in range(6):
            turned = swap_planes(total[part])
            to_across[pl.ds(column * 12 + part * 2, 2)] = jnp.where(own_side, values[part], turned)
            to_sibling[pl.ds(column * 12 + part * 2, 2)] = jnp.where(own_side, turned, values[part])
        return carry

    lax.fori_loop(0, 2, one_column, 0)


def edges(from_across, from_sibling, plain_a, plain_b, got0, got1, marks, outer_a, outer_b, others_a, others_b):
    own_side = marks[SIDE] > 0
    ring = marks[RING] > 0
    first = rows_of((8, 128)) % 2 == 0
    upper_core = jnp.logical_xor(own_side, first)
    for turn, plain, outer in ((0, plain_a, outer_a), (1, plain_b, outer_b)):
        for row in range(3):
            for column in range(3):
                at, turned = 3 * row + column, 24 + 9 * turn + 3 * column + row
                edge = jnp.where(upper_core, from_sibling[turned], from_across[turned])
                outer[at] = jnp.where(first, swap_planes(edge), plain[at])
                outer[at + 9] = jnp.where(first, -edge, plain[at + 9])
    for at in range(45):
        others_a[at] = jnp.where(ring, got1[at], got0[at])
        others_b[at] = jnp.where(ring, got0[at], got1[at])


def step_a(field, partial, from_across, from_sibling, links, outer, others, own_side):
    single, double = two_laplacians(field, partial, from_across, from_sibling, links, outer, own_side)
    spin = spin_term(others, field)
    return [
        f + (0.5 * KINETIC) * s + (0.5 * QUARTIC) * d + (0.5 * SPIN_WEIGHT) * b
        for f, s, d, b in zip(field, single, double, spin)
    ]


def first_half(field, partial, from_across, from_sibling, links, outer, others, marks, *outs):
    turned_field, *messages = outs
    own_side = marks[SIDE] > 0

    def one_column(column, carry):
        values = step_a(
            load(field, column), load(partial, column), load(from_across, column),
            load(from_sibling, column), links, outer, others, own_side,
        )
        values = product(link_at(others, TIME), values, True)
        store(turned_field, column, values)
        prepare(values, links, own_side, *messages, column)
        return carry

    lax.fori_loop(0, 2, one_column, 0)


def second_half(field, partial, from_across, from_sibling, links, outer, others, source, marks, *rest):
    *after, result = rest[:-3] if len(rest) > 1 else rest
    messages = rest[-3:] if len(rest) > 1 else None
    own_side = marks[SIDE] > 0

    def one_column(column, carry):
        values = step_a(
            load(field, column), load(partial, column), load(from_across, column),
            load(from_sibling, column), links, outer, others, own_side,
        )
        values = add(values, load(source, column))
        store(result, column, values)
        if messages is not None:
            prepare(values, after[0], own_side, *messages, column)
        return carry

    lax.fori_loop(0, 2, one_column, 0)


def only_prepare(field, links, marks, *messages):
    own_side = marks[SIDE] > 0

    def one_column(column, carry):
        prepare(load(field, column), links, own_side, *messages, column)
        return carry

    lax.fori_loop(0, 2, one_column, 0)


def smear_start(early_a, early_b, late_a, late_b, links_a, links_b, marks, field_a, field_b, *messages):
    own_side = marks[SIDE] > 0
    half = marks[HALF] > 0
    for turn, early, late, links, field in (
        (0, early_a, late_a, links_a, field_a),
        (1, early_b, late_b, links_b, field_b),
    ):

        def one_column(column, carry):
            values = [jnp.where(half, b, a) for a, b in zip(load(early, column), load(late, column))]
            store(field, column, values)
            prepare(values, links, own_side, *[ref.at[turn] for ref in messages], column)
            return carry

        lax.fori_loop(0, 2, one_column, 0)


def smear_end(field_a, field_b, partial, from_across, from_sibling, links_a, links_b, outer_a, outer_b, marks, out0, out1):
    own_side = marks[SIDE] > 0
    ring = marks[RING] > 0

    def smeared(turn, field_ref, links, outer, column):
        field = load(field_ref, column)
        single, double = two_laplacians(
            field, load(partial.at[turn], column), load(from_across.at[turn], column),
            load(from_sibling.at[turn], column), links, outer, own_side,
        )
        return [
            f + (2 * SMEAR_WEIGHT) * s + (SMEAR_WEIGHT * SMEAR_WEIGHT) * d
            for f, s, d in zip(field, single, double)
        ]

    def one_column(column, carry):
        one = smeared(0, field_a, links_a, outer_a, column)
        other = smeared(1, field_b, links_b, outer_b, column)
        store(out0, column, [jnp.where(ring, b, a) for a, b in zip(one, other)])
        store(out1, column, [jnp.where(ring, a, b) for a, b in zip(one, other)])
        return carry

    lax.fori_loop(0, 2, one_column, 0)


def deliver(got0, got1, marks, out):
    core = marks[RING] > 0
    for column in range(2):
        for part in range(6):
            for spin in range(2):
                one, other = got0[column, part, spin], got1[column, part, spin]
                out[part, spin, column] = jnp.where(core, other, one)
                out[part, spin, 2 + column] = jnp.where(core, one, other)


def registers(value, lead):
    rows = value.reshape(lead + (2, 4, 128))
    return jnp.swapaxes(rows, -3, -2).reshape(lead + (8, 128))


def exchange(to_across, to_sibling):
    return lax.ppermute(to_across, AXES, across()), lax.ppermute(to_sibling, AXES, sibling())


def full(flag):
    return jnp.broadcast_to(flag.astype(jnp.float32), (8, 128))


def local(carried, source_field, source_slice, space_links, time_links, magnetic):
    section, space = lax.axis_index("section"), lax.axis_index("space")
    core, half, ring = section % 2, section // 2, space // 16
    first = (jnp.arange(8) % 2)[:, None] == core
    side = jnp.broadcast_to(first.astype(jnp.float32), (8, 128))
    marks = jnp.stack([side, full(ring == 1), full(half == 1)])
    core_marks = jnp.stack([side, full(core == 1), full(half == 1)])

    carried = registers(carried, (6, 2, 4))
    source_field = registers(source_field, (6, 2, 4))
    space_links = registers(space_links, (54,))
    time_links = registers(time_links, (18,))
    magnetic = registers(magnetic, (54,))

    (message,) = kernel_call(first_message, [carried, space_links, core_marks], [(78, 8, 128)], False)
    got0 = lax.ppermute(message, AXES, spread(0))
    got1 = lax.ppermute(message[:54], AXES, spread(1))
    (message,) = kernel_call(
        second_message, [source_field, magnetic, time_links, core_marks], [(69, 8, 128)], False
    )
    more0 = lax.ppermute(message, AXES, spread(0))
    more1 = lax.ppermute(message[:45], AXES, spread(1))

    field, links_a, links_b, plain_a, plain_b, partial, to_across, to_sibling = kernel_call(
        arrange,
        [got0, got1, marks],
        [FIELD, (54, 8, 128), (54, 8, 128), (18, 8, 128), (18, 8, 128), FIELD, (42, 8, 128), (42, 8, 128)],
    )
    from_across, from_sibling = exchange(to_across, to_sibling)
    outer_a, outer_b, others_a, others_b = kernel_call(
        edges,
        [from_across, from_sibling, plain_a, plain_b, more0, more1, marks],
        [(18, 8, 128), (18, 8, 128), (45, 8, 128), (45, 8, 128)],
    )
    from_across = from_across[:24].reshape(FIELD)
    from_sibling = from_sibling[:24].reshape(FIELD)
    source = more0[45:].reshape(FIELD)
    here = lax.dynamic_slice_in_dim(source_slice, 2 * ring, 2)
    sources = [
        jnp.where(here == 2 * half + turn, 1.0, 0.0).astype(jnp.float32).reshape(2, 1, 1, 1, 1) * source
        for turn in range(2)
    ]
    links, outer, others = (links_a, links_b), (outer_a, outer_b), (others_a, others_b)
    results = []
    for phase in range(2):
        for turn in range(2):
            field, partial, to_across, to_sibling = kernel_call(
                first_half,
                [field, partial, from_across, from_sibling, links[turn], outer[turn], others[turn], marks],
                [FIELD] * 4,
            )
            from_across, from_sibling = exchange(to_across, to_sibling)
            inputs = [field, partial, from_across, from_sibling, links[turn], outer[turn], others[turn]]
            inputs += [sources[turn], marks]
            if turn == 0:
                field, partial, to_across, to_sibling = kernel_call(
                    second_half, inputs + [links[1]], [FIELD] * 4
                )
                from_across, from_sibling = exchange(to_across, to_sibling)
            else:
                (field,) = kernel_call(second_half, inputs, [FIELD])
            results.append(field)
        if phase == 0:
            field = lax.ppermute(field, AXES, onward())
            partial, to_across, to_sibling = kernel_call(
                only_prepare, [field, links_a, marks], [FIELD] * 3
            )
            from_across, from_sibling = exchange(to_across, to_sibling)

    both = (2,) + FIELD
    field_a, field_b, partial, to_across, to_sibling = kernel_call(
        smear_start, results + [links_a, links_b, marks], [FIELD, FIELD, both, both, both]
    )
    from_across, from_sibling = exchange(to_across, to_sibling)
    out0, out1 = kernel_call(
        smear_end,
        [field_a, field_b, partial, from_across, from_sibling, links_a, links_b, outer_a, outer_b, marks],
        [FIELD, FIELD],
    )
    out0 = lax.ppermute(out0, AXES, collect(0))
    out1 = lax.ppermute(out1, AXES, collect(1))
    (out,) = kernel_call(deliver, [out0, out1, core_marks], [(6, 2, 4, 8, 128)])
    out = jnp.swapaxes(out.reshape(2, 3, 2, 4, 4, 2, 128), -3, -2)
    return out.reshape(1, 2, 3, 2, 4, 2, 512)


def solution(mesh):
    return jax.shard_map(
        local,
        mesh=mesh,
        in_specs=(
            P(None, None, None, None, "space", None),
            P(None, None, None, None, "space", None),
            P(),
            P("section", None, None, None, None, "space", None),
            P("section", None, None, None, "space", None),
            P("section", None, None, None, None, "space", None),
        ),
        out_specs=P("section", None, None, None, None, "space", None),
        check_vma=False,
    )
```

profile of v0, /device:TPU:32, one launch (start us, length us, event | category | flops | bytes accessed | tf_op | source)
XLA Modules:
  0.0 114.3 jit_solution(14252857723075764719)
XLA Ops:
  0.4 0.9 copy-done.1
  1.3 0.9 copy-done.3
  2.3 7.1 %collective-permute-start = (f32[78,8,128]{2,1,0:T(8,128)S(1)}, f32[78,8,128]{2,1,0:T(8,128)S(1)}, u32[]{:S(2)}, u32[]{:S(2)}) collective-permute-start(f32[78,8,128]{2,1,0:T(8,128)S(1)} %shard_map.64), channel_id=1, source_target_pairs={{0,1},{1,33},{2,0},{3,32},{4,4},{5,36},{6,5},{7,37},{8,9},{9,41},{... | collective-permute-start | bytes 958472 | tf_op jit(solution)/shard_map/ppermute | solution.py:467
  9.4 2.4 %collective-permute-start.1 = (f32[54,8,128]{2,1,0:T(8,128)S(1)}, f32[54,8,128]{2,1,0:T(8,128)S(1)}, u32[]{:S(2)}, u32[]{:S(2)}) collective-permute-start(f32[54,8,128]{2,1,0:T(8,128)S(1)} %slice.20), channel_id=1, source_target_pairs={{32,1},{33,33},{34,0},{35,32},{36,4},{37,36},{38,5},{39,37},{40,9}... | collective-permute-start | bytes 663560 | tf_op jit(solution)/shard_map/ppermute | solution.py:468
  11.8 4.1 %collective-permute-start.4 = (f32[69,8,128]{2,1,0:T(8,128)S(1)}, f32[69,8,128]{2,1,0:T(8,128)S(1)}, u32[]{:S(2)}, u32[]{:S(2)}) collective-permute-start(f32[69,8,128]{2,1,0:T(8,128)S(1)} %shard_map.66), channel_id=1, source_target_pairs={{0,1},{1,33},{2,0},{3,32},{4,4},{5,36},{6,5},{7,37},{8,9},{9,41},{... | collective-permute-start | bytes 847880 | tf_op jit(solution)/shard_map/ppermute | solution.py:472
  16.0 6.4 %collective-permute-start.5 = (f32[45,8,128]{2,1,0:T(8,128)S(1)}, f32[45,8,128]{2,1,0:T(8,128)S(1)}, u32[]{:S(2)}, u32[]{:S(2)}) collective-permute-start(f32[45,8,128]{2,1,0:T(8,128)S(1)} %slice.23), channel_id=1, source_target_pairs={{32,1},{33,33},{34,0},{35,32},{36,4},{37,36},{38,5},{39,37},{40,9}... | collective-permute-start | bytes 552968 | tf_op jit(solution)/shard_map/ppermute | solution.py:473
  22.4 0.4 shard_map.65
  22.8 20.2 %collective-permute-start.2 = (f32[42,8,128]{2,1,0:T(8,128)S(1)}, f32[42,8,128]{2,1,0:T(8,128)S(1)}, u32[]{:S(2)}, u32[]{:S(2)}) collective-permute-start(f32[42,8,128]{2,1,0:T(8,128)S(1)} %get-tuple-element.53), channel_id=1, source_target_pairs={{1,34},{33,0},{0,33},{32,4},{4,32},{36,5},{5,36},{37,9},{9,37},{41... | collective-permute-start | bytes 516104 | tf_op jit(solution)/shard_map/ppermute | solution.py:445
  43.0 0.7 collective-permute-start.3
  43.7 0.7 copy-done.6
  44.4 1.6 %collective-permute-done.2.from_across = f32[42,8,128]{2,1,0:T(8,128)S(1)} collective-permute-done((f32[42,8,128]{2,1,0:T(8,128)S(1)}, f32[42,8,128]{2,1,0:T(8,128)S(1)}, u32[]{:S(2)}, u32[]{:S(2)}) %collective-permute-start.2) | collective-permute-done | bytes 172064 | tf_op jit(solution)/shard_map/ppermute | solution.py:445
  46.2 0.9 shard_map.68
  47.1 6.5 %collective-permute-start.6 = (f32[2,6,2,8,128]{4,3,2,1,0:T(8,128)S(1)}, f32[2,6,2,8,128]{4,3,2,1,0:T(8,128)S(1)}, u32[]{:S(2)}, u32[]{:S(2)}) collective-permute-start(f32[2,6,2,8,128]{4,3,2,1,0:T(8,128)S(1)} %get-tuple-element.62), channel_id=1, source_target_pairs={{1,34},{33,0},{0,33},{32,4},{4,32},{36,5},{5,36},{37,9},{9,37},{41... | collective-permute-start | bytes 294920 | tf_op jit(solution)/shard_map/ppermute | solution.py:445
  53.5 0.7 collective-permute-start.7
  54.4 1.5 %collective-permute-done.6.from_across = f32[2,6,2,8,128]{4,3,2,1,0:T(8,128)S(1)} collective-permute-done((f32[2,6,2,8,128]{4,3,2,1,0:T(8,128)S(1)}, f32[2,6,2,8,128]{4,3,2,1,0:T(8,128)S(1)}, u32[]{:S(2)}, u32[]{:S(2)}) %collective-permute-start.6) | collective-permute-done | bytes 98336 | tf_op jit(solution)/shard_map/ppermute | solution.py:445
  55.9 0.8 shard_map.69
  56.7 3.0 %collective-permute-start.8 = (f32[2,6,2,8,128]{4,3,2,1,0:T(8,128)S(1)}, f32[2,6,2,8,128]{4,3,2,1,0:T(8,128)S(1)}, u32[]{:S(2)}, u32[]{:S(2)}) collective-permute-start(f32[2,6,2,8,128]{4,3,2,1,0:T(8,128)S(1)} %get-tuple-element.67), channel_id=1, source_target_pairs={{1,34},{33,0},{0,33},{32,4},{4,32},{36,5},{5,36},{37,9},{9,37},{41... | collective-permute-start | bytes 294920 | tf_op jit(solution)/shard_map/ppermute | solution.py:445
  59.7 2.3 %collective-permute-done.8.from_across = f32[2,6,2,8,128]{4,3,2,1,0:T(8,128)S(1)} collective-permute-done((f32[2,6,2,8,128]{4,3,2,1,0:T(8,128)S(1)}, f32[2,6,2,8,128]{4,3,2,1,0:T(8,128)S(1)}, u32[]{:S(2)}, u32[]{:S(2)}) %collective-permute-start.8) | collective-permute-done | bytes 98336 | tf_op jit(solution)/shard_map/ppermute | solution.py:445
  62.0 0.9 shard_map.70
  62.9 2.1 %collective-permute-start.10 = (f32[2,6,2,8,128]{4,3,2,1,0:T(8,128)S(1)}, f32[2,6,2,8,128]{4,3,2,1,0:T(8,128)S(1)}, u32[]{:S(2)}, u32[]{:S(2)}) collective-permute-start(f32[2,6,2,8,128]{4,3,2,1,0:T(8,128)S(1)} %get-tuple-element.73), channel_id=1, source_target_pairs={{1,34},{33,0},{0,33},{32,4},{4,32},{36,5},{5,36},{37,9},{9,37},{41... | collective-permute-start | bytes 294920 | tf_op jit(solution)/shard_map/ppermute | solution.py:445
  65.0 2.3 %collective-permute-done.10.from_across = f32[2,6,2,8,128]{4,3,2,1,0:T(8,128)S(1)} collective-permute-done((f32[2,6,2,8,128]{4,3,2,1,0:T(8,128)S(1)}, f32[2,6,2,8,128]{4,3,2,1,0:T(8,128)S(1)}, u32[]{:S(2)}, u32[]{:S(2)}) %collective-permute-start.10) | collective-permute-done | bytes 98336 | tf_op jit(solution)/shard_map/ppermute | solution.py:445
  67.3 0.5 shard_map.71.early_b
  67.9 3.1 %collective-permute-start.12 = (f32[2,6,2,8,128]{4,3,2,1,0:T(8,128)S(1)}, f32[2,6,2,8,128]{4,3,2,1,0:T(8,128)S(1)}, u32[]{:S(2)}, u32[]{:S(2)}) collective-permute-start(f32[2,6,2,8,128]{4,3,2,1,0:T(8,128)S(1)} %shard_map.71.early_b), channel_id=1, source_target_pairs={{1,65},{33,97},{0,64},{32,96},{4,68},{36,100},{5,69},{37,101},{9,7... | collective-permute-start | bytes 294920 | tf_op jit(solution)/shard_map/ppermute | solution.py:515
  70.9 3.1 %collective-permute-done.12.field = f32[2,6,2,8,128]{4,3,2,1,0:T(8,128)S(1)} collective-permute-done((f32[2,6,2,8,128]{4,3,2,1,0:T(8,128)S(1)}, f32[2,6,2,8,128]{4,3,2,1,0:T(8,128)S(1)}, u32[]{:S(2)}, u32[]{:S(2)}) %collective-permute-start.12) | collective-permute-done | bytes 98336 | tf_op jit(solution)/shard_map/ppermute | solution.py:515
  74.1 0.3 shard_map.72
  74.4 1.0 collective-permute-start.13
  75.4 0.3 collective-permute-start.14
  75.7 2.9 %collective-permute-done.13.from_across = f32[2,6,2,8,128]{4,3,2,1,0:T(8,128)S(1)} collective-permute-done((f32[2,6,2,8,128]{4,3,2,1,0:T(8,128)S(1)}, f32[2,6,2,8,128]{4,3,2,1,0:T(8,128)S(1)}, u32[]{:S(2)}, u32[]{:S(2)}) %collective-permute-start.13) | collective-permute-done | bytes 98336 | tf_op jit(solution)/shard_map/ppermute | solution.py:445
  78.5 0.9 shard_map.73
  79.5 1.0 collective-permute-start.15
  80.4 0.3 collective-permute-start.16
  80.7 2.9 %collective-permute-done.15.from_across = f32[2,6,2,8,128]{4,3,2,1,0:T(8,128)S(1)} collective-permute-done((f32[2,6,2,8,128]{4,3,2,1,0:T(8,128)S(1)}, f32[2,6,2,8,128]{4,3,2,1,0:T(8,128)S(1)}, u32[]{:S(2)}, u32[]{:S(2)}) %collective-permute-start.15) | collective-permute-done | bytes 98336 | tf_op jit(solution)/shard_map/ppermute | solution.py:445
  83.6 0.8 shard_map.74
  84.4 1.0 collective-permute-start.17
  85.6 2.9 %collective-permute-done.17.from_across = f32[2,6,2,8,128]{4,3,2,1,0:T(8,128)S(1)} collective-permute-done((f32[2,6,2,8,128]{4,3,2,1,0:T(8,128)S(1)}, f32[2,6,2,8,128]{4,3,2,1,0:T(8,128)S(1)}, u32[]{:S(2)}, u32[]{:S(2)}) %collective-permute-start.17) | collective-permute-done | bytes 98336 | tf_op jit(solution)/shard_map/ppermute | solution.py:445
  88.5 0.9 shard_map.75
  89.4 1.0 collective-permute-start.19
  90.7 2.9 %collective-permute-done.19.from_across = f32[2,6,2,8,128]{4,3,2,1,0:T(8,128)S(1)} collective-permute-done((f32[2,6,2,8,128]{4,3,2,1,0:T(8,128)S(1)}, f32[2,6,2,8,128]{4,3,2,1,0:T(8,128)S(1)}, u32[]{:S(2)}, u32[]{:S(2)}) %collective-permute-start.19) | collective-permute-done | bytes 98336 | tf_op jit(solution)/shard_map/ppermute | solution.py:445
  93.5 0.5 shard_map.76.late_b
  94.1 0.7 shard_map.77
  94.7 1.0 collective-permute-start.21
  96.0 3.9 %collective-permute-done.21.from_across = f32[2,2,6,2,8,128]{5,4,3,2,1,0:T(8,128)S(1)} collective-permute-done((f32[2,2,6,2,8,128]{5,4,3,2,1,0:T(8,128)S(1)}, f32[2,2,6,2,8,128]{5,4,3,2,1,0:T(8,128)S(1)}, u32[]{:S(2)}, u32[]{:S(2)}) %collective-permute-start.21) | collective-permute-done | bytes 196640 | tf_op jit(solution)/shard_map/ppermute | solution.py:445
  99.9 0.8 shard_map.78
  100.7 2.7 %collective-permute-start.23 = (f32[2,6,2,8,128]{4,3,2,1,0:T(8,128)S(1)}, f32[2,6,2,8,128]{4,3,2,1,0:T(8,128)S(1)}, u32[]{:S(2)}, u32[]{:S(2)}) collective-permute-start(f32[2,6,2,8,128]{4,3,2,1,0:T(8,128)S(1)} %get-tuple-element.95), channel_id=1, source_target_pairs={{1,0},{33,1},{0,2},{32,3},{4,4},{36,5},{5,6},{37,7},{9,8},{41,9},{... | collective-permute-start | bytes 294920 | tf_op jit(solution)/shard_map/ppermute | solution.py:531
  103.5 5.5 %collective-permute-start.24 = (f32[2,6,2,8,128]{4,3,2,1,0:T(8,128)S(1)}, f32[2,6,2,8,128]{4,3,2,1,0:T(8,128)S(1)}, u32[]{:S(2)}, u32[]{:S(2)}) collective-permute-start(f32[2,6,2,8,128]{4,3,2,1,0:T(8,128)S(1)} %get-tuple-element.96), channel_id=1, source_target_pairs={{1,32},{33,33},{0,34},{32,35},{4,36},{36,37},{5,38},{37,39},{9,40}... | collective-permute-start | bytes 294920 | tf_op jit(solution)/shard_map/ppermute | solution.py:532
  109.0 2.8 %collective-permute-done.23.got0 = f32[2,6,2,8,128]{4,3,2,1,0:T(8,128)S(1)} collective-permute-done((f32[2,6,2,8,128]{4,3,2,1,0:T(8,128)S(1)}, f32[2,6,2,8,128]{4,3,2,1,0:T(8,128)S(1)}, u32[]{:S(2)}, u32[]{:S(2)}) %collective-permute-start.23) | collective-permute-done | bytes 98336 | tf_op jit(solution)/shard_map/ppermute | solution.py:531
  111.8 1.9 %collective-permute-done.24.got1 = f32[2,6,2,8,128]{4,3,2,1,0:T(8,128)S(1)} collective-permute-done((f32[2,6,2,8,128]{4,3,2,1,0:T(8,128)S(1)}, f32[2,6,2,8,128]{4,3,2,1,0:T(8,128)S(1)}, u32[]{:S(2)}, u32[]{:S(2)}) %collective-permute-start.24) | collective-permute-done | bytes 98336 | tf_op jit(solution)/shard_map/ppermute | solution.py:532
  113.6 0.7 copy.13
  (47 shorter events, 1.6 us)
Async XLA Ops:
  0.4 0.9 copy-start.1
  1.3 0.9 copy-start.3
  2.2 9.5 %copy-start.5 = (f32[1,2,3,3,2,512]{5,4,3,2,1,0:T(2,128)S(1)}, f32[1,2,3,3,2,512]{5,4,3,2,1,0:T(2,128)}, u32[]{:S(2)}) copy-start(f32[1,2,3,3,2,512]{5,4,3,2,1,0:T(2,128)} %param.10) | copy-start | bytes 221188
  2.3 9.5 %copy-start.2 = (f32[1,3,2,3,3,2,512]{6,5,4,3,2,1,0:T(2,128)S(1)}, f32[1,3,2,3,3,2,512]{6,5,4,3,2,1,0:T(2,128)}, u32[]{:S(2)}) copy-start(f32[1,3,2,3,3,2,512]{6,5,4,3,2,1,0:T(2,128)} %param.11) | copy-start | bytes 663556
  2.3 9.5 %copy-start.4 = (f32[2,3,2,4,2,512]{5,4,3,2,1,0:T(2,128)S(1)}, f32[2,3,2,4,2,512]{5,4,3,2,1,0:T(2,128)}, u32[]{:S(2)}) copy-start(f32[2,3,2,4,2,512]{5,4,3,2,1,0:T(2,128)} %param.7) | copy-start | bytes 589828
  2.3 20.0 %collective-permute-start = (f32[78,8,128]{2,1,0:T(8,128)S(1)}, f32[78,8,128]{2,1,0:T(8,128)S(1)}, u32[]{:S(2)}, u32[]{:S(2)}) collective-permute-start(f32[78,8,128]{2,1,0:T(8,128)S(1)} %shard_map.64), channel_id=1, source_target_pairs={{0,1},{1,33},{2,0},{3,32},{4,4},{5,36},{6,5},{7,37},{8,9},{9,41},{... | collective-permute-start | bytes 958472 | tf_op jit(solution)/shard_map/ppermute | solution.py:467
  9.4 12.9 %collective-permute-start.1 = (f32[54,8,128]{2,1,0:T(8,128)S(1)}, f32[54,8,128]{2,1,0:T(8,128)S(1)}, u32[]{:S(2)}, u32[]{:S(2)}) collective-permute-start(f32[54,8,128]{2,1,0:T(8,128)S(1)} %slice.20), channel_id=1, source_target_pairs={{32,1},{33,33},{34,0},{35,32},{36,4},{37,36},{38,5},{39,37},{40,9}... | collective-permute-start | bytes 663560 | tf_op jit(solution)/shard_map/ppermute | solution.py:468
  11.8 32.6 %collective-permute-start.4 = (f32[69,8,128]{2,1,0:T(8,128)S(1)}, f32[69,8,128]{2,1,0:T(8,128)S(1)}, u32[]{:S(2)}, u32[]{:S(2)}) collective-permute-start(f32[69,8,128]{2,1,0:T(8,128)S(1)} %shard_map.66), channel_id=1, source_target_pairs={{0,1},{1,33},{2,0},{3,32},{4,4},{5,36},{6,5},{7,37},{8,9},{9,41},{... | collective-permute-start | bytes 847880 | tf_op jit(solution)/shard_map/ppermute | solution.py:472
  16.0 30.1 %collective-permute-start.5 = (f32[45,8,128]{2,1,0:T(8,128)S(1)}, f32[45,8,128]{2,1,0:T(8,128)S(1)}, u32[]{:S(2)}, u32[]{:S(2)}) collective-permute-start(f32[45,8,128]{2,1,0:T(8,128)S(1)} %slice.23), channel_id=1, source_target_pairs={{32,1},{33,33},{34,0},{35,32},{36,4},{37,36},{38,5},{39,37},{40,9}... | collective-permute-start | bytes 552968 | tf_op jit(solution)/shard_map/ppermute | solution.py:473
  22.8 23.3 %collective-permute-start.2 = (f32[42,8,128]{2,1,0:T(8,128)S(1)}, f32[42,8,128]{2,1,0:T(8,128)S(1)}, u32[]{:S(2)}, u32[]{:S(2)}) collective-permute-start(f32[42,8,128]{2,1,0:T(8,128)S(1)} %get-tuple-element.53), channel_id=1, source_target_pairs={{1,34},{33,0},{0,33},{32,4},{4,32},{36,5},{5,36},{37,9},{9,37},{41... | collective-permute-start | bytes 516104 | tf_op jit(solution)/shard_map/ppermute | solution.py:445
  43.0 3.1 %collective-permute-start.3 = (f32[42,8,128]{2,1,0:T(8,128)S(1)}, f32[42,8,128]{2,1,0:T(8,128)S(1)}, u32[]{:S(2)}, u32[]{:S(2)}) collective-permute-start(f32[42,8,128]{2,1,0:T(8,128)S(1)} %get-tuple-element.54), channel_id=1, source_target_pairs={{1,33},{33,1},{0,32},{32,0},{4,36},{36,4},{5,37},{37,5},{9,41},{41... | collective-permute-start | bytes 516104 | tf_op jit(solution)/shard_map/ppermute | solution.py:445
  43.7 0.7 copy-start.6
  44.4 1.7 %copy-start = (f32[69,8,128]{2,1,0:T(8,128)}, f32[69,8,128]{2,1,0:T(8,128)S(1)}, u32[]{:S(2)}) copy-start(f32[69,8,128]{2,1,0:T(8,128)S(1)} %collective-permute-done.4.got0) | copy-start | bytes 847876
  46.2 8.1 %slice-start = ((f32[69,8,128]{2,1,0:T(8,128)}), f32[24,8,128]{2,1,0:T(8,128)S(1)}, s32[]{:S(2)}) async-start(f32[69,8,128]{2,1,0:T(8,128)} %copy-done), calls=%async_computation | async-start | bytes 196608 | tf_op jit(solution)/shard_map/slice | solution.py:488
  47.1 8.8 %collective-permute-start.6 = (f32[2,6,2,8,128]{4,3,2,1,0:T(8,128)S(1)}, f32[2,6,2,8,128]{4,3,2,1,0:T(8,128)S(1)}, u32[]{:S(2)}, u32[]{:S(2)}) collective-permute-start(f32[2,6,2,8,128]{4,3,2,1,0:T(8,128)S(1)} %get-tuple-element.62), channel_id=1, source_target_pairs={{1,34},{33,0},{0,33},{32,4},{4,32},{36,5},{5,36},{37,9},{9,37},{41... | collective-permute-start | bytes 294920 | tf_op jit(solution)/shard_map/ppermute | solution.py:445
  53.5 2.3 %collective-permute-start.7 = (f32[2,6,2,8,128]{4,3,2,1,0:T(8,128)S(1)}, f32[2,6,2,8,128]{4,3,2,1,0:T(8,128)S(1)}, u32[]{:S(2)}, u32[]{:S(2)}) collective-permute-start(f32[2,6,2,8,128]{4,3,2,1,0:T(8,128)S(1)} %get-tuple-element.63), channel_id=1, source_target_pairs={{1,33},{33,1},{0,32},{32,0},{4,36},{36,4},{5,37},{37,5},{9,41},{41... | collective-permute-start | bytes 294920 | tf_op jit(solution)/shard_map/ppermute | solution.py:445
  56.7 5.3 %collective-permute-start.8 = (f32[2,6,2,8,128]{4,3,2,1,0:T(8,128)S(1)}, f32[2,6,2,8,128]{4,3,2,1,0:T(8,128)S(1)}, u32[]{:S(2)}, u32[]{:S(2)}) collective-permute-start(f32[2,6,2,8,128]{4,3,2,1,0:T(8,128)S(1)} %get-tuple-element.67), channel_id=1, source_target_pairs={{1,34},{33,0},{0,33},{32,4},{4,32},{36,5},{5,36},{37,9},{9,37},{41... | collective-permute-start | bytes 294920 | tf_op jit(solution)/shard_map/ppermute | solution.py:445
  59.7 2.3 %collective-permute-start.9 = (f32[2,6,2,8,128]{4,3,2,1,0:T(8,128)S(1)}, f32[2,6,2,8,128]{4,3,2,1,0:T(8,128)S(1)}, u32[]{:S(2)}, u32[]{:S(2)}) collective-permute-start(f32[2,6,2,8,128]{4,3,2,1,0:T(8,128)S(1)} %get-tuple-element.68), channel_id=1, source_target_pairs={{1,33},{33,1},{0,32},{32,0},{4,36},{36,4},{5,37},{37,5},{9,41},{41... | collective-permute-start | bytes 294920 | tf_op jit(solution)/shard_map/ppermute | solution.py:445
  62.9 4.4 %collective-permute-start.10 = (f32[2,6,2,8,128]{4,3,2,1,0:T(8,128)S(1)}, f32[2,6,2,8,128]{4,3,2,1,0:T(8,128)S(1)}, u32[]{:S(2)}, u32[]{:S(2)}) collective-permute-start(f32[2,6,2,8,128]{4,3,2,1,0:T(8,128)S(1)} %get-tuple-element.73), channel_id=1, source_target_pairs={{1,34},{33,0},{0,33},{32,4},{4,32},{36,5},{5,36},{37,9},{9,37},{41... | collective-permute-start | bytes 294920 | tf_op jit(solution)/shard_map/ppermute | solution.py:445
  65.0 2.3 %collective-permute-start.11 = (f32[2,6,2,8,128]{4,3,2,1,0:T(8,128)S(1)}, f32[2,6,2,8,128]{4,3,2,1,0:T(8,128)S(1)}, u32[]{:S(2)}, u32[]{:S(2)}) collective-permute-start(f32[2,6,2,8,128]{4,3,2,1,0:T(8,128)S(1)} %get-tuple-element.74), channel_id=1, source_target_pairs={{1,33},{33,1},{0,32},{32,0},{4,36},{36,4},{5,37},{37,5},{9,41},{41... | collective-permute-start | bytes 294920 | tf_op jit(solution)/shard_map/ppermute | solution.py:445
  67.9 6.2 %collective-permute-start.12 = (f32[2,6,2,8,128]{4,3,2,1,0:T(8,128)S(1)}, f32[2,6,2,8,128]{4,3,2,1,0:T(8,128)S(1)}, u32[]{:S(2)}, u32[]{:S(2)}) collective-permute-start(f32[2,6,2,8,128]{4,3,2,1,0:T(8,128)S(1)} %shard_map.71.early_b), channel_id=1, source_target_pairs={{1,65},{33,97},{0,64},{32,96},{4,68},{36,100},{5,69},{37,101},{9,7... | collective-permute-start | bytes 294920 | tf_op jit(solution)/shard_map/ppermute | solution.py:515
  74.4 4.1 %collective-permute-start.13 = (f32[2,6,2,8,128]{4,3,2,1,0:T(8,128)S(1)}, f32[2,6,2,8,128]{4,3,2,1,0:T(8,128)S(1)}, u32[]{:S(2)}, u32[]{:S(2)}) collective-permute-start(f32[2,6,2,8,128]{4,3,2,1,0:T(8,128)S(1)} %get-tuple-element.76), channel_id=1, source_target_pairs={{1,34},{33,0},{0,33},{32,4},{4,32},{36,5},{5,36},{37,9},{9,37},{41... | collective-permute-start | bytes 294920 | tf_op jit(solution)/shard_map/ppermute | solution.py:445
  75.4 3.2 %collective-permute-start.14 = (f32[2,6,2,8,128]{4,3,2,1,0:T(8,128)S(1)}, f32[2,6,2,8,128]{4,3,2,1,0:T(8,128)S(1)}, u32[]{:S(2)}, u32[]{:S(2)}) collective-permute-start(f32[2,6,2,8,128]{4,3,2,1,0:T(8,128)S(1)} %get-tuple-element.77), channel_id=1, source_target_pairs={{1,33},{33,1},{0,32},{32,0},{4,36},{36,4},{5,37},{37,5},{9,41},{41... | collective-permute-start | bytes 294920 | tf_op jit(solution)/shard_map/ppermute | solution.py:445
  79.5 4.1 %collective-permute-start.15 = (f32[2,6,2,8,128]{4,3,2,1,0:T(8,128)S(1)}, f32[2,6,2,8,128]{4,3,2,1,0:T(8,128)S(1)}, u32[]{:S(2)}, u32[]{:S(2)}) collective-permute-start(f32[2,6,2,8,128]{4,3,2,1,0:T(8,128)S(1)} %get-tuple-element.80), channel_id=1, source_target_pairs={{1,34},{33,0},{0,33},{32,4},{4,32},{36,5},{5,36},{37,9},{9,37},{41... | collective-permute-start | bytes 294920 | tf_op jit(solution)/shard_map/ppermute | solution.py:445
  80.4 3.2 %collective-permute-start.16 = (f32[2,6,2,8,128]{4,3,2,1,0:T(8,128)S(1)}, f32[2,6,2,8,128]{4,3,2,1,0:T(8,128)S(1)}, u32[]{:S(2)}, u32[]{:S(2)}) collective-permute-start(f32[2,6,2,8,128]{4,3,2,1,0:T(8,128)S(1)} %get-tuple-element.81), channel_id=1, source_target_pairs={{1,33},{33,1},{0,32},{32,0},{4,36},{36,4},{5,37},{37,5},{9,41},{41... | collective-permute-start | bytes 294920 | tf_op jit(solution)/shard_map/ppermute | solution.py:445
  84.4 4.1 %collective-permute-start.17 = (f32[2,6,2,8,128]{4,3,2,1,0:T(8,128)S(1)}, f32[2,6,2,8,128]{4,3,2,1,0:T(8,128)S(1)}, u32[]{:S(2)}, u32[]{:S(2)}) collective-permute-start(f32[2,6,2,8,128]{4,3,2,1,0:T(8,128)S(1)} %get-tuple-element.84), channel_id=1, source_target_pairs={{1,34},{33,0},{0,33},{32,4},{4,32},{36,5},{5,36},{37,9},{9,37},{41... | collective-permute-start | bytes 294920 | tf_op jit(solution)/shard_map/ppermute | solution.py:445
  85.4 3.2 %collective-permute-start.18 = (f32[2,6,2,8,128]{4,3,2,1,0:T(8,128)S(1)}, f32[2,6,2,8,128]{4,3,2,1,0:T(8,128)S(1)}, u32[]{:S(2)}, u32[]{:S(2)}) collective-permute-start(f32[2,6,2,8,128]{4,3,2,1,0:T(8,128)S(1)} %get-tuple-element.85), channel_id=1, source_target_pairs={{1,33},{33,1},{0,32},{32,0},{4,36},{36,4},{5,37},{37,5},{9,41},{41... | collective-permute-start | bytes 294920 | tf_op jit(solution)/shard_map/ppermute | solution.py:445
  89.4 4.1 %collective-permute-start.19 = (f32[2,6,2,8,128]{4,3,2,1,0:T(8,128)S(1)}, f32[2,6,2,8,128]{4,3,2,1,0:T(8,128)S(1)}, u32[]{:S(2)}, u32[]{:S(2)}) collective-permute-start(f32[2,6,2,8,128]{4,3,2,1,0:T(8,128)S(1)} %get-tuple-element.88), channel_id=1, source_target_pairs={{1,34},{33,0},{0,33},{32,4},{4,32},{36,5},{5,36},{37,9},{9,37},{41... | collective-permute-start | bytes 294920 | tf_op jit(solution)/shard_map/ppermute | solution.py:445
  90.4 3.2 %collective-permute-start.20 = (f32[2,6,2,8,128]{4,3,2,1,0:T(8,128)S(1)}, f32[2,6,2,8,128]{4,3,2,1,0:T(8,128)S(1)}, u32[]{:S(2)}, u32[]{:S(2)}) collective-permute-start(f32[2,6,2,8,128]{4,3,2,1,0:T(8,128)S(1)} %get-tuple-element.89), channel_id=1, source_target_pairs={{1,33},{33,1},{0,32},{32,0},{4,36},{36,4},{5,37},{37,5},{9,41},{41... | collective-permute-start | bytes 294920 | tf_op jit(solution)/shard_map/ppermute | solution.py:445
  94.7 5.2 %collective-permute-start.21 = (f32[2,2,6,2,8,128]{5,4,3,2,1,0:T(8,128)S(1)}, f32[2,2,6,2,8,128]{5,4,3,2,1,0:T(8,128)S(1)}, u32[]{:S(2)}, u32[]{:S(2)}) collective-permute-start(f32[2,2,6,2,8,128]{5,4,3,2,1,0:T(8,128)S(1)} %get-tuple-element.93), channel_id=1, source_target_pairs={{1,34},{33,0},{0,33},{32,4},{4,32},{36,5},{5,36},{37,9},{9,37},{41... | collective-permute-start | bytes 589832 | tf_op jit(solution)/shard_map/ppermute | solution.py:445
  95.7 4.2 %collective-permute-start.22 = (f32[2,2,6,2,8,128]{5,4,3,2,1,0:T(8,128)S(1)}, f32[2,2,6,2,8,128]{5,4,3,2,1,0:T(8,128)S(1)}, u32[]{:S(2)}, u32[]{:S(2)}) collective-permute-start(f32[2,2,6,2,8,128]{5,4,3,2,1,0:T(8,128)S(1)} %get-tuple-element.94), channel_id=1, source_target_pairs={{1,33},{33,1},{0,32},{32,0},{4,36},{36,4},{5,37},{37,5},{9,41},{41... | collective-permute-start | bytes 589832 | tf_op jit(solution)/shard_map/ppermute | solution.py:445
  100.7 11.0 %collective-permute-start.23 = (f32[2,6,2,8,128]{4,3,2,1,0:T(8,128)S(1)}, f32[2,6,2,8,128]{4,3,2,1,0:T(8,128)S(1)}, u32[]{:S(2)}, u32[]{:S(2)}) collective-permute-start(f32[2,6,2,8,128]{4,3,2,1,0:T(8,128)S(1)} %get-tuple-element.95), channel_id=1, source_target_pairs={{1,0},{33,1},{0,2},{32,3},{4,4},{36,5},{5,6},{37,7},{9,8},{41,9},{... | collective-permute-start | bytes 294920 | tf_op jit(solution)/shard_map/ppermute | solution.py:531
  103.5 10.1 %collective-permute-start.24 = (f32[2,6,2,8,128]{4,3,2,1,0:T(8,128)S(1)}, f32[2,6,2,8,128]{4,3,2,1,0:T(8,128)S(1)}, u32[]{:S(2)}, u32[]{:S(2)}) collective-permute-start(f32[2,6,2,8,128]{4,3,2,1,0:T(8,128)S(1)} %get-tuple-element.96), channel_id=1, source_target_pairs={{1,32},{33,33},{0,34},{32,35},{4,36},{36,37},{5,38},{37,39},{9,40}... | collective-permute-start | bytes 294920 | tf_op jit(solution)/shard_map/ppermute | solution.py:532
where the time goes:
time: 116 us; the launch traced here: 114 us
  starting transfers between devices  70.6 us (61%)
  waiting for transfers between devices  31 us (27%)
  Pallas kernels  8.59 us (7%)
  local copies, waits for them, and re-layouts  3.56 us (3%)
    ppermute x9, starting transfers between devices, exchange(): lax.ppermute(to_across, AXES, across())  36.6 us
    ppermute x9, waiting for transfers between devices, exchange(): lax.ppermute(to_across, AXES, across())  23.2 us
    pallas_call x16, Pallas kernels, kernel_call(): pl.pallas_call(body, in_specs=[spec] * len(inputs), out_specs=[spec] * le...  8.59 us
    ppermute x1, starting transfers between devices, local(): got0 = lax.ppermute(message, AXES, spread(0))  7.06 us
    ppermute x1, starting transfers between devices, local(): more1 = lax.ppermute(message[:45], AXES, spread(1))  6.35 us
    ppermute x1, starting transfers between devices, local(): out1 = lax.ppermute(out1, AXES, collect(1))  5.49 us
    ppermute x1, starting transfers between devices, local(): more0 = lax.ppermute(message, AXES, spread(0))  4.1 us
    unnamed x15, local copies, waits for them, and re-layouts  3.22 us
  transfers between devices with their start and end apart: 25, of which 12 were waited for; matrix products, arithmetic and copies ran while one was open for 0% of the time, Pallas kernels for 0%

commit v1 on v0

--- a/solution.py
+++ b/solution.py
@@ -13,16 +13,22 @@
 SMEAR_WEIGHT = 0.1
 AXES = ("section", "space")
 VMEM = pltpu.VMEM
-PATH = (
-    (1, 0), (0, 0), (0, 1), (1, 1), (1, 2), (0, 2), (0, 3), (1, 3),
-    (2, 3), (3, 3), (3, 2), (2, 2), (2, 1), (3, 1), (3, 0), (2, 0),
+PATHS = (
+    (
+        (1, 0, 0), (0, 0, 0), (0, 1, 0), (1, 1, 0), (1, 2, 0), (0, 2, 0), (0, 3, 0), (1, 3, 0),
+        (1, 3, 1), (0, 3, 1), (0, 2, 1), (1, 2, 1), (1, 1, 1), (0, 1, 1), (0, 0, 1), (1, 0, 1),
+    ),
+    (
+        (3, 0, 0), (2, 0, 0), (2, 1, 0), (3, 1, 0), (3, 2, 0), (2, 2, 0), (2, 3, 0), (3, 3, 0),
+        (3, 3, 1), (2, 3, 1), (2, 2, 1), (3, 2, 1), (3, 1, 1), (2, 1, 1), (2, 0, 1), (3, 0, 1),
+    ),
 )
-BLOCKS = len(PATH)
+BLOCKS = 16
 
 
 def place(half, ring, block, core):
-    x, y = PATH[block % BLOCKS]
-    return (2 * half + core) * 32 + ring * 16 + y * 4 + x
+    x, y, z = PATHS[ring][block % BLOCKS]
+    return (2 * half + core) * 32 + z * 16 + y * 4 + x
 
 
 def natural(half, turn, pair):
@@ -54,14 +60,16 @@
     return [(place(h, r, m, c), place(1 - h, r, m, c)) for h, r, m, c in every()]
 
 
-def spread(way):
-    return [
-        (natural(h, r ^ way, 2 * m + c), place(h, r, m, c)) for h, r, m, c in every()
-    ]
-
-
-def collect(way):
-    return [(there, here) for here, there in spread(way)]
+def mate():
+    return [(natural(h, t, j), natural(h, 1 - t, j)) for h in range(2) for t in range(2) for j in range(32)]
+
+
+def spread():
+    return [(natural(h, r, 2 * m + c), place(h, r, m, c)) for h, r, m, c in every()]
+
+
+def collect():
+    return [(there, here) for here, there in spread()]
 
 
 def rows_of(shape):
@@ -192,21 +200,20 @@
 
 
 def load(ref, column):
-    return [ref[column, part] for part in range(6)]
+    return [ref[pl.ds(column * 12 + 2 * part, 2)] for part in range(6)]
 
 
 def store(ref, column, field):
     for part in range(6):
-        ref[column, part] = field[part]
+        ref[pl.ds(column * 12 + 2 * part, 2)] = field[part]
 
 
 def prepare(field, links, own_side, partial_ref, across_ref, sibling_ref, column):
     partial = within(links, field)
+    turned = [swap_planes(a) for a in partial]
     store(partial_ref, column, partial)
-    for part in range(6):
-        turned = swap_planes(partial[part])
-        across_ref[column, part] = jnp.where(own_side, field[part], turned)
-        sibling_ref[column, part] = jnp.where(own_side, turned, field[part])
+    store(across_ref, column, [jnp.where(own_side, f, t) for f, t in zip(field, turned)])
+    store(sibling_ref, column, [jnp.where(own_side, t, f) for f, t in zip(field, turned)])
 
 
 def two_laplacians(field, partial, from_across, from_sibling, links, outer, own_side):
@@ -234,23 +241,19 @@
     )(*inputs)
 
 
-FIELD = (2, 6, 2, 8, 128)
+FIELD = (24, 8, 128)
 SIDE, RING, HALF = 0, 1, 2
 
 
-def first_message(carried, space, marks, message):
-    core = marks[RING] > 0
-    message[pl.ds(0, 54)] = space[...]
+def own_columns(field, core, message, base):
     for column in range(2):
         for part in range(6):
             for spin in range(2):
-                picked = jnp.where(core, carried[part, spin, 2 + column], carried[part, spin, column])
-                message[54 + column * 12 + part * 2 + spin] = picked
-
-
-def second_message(source, magnetic, time, marks, message):
-    core = marks[RING] > 0
-
+                picked = jnp.where(core, field[part, spin, 2 + column], field[part, spin, column])
+                message[base + column * 12 + part * 2 + spin] = picked
+
+
+def pack_magnetic(magnetic, others):
     def raw(axis, imag, row, column):
         return magnetic[axis * 18 + imag * 9 + row * 3 + column]
 
@@ -263,70 +266,78 @@
     for row in range(3):
         for column in range(3):
             at = LADDER + 3 * row + column
-            message[at] = real(0, row, column) + imag(1, row, column)
-            message[at + 9] = imag(0, row, column) - real(1, row, column)
-        message[LEVEL + row] = real(2, row, row)
+            others[at] = real(0, row, column) + imag(1, row, column)
+            others[at + 9] = imag(0, row, column) - real(1, row, column)
+        others[LEVEL + row] = real(2, row, row)
     for slot, (row, column) in enumerate(((0, 1), (0, 2), (1, 2))):
-        message[LEVEL + 3 + slot] = real(2, row, column)
-        message[LEVEL + 6 + slot] = imag(2, row, column)
-    message[pl.ds(TIME, 18)] = time[...]
-    for column in range(2):
-        for part in range(6):
-            for spin in range(2):
-                picked = jnp.where(core, source[part, spin, 2 + column], source[part, spin, column])
-                message[45 + column * 12 + part * 2 + spin] = picked
-
-
-def arrange(got0, got1, marks, field, links_a, links_b, plain_a, plain_b, partial, to_across, to_sibling):
-    ring = marks[RING] > 0
+        others[LEVEL + 3 + slot] = real(2, row, column)
+        others[LEVEL + 6 + slot] = imag(2, row, column)
+
+
+def pack_others(magnetic, time, others):
+    pack_magnetic(magnetic, others)
+    others[pl.ds(TIME, 18)] = time[...]
+
+
+def first_message(own_links, mate_links, carried, marks, message):
+    core = marks[RING] > 0
+    for at in range(54):
+        message[at] = jnp.where(core, mate_links[at], own_links[at])
+    own_columns(carried, core, message, 54)
+
+
+def second_message(own_others, mate_others, source, marks, message):
+    core = marks[RING] > 0
+    for at in range(45):
+        message[at] = jnp.where(core, mate_others[at], own_others[at])
+    own_columns(source, core, message, 45)
+
+
+def third_message(own_links, mate_links, own_others, mate_others, marks, message):
+    core = marks[RING] > 0
+    for at in range(54):
+        message[at] = jnp.where(core, own_links[at], mate_links[at])
+    for at in range(45):
+        message[54 + at] = jnp.where(core, own_others[at], mate_others[at])
+
+
+def arrange(got, links, plain, edge):
+    first = rows_of((8, 128)) % 2 == 0
+    links[pl.ds(18, 36)] = got[pl.ds(18, 36)]
+    plain[...] = got[pl.ds(0, 18)]
+    for row in range(3):
+        for column in range(3):
+            at, turned = 3 * row + column, 3 * column + row
+            links[at] = jnp.where(first, got[at], swap_planes(got[turned]))
+            links[at + 9] = jnp.where(first, got[at + 9], -swap_planes(got[turned + 9]))
+    for at in range(9):
+        edge[at] = jnp.where(first, swap_planes(got[at + 9]), got[at])
+
+
+def outgoing(from_across, from_sibling, plain, marks, outer):
+    first = rows_of((8, 128)) % 2 == 0
+    upper_core = jnp.logical_xor(marks[SIDE] > 0, first)
+    for row in range(3):
+        for column in range(3):
+            at, turned = 3 * row + column, 24 + 3 * column + row
+            edge = jnp.where(upper_core, from_sibling[turned], from_across[turned])
+            outer[at] = jnp.where(first, swap_planes(edge), plain[at])
+            outer[at + 9] = jnp.where(first, -edge, plain[at + 9])
+
+
+def begin(got, marks, field, links, plain, edge, partial, to_across, to_sibling):
+    arrange(got, links, plain, edge)
     own_side = marks[SIDE] > 0
-    first = rows_of((8, 128)) % 2 == 0
-    for turn, links, plain in ((0, links_a, plain_a), (1, links_b, plain_b)):
-        for at in range(18, 54):
-            one, other = (got0[at], got1[at]) if turn == 0 else (got1[at], got0[at])
-            links[at] = jnp.where(ring, other, one)
-        for at in range(18):
-            one, other = (got0[at], got1[at]) if turn == 0 else (got1[at], got0[at])
-            plain[at] = jnp.where(ring, other, one)
-        for row in range(3):
-            for column in range(3):
-                at, turned = 3 * row + column, 3 * column + row
-                links[at] = jnp.where(first, plain[at], swap_planes(plain[turned]))
-                links[at + 9] = jnp.where(first, plain[at + 9], -swap_planes(plain[turned + 9]))
-        for at in range(9):
-            edge = jnp.where(first, swap_planes(plain[at + 9]), plain[at])
-            to_across[24 + 9 * turn + at] = edge
-            to_sibling[24 + 9 * turn + at] = edge
 
     def one_column(column, carry):
-        values = [got0[pl.ds(54 + column * 12 + part * 2, 2)] for part in range(6)]
+        values = [got[pl.ds(54 + column * 12 + part * 2, 2)] for part in range(6)]
         store(field, column, values)
-        total = within(links_a, values)
-        store(partial, column, total)
-        for part in range(6):
-            turned = swap_planes(total[part])
-            to_across[pl.ds(column * 12 + part * 2, 2)] = jnp.where(own_side, values[part], turned)
-            to_sibling[pl.ds(column * 12 + part * 2, 2)] = jnp.where(own_side, turned, values[part])
+        prepare(values, links, own_side, partial, to_across, to_sibling, column)
         return carry
 
     lax.fori_loop(0, 2, one_column, 0)
-
-
-def edges(from_across, from_sibling, plain_a, plain_b, got0, got1, marks, outer_a, outer_b, others_a, others_b):
-    own_side = marks[SIDE] > 0
-    ring = marks[RING] > 0
-    first = rows_of((8, 128)) % 2 == 0
-    upper_core = jnp.logical_xor(own_side, first)
-    for turn, plain, outer in ((0, plain_a, outer_a), (1, plain_b, outer_b)):
-        for row in range(3):
-            for column in range(3):
-                at, turned = 3 * row + column, 24 + 9 * turn + 3 * column + row
-                edge = jnp.where(upper_core, from_sibling[turned], from_across[turned])
-                outer[at] = jnp.where(first, swap_planes(edge), plain[at])
-                outer[at + 9] = jnp.where(first, -edge, plain[at + 9])
-    for at in range(45):
-        others_a[at] = jnp.where(ring, got1[at], got0[at])
-        others_b[at] = jnp.where(ring, got0[at], got1[at])
+    to_across[pl.ds(24, 9)] = edge[...]
+    to_sibling[pl.ds(24, 9)] = edge[...]
 
 
 def step_a(field, partial, from_across, from_sibling, links, outer, others, own_side):
@@ -372,6 +383,9 @@
         return carry
 
     lax.fori_loop(0, 2, one_column, 0)
+    if len(after) > 1:
+        for message in messages[1:]:
+            message[pl.ds(24, 9)] = after[1][...]
 
 
 def only_prepare(field, links, marks, *messages):
@@ -395,45 +409,48 @@
         def one_column(column, carry):
             values = [jnp.where(half, b, a) for a, b in zip(load(early, column), load(late, column))]
             store(field, column, values)
-            prepare(values, links, own_side, *[ref.at[turn] for ref in messages], column)
+            prepare(values, links, own_side, *[ref.at[pl.ds(24 * turn, 24)] for ref in messages], column)
             return carry
 
         lax.fori_loop(0, 2, one_column, 0)
 
 
-def smear_end(field_a, field_b, partial, from_across, from_sibling, links_a, links_b, outer_a, outer_b, marks, out0, out1):
+def smear_end(field_a, field_b, partial, from_across, from_sibling, links_a, links_b, outer_a, outer_b, marks, out):
     own_side = marks[SIDE] > 0
-    ring = marks[RING] > 0
-
-    def smeared(turn, field_ref, links, outer, column):
-        field = load(field_ref, column)
-        single, double = two_laplacians(
-            field, load(partial.at[turn], column), load(from_across.at[turn], column),
-            load(from_sibling.at[turn], column), links, outer, own_side,
-        )
-        return [
-            f + (2 * SMEAR_WEIGHT) * s + (SMEAR_WEIGHT * SMEAR_WEIGHT) * d
-            for f, s, d in zip(field, single, double)
-        ]
-
-    def one_column(column, carry):
-        one = smeared(0, field_a, links_a, outer_a, column)
-        other = smeared(1, field_b, links_b, outer_b, column)
-        store(out0, column, [jnp.where(ring, b, a) for a, b in zip(one, other)])
-        store(out1, column, [jnp.where(ring, a, b) for a, b in zip(one, other)])
-        return carry
-
-    lax.fori_loop(0, 2, one_column, 0)
-
-
-def deliver(got0, got1, marks, out):
+    for turn, field_ref, links, outer in ((0, field_a, links_a, outer_a), (1, field_b, links_b, outer_b)):
+
+        def one_column(column, carry):
+            at = column + 2 * turn
+            field = load(field_ref, column)
+            single, double = two_laplacians(
+                field, load(partial, at), load(from_across, at), load(from_sibling, at),
+                links, outer, own_side,
+            )
+            values = [
+                f + (2 * SMEAR_WEIGHT) * s + (SMEAR_WEIGHT * SMEAR_WEIGHT) * d
+                for f, s, d in zip(field, single, double)
+            ]
+            store(out, at, values)
+            return carry
+
+        lax.fori_loop(0, 2, one_column, 0)
+
+
+def for_mate(got, marks, message):
+    core = marks[RING] > 0
+    for at in range(24):
+        message[at] = jnp.where(core, got[at], got[24 + at])
+
+
+def deliver(got, other, marks, out):
     core = marks[RING] > 0
     for column in range(2):
         for part in range(6):
             for spin in range(2):
-                one, other = got0[column, part, spin], got1[column, part, spin]
-                out[part, spin, column] = jnp.where(core, other, one)
-                out[part, spin, 2 + column] = jnp.where(core, one, other)
+                at = column * 12 + part * 2 + spin
+                mine = jnp.where(core, got[24 + at], got[at])
+                out[part, spin, column] = jnp.where(core, other[at], mine)
+                out[part, spin, 2 + column] = jnp.where(core, mine, other[at])
 
 
 def registers(value, lead):
@@ -451,11 +468,10 @@
 
 def local(carried, source_field, source_slice, space_links, time_links, magnetic):
     section, space = lax.axis_index("section"), lax.axis_index("space")
-    core, half, ring = section % 2, section // 2, space // 16
+    core, half, ring = section % 2, section // 2, space % 4 // 2
     first = (jnp.arange(8) % 2)[:, None] == core
     side = jnp.broadcast_to(first.astype(jnp.float32), (8, 128))
-    marks = jnp.stack([side, full(ring == 1), full(half == 1)])
-    core_marks = jnp.stack([side, full(core == 1), full(half == 1)])
+    marks = jnp.stack([side, full(core == 1), full(half == 1)])
 
     carried = registers(carried, (6, 2, 4))
     source_field = registers(source_field, (6, 2, 4))
@@ -463,49 +479,60 @@
     time_links = registers(time_links, (18,))
     magnetic = registers(magnetic, (54,))
 
-    (message,) = kernel_call(first_message, [carried, space_links, core_marks], [(78, 8, 128)], False)
-    got0 = lax.ppermute(message, AXES, spread(0))
-    got1 = lax.ppermute(message[:54], AXES, spread(1))
+    mate_links = lax.ppermute(space_links, AXES, mate())
+    (own_others,) = kernel_call(pack_others, [magnetic, time_links], [(45, 8, 128)], False)
+    mate_others = lax.ppermute(own_others, AXES, mate())
+    (message,) = kernel_call(first_message, [space_links, mate_links, carried, marks], [(78, 8, 128)], False)
+    got = lax.ppermute(message, AXES, spread())
     (message,) = kernel_call(
-        second_message, [source_field, magnetic, time_links, core_marks], [(69, 8, 128)], False
-    )
-    more0 = lax.ppermute(message, AXES, spread(0))
-    more1 = lax.ppermute(message[:45], AXES, spread(1))
-
-    field, links_a, links_b, plain_a, plain_b, partial, to_across, to_sibling = kernel_call(
-        arrange,
-        [got0, got1, marks],
-        [FIELD, (54, 8, 128), (54, 8, 128), (18, 8, 128), (18, 8, 128), FIELD, (42, 8, 128), (42, 8, 128)],
+        second_message, [own_others, mate_others, source_field, marks], [(69, 8, 128)], False
+    )
+    others_a = lax.ppermute(message, AXES, spread())
+    (message,) = kernel_call(
+        third_message, [space_links, mate_links, own_others, mate_others, marks], [(99, 8, 128)], False
+    )
+    got_b = lax.ppermute(message, AXES, spread())
+
+    with_edge = (33, 8, 128)
+    field, links_a, plain_a, _, partial, to_across, to_sibling = kernel_call(
+        begin,
+        [got, marks],
+        [FIELD, (54, 8, 128), (18, 8, 128), (9, 8, 128), FIELD, with_edge, with_edge],
     )
     from_across, from_sibling = exchange(to_across, to_sibling)
-    outer_a, outer_b, others_a, others_b = kernel_call(
-        edges,
-        [from_across, from_sibling, plain_a, plain_b, more0, more1, marks],
-        [(18, 8, 128), (18, 8, 128), (45, 8, 128), (45, 8, 128)],
-    )
-    from_across = from_across[:24].reshape(FIELD)
-    from_sibling = from_sibling[:24].reshape(FIELD)
-    source = more0[45:].reshape(FIELD)
+    (outer_a,) = kernel_call(outgoing, [from_across, from_sibling, plain_a, marks], [(18, 8, 128)])
+    links_b, plain_b, edge_b = kernel_call(
+        arrange, [got_b], [(54, 8, 128), (18, 8, 128), (9, 8, 128)]
+    )
+    others_b = got_b[54:]
+    source = others_a[45:]
     here = lax.dynamic_slice_in_dim(source_slice, 2 * ring, 2)
     sources = [
-        jnp.where(here == 2 * half + turn, 1.0, 0.0).astype(jnp.float32).reshape(2, 1, 1, 1, 1) * source
+        jnp.repeat((here == 2 * half + turn).astype(jnp.float32), 12).reshape(24, 1, 1) * source
         for turn in range(2)
     ]
-    links, outer, others = (links_a, links_b), (outer_a, outer_b), (others_a, others_b)
+    links, others = (links_a, links_b), (others_a, others_b)
+    outer_b = None
     results = []
     for phase in range(2):
         for turn in range(2):
+            if phase == 0 and turn == 1:
+                (outer_b,) = kernel_call(
+                    outgoing, [from_across, from_sibling, plain_b, marks], [(18, 8, 128)]
+                )
+            outer = (outer_a, outer_b)[turn]
             field, partial, to_across, to_sibling = kernel_call(
                 first_half,
-                [field, partial, from_across, from_sibling, links[turn], outer[turn], others[turn], marks],
+                [field, partial, from_across, from_sibling, links[turn], outer, others[turn], marks],
                 [FIELD] * 4,
             )
             from_across, from_sibling = exchange(to_across, to_sibling)
-            inputs = [field, partial, from_across, from_sibling, links[turn], outer[turn], others[turn]]
+            inputs = [field, partial, from_across, from_sibling, links[turn], outer, others[turn]]
             inputs += [sources[turn], marks]
             if turn == 0:
+                more, size = ([edge_b], with_edge) if phase == 0 else ([], FIELD)
                 field, partial, to_across, to_sibling = kernel_call(
-                    second_half, inputs + [links[1]], [FIELD] * 4
+                    second_half, inputs + [links_b] + more, [FIELD, FIELD, size, size]
                 )
                 from_across, from_sibling = exchange(to_across, to_sibling)
             else:
@@ -518,19 +545,20 @@
             )
             from_across, from_sibling = exchange(to_across, to_sibling)
 
-    both = (2,) + FIELD
+    both = (48, 8, 128)
     field_a, field_b, partial, to_across, to_sibling = kernel_call(
         smear_start, results + [links_a, links_b, marks], [FIELD, FIELD, both, both, both]
     )
     from_across, from_sibling = exchange(to_across, to_sibling)
-    out0, out1 = kernel_call(
+    (out,) = kernel_call(
         smear_end,
         [field_a, field_b, partial, from_across, from_sibling, links_a, links_b, outer_a, outer_b, marks],
-        [FIELD, FIELD],
-    )
-    out0 = lax.ppermute(out0, AXES, collect(0))
-    out1 = lax.ppermute(out1, AXES, collect(1))
-    (out,) = kernel_call(deliver, [out0, out1, core_marks], [(6, 2, 4, 8, 128)])
+        [both],
+    )
+    got = lax.ppermute(out, AXES, collect())
+    (message,) = kernel_call(for_mate, [got, marks], [FIELD])
+    other = lax.ppermute(message, AXES, mate())
+    (out,) = kernel_call(deliver, [got, other, marks], [(6, 2, 4, 8, 128)])
     out = jnp.swapaxes(out.reshape(2, 3, 2, 4, 4, 2, 128), -3, -2)
     return out.reshape(1, 2, 3, 2, 4, 2, 512)
 

time: 116 us -> 95.6 us (0.82)
  starting transfers between devices: 70.6 us -> 37.3 us
  waiting for transfers between devices: 31 us -> 42.3 us
    ppermute x9, starting transfers between devices: 36.6 us -> 13.9 us  [exchange(): lax.ppermute(to_across, AXES, across())]
    ppermute x6 -> x7, starting transfers between devices: 28.1 us -> 19 us  [the longest x1 7.02 us: local(): got_b = lax.ppermute(message, AXES, spread())]
    ppermute x9, waiting for transfers between devices: 23.2 us -> 28.5 us  [exchange(): lax.ppermute(to_across, AXES, across())]
    ppermute x6 -> x7, waiting for transfers between devices: 4.63 us -> 9.81 us  [the longest x1 7.67 us: local(): got = lax.ppermute(out, AXES, collect())]
    ppermute x9, starting transfers between devices: 2.79 us -> 1.4 us  [exchange(): lax.ppermute(to_sibling, AXES, sibling())]
    pallas_call x16 -> x21, Pallas kernels: 8.59 us -> 9.43 us  [kernel_call(): pl.pallas_call(body, in_specs=[spec] * len(inputs), out_specs=[spec] * le...]
    unnamed x15 -> x13, local copies, waits for them, and re-layouts: 3.22 us -> 3.98 us
  transfers between devices with their start and end apart: 25 -> 26, of which waited for: 12 -> 13; matrix products, arithmetic and copies ran while one was open for 0% -> 1% of each run, Pallas kernels for 0% -> 2%
where the time goes in v1:
time: 95.6 us; the launch traced here: 94.1 us
  waiting for transfers between devices  42.3 us (44%)
  starting transfers between devices  37.3 us (39%)
  Pallas kernels  9.43 us (10%)
  local copies, waits for them, and re-layouts  4.52 us (5%)
    ppermute x9, waiting for transfers between devices, exchange(): lax.ppermute(to_across, AXES, across())  28.5 us
    ppermute x9, starting transfers between devices, exchange(): lax.ppermute(to_across, AXES, across())  13.9 us
    pallas_call x21, Pallas kernels, kernel_call(): pl.pallas_call(body, in_specs=[spec] * len(inputs), out_specs=[spec] * le...  9.43 us
    ppermute x1, waiting for transfers between devices, local(): got = lax.ppermute(out, AXES, collect())  7.67 us
    ppermute x1, starting transfers between devices, local(): got_b = lax.ppermute(message, AXES, spread())  7.02 us
    ppermute x1, starting transfers between devices, local(): got = lax.ppermute(message, AXES, spread())  5.98 us
    ppermute x1, waiting for transfers between devices, local(): field = lax.ppermute(field, AXES, onward())  4 us
    unnamed x13, local copies, waits for them, and re-layouts  3.98 us
  transfers between devices with their start and end apart: 26, of which 13 were waited for; matrix products, arithmetic and copies ran while one was open for 1% of the time, Pallas kernels for 2%

profile of v1, /device:TPU:32, one launch (start us, length us, event | category | flops | bytes accessed | tf_op | source)
XLA Modules:
  0.0 94.1 jit_solution(5791278218330384016)
XLA Ops:
  0.0 0.9 copy-done.1
  0.9 0.9 copy-done.4
  1.9 0.8 copy-done
  3.1 1.2 %collective-permute-done.mate_links = f32[54,8,128]{2,1,0:T(8,128)S(1)} collective-permute-done((f32[54,8,128]{2,1,0:T(8,128)S(1)}, f32[54,8,128]{2,1,0:T(8,128)S(1)}, u32[]{:S(2)}, u32[]{:S(2)}) %collective-permute-start) | collective-permute-done | bytes 221216 | tf_op jit(solution)/shard_map/ppermute | solution.py:482
  4.3 6.0 %collective-permute-start.1 = (f32[78,8,128]{2,1,0:T(8,128)S(1)}, f32[78,8,128]{2,1,0:T(8,128)S(1)}, u32[]{:S(2)}, u32[]{:S(2)}) collective-permute-start(f32[78,8,128]{2,1,0:T(8,128)S(1)} %shard_map.64), channel_id=1, source_target_pairs={{0,1},{1,33},{2,0},{3,32},{4,4},{5,36},{6,5},{7,37},{8,9},{9,41},{... | collective-permute-start | bytes 958472 | tf_op jit(solution)/shard_map/ppermute | solution.py:486
  10.3 1.9 %collective-permute-start.5 = (f32[69,8,128]{2,1,0:T(8,128)S(1)}, f32[69,8,128]{2,1,0:T(8,128)S(1)}, u32[]{:S(2)}, u32[]{:S(2)}) collective-permute-start(f32[69,8,128]{2,1,0:T(8,128)S(1)} %shard_map.68), channel_id=1, source_target_pairs={{0,1},{1,33},{2,0},{3,32},{4,4},{5,36},{6,5},{7,37},{8,9},{9,41},{... | collective-permute-start | bytes 847880 | tf_op jit(solution)/shard_map/ppermute | solution.py:490
  12.3 7.0 %collective-permute-start.8 = (f32[99,8,128]{2,1,0:T(8,128)S(1)}, f32[99,8,128]{2,1,0:T(8,128)S(1)}, u32[]{:S(2)}, u32[]{:S(2)}) collective-permute-start(f32[99,8,128]{2,1,0:T(8,128)S(1)} %shard_map.70), channel_id=1, source_target_pairs={{0,1},{1,33},{2,0},{3,32},{4,4},{5,36},{6,5},{7,37},{8,9},{9,41},{... | collective-permute-start | bytes 1216520 | tf_op jit(solution)/shard_map/ppermute | solution.py:494
  19.4 0.9 shard_map.65
  20.3 7.6 %collective-permute-start.2 = (f32[33,8,128]{2,1,0:T(8,128)S(1)}, f32[33,8,128]{2,1,0:T(8,128)S(1)}, u32[]{:S(2)}, u32[]{:S(2)}) collective-permute-start(f32[33,8,128]{2,1,0:T(8,128)S(1)} %get-tuple-element.48), channel_id=1, source_target_pairs={{1,49},{33,0},{0,33},{32,4},{4,32},{36,5},{5,36},{37,9},{9,37},{41... | collective-permute-start | bytes 405512 | tf_op jit(solution)/shard_map/ppermute | solution.py:462
  27.9 0.7 copy-done.5
  28.9 1.6 %collective-permute-done.2.from_across = f32[33,8,128]{2,1,0:T(8,128)S(1)} collective-permute-done((f32[33,8,128]{2,1,0:T(8,128)S(1)}, f32[33,8,128]{2,1,0:T(8,128)S(1)}, u32[]{:S(2)}, u32[]{:S(2)}) %collective-permute-start.2) | collective-permute-done | bytes 135200 | tf_op jit(solution)/shard_map/ppermute | solution.py:462
  30.6 0.9 shard_map.69
  31.5 1.8 %collective-permute-start.6 = (f32[24,8,128]{2,1,0:T(8,128)S(1)}, f32[24,8,128]{2,1,0:T(8,128)S(1)}, u32[]{:S(2)}, u32[]{:S(2)}) collective-permute-start(f32[24,8,128]{2,1,0:T(8,128)S(1)} %get-tuple-element.54), channel_id=1, source_target_pairs={{1,49},{33,0},{0,33},{32,4},{4,32},{36,5},{5,36},{37,9},{9,37},{41... | collective-permute-start | bytes 294920 | tf_op jit(solution)/shard_map/ppermute | solution.py:462
  33.3 0.1 slice_multiply_fusion
  33.5 2.1 %collective-permute-done.6.from_across = f32[24,8,128]{2,1,0:T(8,128)S(1)} collective-permute-done((f32[24,8,128]{2,1,0:T(8,128)S(1)}, f32[24,8,128]{2,1,0:T(8,128)S(1)}, u32[]{:S(2)}, u32[]{:S(2)}) %collective-permute-start.6) | collective-permute-done | bytes 98336 | tf_op jit(solution)/shard_map/ppermute | solution.py:462
  35.6 0.8 shard_map.72
  36.5 1.8 %collective-permute-start.9 = (f32[33,8,128]{2,1,0:T(8,128)S(1)}, f32[33,8,128]{2,1,0:T(8,128)S(1)}, u32[]{:S(2)}, u32[]{:S(2)}) collective-permute-start(f32[33,8,128]{2,1,0:T(8,128)S(1)} %get-tuple-element.60), channel_id=1, source_target_pairs={{1,49},{33,0},{0,33},{32,4},{4,32},{36,5},{5,36},{37,9},{9,37},{41... | collective-permute-start | bytes 405512 | tf_op jit(solution)/shard_map/ppermute | solution.py:462
  38.3 2.7 %collective-permute-done.9.from_across = f32[33,8,128]{2,1,0:T(8,128)S(1)} collective-permute-done((f32[33,8,128]{2,1,0:T(8,128)S(1)}, f32[33,8,128]{2,1,0:T(8,128)S(1)}, u32[]{:S(2)}, u32[]{:S(2)}) %collective-permute-start.9) | collective-permute-done | bytes 135200 | tf_op jit(solution)/shard_map/ppermute | solution.py:462
  41.0 0.9 shard_map.74
  42.0 2.1 %collective-permute-start.11 = (f32[24,8,128]{2,1,0:T(8,128)S(1)}, f32[24,8,128]{2,1,0:T(8,128)S(1)}, u32[]{:S(2)}, u32[]{:S(2)}) collective-permute-start(f32[24,8,128]{2,1,0:T(8,128)S(1)} %get-tuple-element.65), channel_id=1, source_target_pairs={{1,49},{33,0},{0,33},{32,4},{4,32},{36,5},{5,36},{37,9},{9,37},{41... | collective-permute-start | bytes 294920 | tf_op jit(solution)/shard_map/ppermute | solution.py:462
  44.1 2.3 %collective-permute-done.11.from_across = f32[24,8,128]{2,1,0:T(8,128)S(1)} collective-permute-done((f32[24,8,128]{2,1,0:T(8,128)S(1)}, f32[24,8,128]{2,1,0:T(8,128)S(1)}, u32[]{:S(2)}, u32[]{:S(2)}) %collective-permute-start.11) | collective-permute-done | bytes 98336 | tf_op jit(solution)/shard_map/ppermute | solution.py:462
  46.4 0.6 shard_map.75.early_b
  46.9 3.1 %collective-permute-start.13 = (f32[24,8,128]{2,1,0:T(8,128)S(1)}, f32[24,8,128]{2,1,0:T(8,128)S(1)}, u32[]{:S(2)}, u32[]{:S(2)}) collective-permute-start(f32[24,8,128]{2,1,0:T(8,128)S(1)} %shard_map.75.early_b), channel_id=1, source_target_pairs={{1,65},{33,97},{0,64},{32,96},{4,68},{36,100},{5,69},{37,101},{9,7... | collective-permute-start | bytes 294920 | tf_op jit(solution)/shard_map/ppermute | solution.py:542
  50.0 4.0 %collective-permute-done.13.field = f32[24,8,128]{2,1,0:T(8,128)S(1)} collective-permute-done((f32[24,8,128]{2,1,0:T(8,128)S(1)}, f32[24,8,128]{2,1,0:T(8,128)S(1)}, u32[]{:S(2)}, u32[]{:S(2)}) %collective-permute-start.13) | collective-permute-done | bytes 98336 | tf_op jit(solution)/shard_map/ppermute | solution.py:542
  54.0 0.3 shard_map.76
  54.3 0.1 collective-permute-start.14
  54.4 0.3 collective-permute-start.15
  54.7 3.7 %collective-permute-done.14.from_across = f32[24,8,128]{2,1,0:T(8,128)S(1)} collective-permute-done((f32[24,8,128]{2,1,0:T(8,128)S(1)}, f32[24,8,128]{2,1,0:T(8,128)S(1)}, u32[]{:S(2)}, u32[]{:S(2)}) %collective-permute-start.14) | collective-permute-done | bytes 98336 | tf_op jit(solution)/shard_map/ppermute | solution.py:462
  58.5 0.9 shard_map.77
  59.4 0.3 collective-permute-start.17
  59.7 3.7 %collective-permute-done.16.from_across = f32[24,8,128]{2,1,0:T(8,128)S(1)} collective-permute-done((f32[24,8,128]{2,1,0:T(8,128)S(1)}, f32[24,8,128]{2,1,0:T(8,128)S(1)}, u32[]{:S(2)}, u32[]{:S(2)}) %collective-permute-start.16) | collective-permute-done | bytes 98336 | tf_op jit(solution)/shard_map/ppermute | solution.py:462
  63.5 0.8 shard_map.78
  64.4 0.3 collective-permute-start.19
  64.7 3.7 %collective-permute-done.18.from_across = f32[24,8,128]{2,1,0:T(8,128)S(1)} collective-permute-done((f32[24,8,128]{2,1,0:T(8,128)S(1)}, f32[24,8,128]{2,1,0:T(8,128)S(1)}, u32[]{:S(2)}, u32[]{:S(2)}) %collective-permute-start.18) | collective-permute-done | bytes 98336 | tf_op jit(solution)/shard_map/ppermute | solution.py:462
  68.4 0.9 shard_map.79
  69.3 0.1 collective-permute-start.20
  69.4 0.3 collective-permute-start.21
  69.7 3.7 %collective-permute-done.20.from_across = f32[24,8,128]{2,1,0:T(8,128)S(1)} collective-permute-done((f32[24,8,128]{2,1,0:T(8,128)S(1)}, f32[24,8,128]{2,1,0:T(8,128)S(1)}, u32[]{:S(2)}, u32[]{:S(2)}) %collective-permute-start.20) | collective-permute-done | bytes 98336 | tf_op jit(solution)/shard_map/ppermute | solution.py:462
  73.5 0.6 shard_map.80.late_b
  74.0 0.7 shard_map.81
  74.8 0.3 collective-permute-start.23
  75.1 4.8 %collective-permute-done.22.from_across = f32[48,8,128]{2,1,0:T(8,128)S(1)} collective-permute-done((f32[48,8,128]{2,1,0:T(8,128)S(1)}, f32[48,8,128]{2,1,0:T(8,128)S(1)}, u32[]{:S(2)}, u32[]{:S(2)}) %collective-permute-start.22) | collective-permute-done | bytes 196640 | tf_op jit(solution)/shard_map/ppermute | solution.py:462
  79.9 0.9 shard_map.82
  80.8 2.5 %collective-permute-start.24 = (f32[48,8,128]{2,1,0:T(8,128)S(1)}, f32[48,8,128]{2,1,0:T(8,128)S(1)}, u32[]{:S(2)}, u32[]{:S(2)}) collective-permute-start(f32[48,8,128]{2,1,0:T(8,128)S(1)} %shard_map.82), channel_id=1, source_target_pairs={{1,0},{33,1},{0,2},{32,3},{4,4},{36,5},{5,6},{37,7},{9,8},{41,9},{... | collective-permute-start | bytes 589832 | tf_op jit(solution)/shard_map/ppermute | solution.py:558
  83.3 7.7 %collective-permute-done.24.got = f32[48,8,128]{2,1,0:T(8,128)S(1)} collective-permute-done((f32[48,8,128]{2,1,0:T(8,128)S(1)}, f32[48,8,128]{2,1,0:T(8,128)S(1)}, u32[]{:S(2)}, u32[]{:S(2)}) %collective-permute-start.24) | collective-permute-done | bytes 196640 | tf_op jit(solution)/shard_map/ppermute | solution.py:558
  91.0 1.5 %collective-permute-start.25 = (f32[24,8,128]{2,1,0:T(8,128)S(1)}, f32[24,8,128]{2,1,0:T(8,128)S(1)}, u32[]{:S(2)}, u32[]{:S(2)}) collective-permute-start(f32[24,8,128]{2,1,0:T(8,128)S(1)} %shard_map.83), channel_id=1, source_target_pairs={{0,32},{1,33},{2,34},{3,35},{4,36},{5,37},{6,38},{7,39},{8,40},{9,... | collective-permute-start | bytes 294920 | tf_op jit(solution)/shard_map/ppermute | solution.py:560
  92.5 0.9 %collective-permute-done.25.other = f32[24,8,128]{2,1,0:T(8,128)S(1)} collective-permute-done((f32[24,8,128]{2,1,0:T(8,128)S(1)}, f32[24,8,128]{2,1,0:T(8,128)S(1)}, u32[]{:S(2)}, u32[]{:S(2)}) %collective-permute-start.25) | collective-permute-done | bytes 98336 | tf_op jit(solution)/shard_map/ppermute | solution.py:560
  93.4 0.7 copy.13
  (50 shorter events, 1.4 us)
Async XLA Ops:
  0.0 0.9 copy-start.1
  0.9 0.9 copy-start.4
  1.8 0.9 copy-start
  1.8 2.4 %copy-start.3 = (f32[2,3,2,4,2,512]{5,4,3,2,1,0:T(2,128)S(1)}, f32[2,3,2,4,2,512]{5,4,3,2,1,0:T(2,128)}, u32[]{:S(2)}) copy-start(f32[2,3,2,4,2,512]{5,4,3,2,1,0:T(2,128)} %param.6) | copy-start | bytes 589828
  1.8 8.4 %collective-permute-start.4 = (f32[45,8,128]{2,1,0:T(8,128)S(1)}, f32[45,8,128]{2,1,0:T(8,128)S(1)}, u32[]{:S(2)}, u32[]{:S(2)}) collective-permute-start(f32[45,8,128]{2,1,0:T(8,128)S(1)} %shard_map.67.own_others), channel_id=1, source_target_pairs={{0,32},{1,33},{2,34},{3,35},{4,36},{5,37},{6,38},{7,39},{8,40},{9,... | collective-permute-start | bytes 552968 | tf_op jit(solution)/shard_map/ppermute | solution.py:484
  2.8 1.5 %collective-permute-start = (f32[54,8,128]{2,1,0:T(8,128)S(1)}, f32[54,8,128]{2,1,0:T(8,128)S(1)}, u32[]{:S(2)}, u32[]{:S(2)}) collective-permute-start(f32[54,8,128]{2,1,0:T(8,128)S(1)} %bitcast.33), channel_id=1, source_target_pairs={{0,32},{1,33},{2,34},{3,35},{4,36},{5,37},{6,38},{7,39},{8,40},{9,... | collective-permute-start | bytes 663560 | tf_op jit(solution)/shard_map/ppermute | solution.py:482
  4.2 6.1 %copy-start.2 = (f32[2,3,2,4,2,512]{5,4,3,2,1,0:T(2,128)S(1)}, f32[2,3,2,4,2,512]{5,4,3,2,1,0:T(2,128)}, u32[]{:S(2)}) copy-start(f32[2,3,2,4,2,512]{5,4,3,2,1,0:T(2,128)} %param.7) | copy-start | bytes 589828
  4.3 15.1 %collective-permute-start.1 = (f32[78,8,128]{2,1,0:T(8,128)S(1)}, f32[78,8,128]{2,1,0:T(8,128)S(1)}, u32[]{:S(2)}, u32[]{:S(2)}) collective-permute-start(f32[78,8,128]{2,1,0:T(8,128)S(1)} %shard_map.64), channel_id=1, source_target_pairs={{0,1},{1,33},{2,0},{3,32},{4,4},{5,36},{6,5},{7,37},{8,9},{9,41},{... | collective-permute-start | bytes 958472 | tf_op jit(solution)/shard_map/ppermute | solution.py:486
  10.3 20.3 %collective-permute-start.5 = (f32[69,8,128]{2,1,0:T(8,128)S(1)}, f32[69,8,128]{2,1,0:T(8,128)S(1)}, u32[]{:S(2)}, u32[]{:S(2)}) collective-permute-start(f32[69,8,128]{2,1,0:T(8,128)S(1)} %shard_map.68), channel_id=1, source_target_pairs={{0,1},{1,33},{2,0},{3,32},{4,4},{5,36},{6,5},{7,37},{8,9},{9,41},{... | collective-permute-start | bytes 847880 | tf_op jit(solution)/shard_map/ppermute | solution.py:490
  12.3 21.1 %collective-permute-start.8 = (f32[99,8,128]{2,1,0:T(8,128)S(1)}, f32[99,8,128]{2,1,0:T(8,128)S(1)}, u32[]{:S(2)}, u32[]{:S(2)}) collective-permute-start(f32[99,8,128]{2,1,0:T(8,128)S(1)} %shard_map.70), channel_id=1, source_target_pairs={{0,1},{1,33},{2,0},{3,32},{4,4},{5,36},{6,5},{7,37},{8,9},{9,41},{... | collective-permute-start | bytes 1216520 | tf_op jit(solution)/shard_map/ppermute | solution.py:494
  20.3 10.3 %collective-permute-start.2 = (f32[33,8,128]{2,1,0:T(8,128)S(1)}, f32[33,8,128]{2,1,0:T(8,128)S(1)}, u32[]{:S(2)}, u32[]{:S(2)}) collective-permute-start(f32[33,8,128]{2,1,0:T(8,128)S(1)} %get-tuple-element.48), channel_id=1, source_target_pairs={{1,49},{33,0},{0,33},{32,4},{4,32},{36,5},{5,36},{37,9},{9,37},{41... | collective-permute-start | bytes 405512 | tf_op jit(solution)/shard_map/ppermute | solution.py:462
  27.9 2.7 %collective-permute-start.3 = (f32[33,8,128]{2,1,0:T(8,128)S(1)}, f32[33,8,128]{2,1,0:T(8,128)S(1)}, u32[]{:S(2)}, u32[]{:S(2)}) collective-permute-start(f32[33,8,128]{2,1,0:T(8,128)S(1)} %get-tuple-element.49), channel_id=1, source_target_pairs={{1,33},{33,1},{0,32},{32,0},{4,36},{36,4},{5,37},{37,5},{9,41},{41... | collective-permute-start | bytes 405512 | tf_op jit(solution)/shard_map/ppermute | solution.py:462
  27.9 0.7 copy-start.5
  31.5 4.1 %collective-permute-start.6 = (f32[24,8,128]{2,1,0:T(8,128)S(1)}, f32[24,8,128]{2,1,0:T(8,128)S(1)}, u32[]{:S(2)}, u32[]{:S(2)}) collective-permute-start(f32[24,8,128]{2,1,0:T(8,128)S(1)} %get-tuple-element.54), channel_id=1, source_target_pairs={{1,49},{33,0},{0,33},{32,4},{4,32},{36,5},{5,36},{37,9},{9,37},{41... | collective-permute-start | bytes 294920 | tf_op jit(solution)/shard_map/ppermute | solution.py:462
  33.3 2.3 %collective-permute-start.7 = (f32[24,8,128]{2,1,0:T(8,128)S(1)}, f32[24,8,128]{2,1,0:T(8,128)S(1)}, u32[]{:S(2)}, u32[]{:S(2)}) collective-permute-start(f32[24,8,128]{2,1,0:T(8,128)S(1)} %get-tuple-element.55), channel_id=1, source_target_pairs={{1,33},{33,1},{0,32},{32,0},{4,36},{36,4},{5,37},{37,5},{9,41},{41... | collective-permute-start | bytes 294920 | tf_op jit(solution)/shard_map/ppermute | solution.py:462
  36.5 4.5 %collective-permute-start.9 = (f32[33,8,128]{2,1,0:T(8,128)S(1)}, f32[33,8,128]{2,1,0:T(8,128)S(1)}, u32[]{:S(2)}, u32[]{:S(2)}) collective-permute-start(f32[33,8,128]{2,1,0:T(8,128)S(1)} %get-tuple-element.60), channel_id=1, source_target_pairs={{1,49},{33,0},{0,33},{32,4},{4,32},{36,5},{5,36},{37,9},{9,37},{41... | collective-permute-start | bytes 405512 | tf_op jit(solution)/shard_map/ppermute | solution.py:462
  38.3 2.7 %collective-permute-start.10 = (f32[33,8,128]{2,1,0:T(8,128)S(1)}, f32[33,8,128]{2,1,0:T(8,128)S(1)}, u32[]{:S(2)}, u32[]{:S(2)}) collective-permute-start(f32[33,8,128]{2,1,0:T(8,128)S(1)} %get-tuple-element.61), channel_id=1, source_target_pairs={{1,33},{33,1},{0,32},{32,0},{4,36},{36,4},{5,37},{37,5},{9,41},{41... | collective-permute-start | bytes 405512 | tf_op jit(solution)/shard_map/ppermute | solution.py:462
  42.0 4.4 %collective-permute-start.11 = (f32[24,8,128]{2,1,0:T(8,128)S(1)}, f32[24,8,128]{2,1,0:T(8,128)S(1)}, u32[]{:S(2)}, u32[]{:S(2)}) collective-permute-start(f32[24,8,128]{2,1,0:T(8,128)S(1)} %get-tuple-element.65), channel_id=1, source_target_pairs={{1,49},{33,0},{0,33},{32,4},{4,32},{36,5},{5,36},{37,9},{9,37},{41... | collective-permute-start | bytes 294920 | tf_op jit(solution)/shard_map/ppermute | solution.py:462
  44.1 2.3 %collective-permute-start.12 = (f32[24,8,128]{2,1,0:T(8,128)S(1)}, f32[24,8,128]{2,1,0:T(8,128)S(1)}, u32[]{:S(2)}, u32[]{:S(2)}) collective-permute-start(f32[24,8,128]{2,1,0:T(8,128)S(1)} %get-tuple-element.66), channel_id=1, source_target_pairs={{1,33},{33,1},{0,32},{32,0},{4,36},{36,4},{5,37},{37,5},{9,41},{41... | collective-permute-start | bytes 294920 | tf_op jit(solution)/shard_map/ppermute | solution.py:462
  46.9 7.1 %collective-permute-start.13 = (f32[24,8,128]{2,1,0:T(8,128)S(1)}, f32[24,8,128]{2,1,0:T(8,128)S(1)}, u32[]{:S(2)}, u32[]{:S(2)}) collective-permute-start(f32[24,8,128]{2,1,0:T(8,128)S(1)} %shard_map.75.early_b), channel_id=1, source_target_pairs={{1,65},{33,97},{0,64},{32,96},{4,68},{36,100},{5,69},{37,101},{9,7... | collective-permute-start | bytes 294920 | tf_op jit(solution)/shard_map/ppermute | solution.py:542
  54.3 4.1 %collective-permute-start.14 = (f32[24,8,128]{2,1,0:T(8,128)S(1)}, f32[24,8,128]{2,1,0:T(8,128)S(1)}, u32[]{:S(2)}, u32[]{:S(2)}) collective-permute-start(f32[24,8,128]{2,1,0:T(8,128)S(1)} %get-tuple-element.68), channel_id=1, source_target_pairs={{1,49},{33,0},{0,33},{32,4},{4,32},{36,5},{5,36},{37,9},{9,37},{41... | collective-permute-start | bytes 294920 | tf_op jit(solution)/shard_map/ppermute | solution.py:462
  54.4 4.0 %collective-permute-start.15 = (f32[24,8,128]{2,1,0:T(8,128)S(1)}, f32[24,8,128]{2,1,0:T(8,128)S(1)}, u32[]{:S(2)}, u32[]{:S(2)}) collective-permute-start(f32[24,8,128]{2,1,0:T(8,128)S(1)} %get-tuple-element.69), channel_id=1, source_target_pairs={{1,33},{33,1},{0,32},{32,0},{4,36},{36,4},{5,37},{37,5},{9,41},{41... | collective-permute-start | bytes 294920 | tf_op jit(solution)/shard_map/ppermute | solution.py:462
  59.3 4.1 %collective-permute-start.16 = (f32[24,8,128]{2,1,0:T(8,128)S(1)}, f32[24,8,128]{2,1,0:T(8,128)S(1)}, u32[]{:S(2)}, u32[]{:S(2)}) collective-permute-start(f32[24,8,128]{2,1,0:T(8,128)S(1)} %get-tuple-element.72), channel_id=1, source_target_pairs={{1,49},{33,0},{0,33},{32,4},{4,32},{36,5},{5,36},{37,9},{9,37},{41... | collective-permute-start | bytes 294920 | tf_op jit(solution)/shard_map/ppermute | solution.py:462
  59.4 4.0 %collective-permute-start.17 = (f32[24,8,128]{2,1,0:T(8,128)S(1)}, f32[24,8,128]{2,1,0:T(8,128)S(1)}, u32[]{:S(2)}, u32[]{:S(2)}) collective-permute-start(f32[24,8,128]{2,1,0:T(8,128)S(1)} %get-tuple-element.73), channel_id=1, source_target_pairs={{1,33},{33,1},{0,32},{32,0},{4,36},{36,4},{5,37},{37,5},{9,41},{41... | collective-permute-start | bytes 294920 | tf_op jit(solution)/shard_map/ppermute | solution.py:462
  64.3 4.1 %collective-permute-start.18 = (f32[24,8,128]{2,1,0:T(8,128)S(1)}, f32[24,8,128]{2,1,0:T(8,128)S(1)}, u32[]{:S(2)}, u32[]{:S(2)}) collective-permute-start(f32[24,8,128]{2,1,0:T(8,128)S(1)} %get-tuple-element.76), channel_id=1, source_target_pairs={{1,49},{33,0},{0,33},{32,4},{4,32},{36,5},{5,36},{37,9},{9,37},{41... | collective-permute-start | bytes 294920 | tf_op jit(solution)/shard_map/ppermute | solution.py:462
  64.4 4.0 %collective-permute-start.19 = (f32[24,8,128]{2,1,0:T(8,128)S(1)}, f32[24,8,128]{2,1,0:T(8,128)S(1)}, u32[]{:S(2)}, u32[]{:S(2)}) collective-permute-start(f32[24,8,128]{2,1,0:T(8,128)S(1)} %get-tuple-element.77), channel_id=1, source_target_pairs={{1,33},{33,1},{0,32},{32,0},{4,36},{36,4},{5,37},{37,5},{9,41},{41... | collective-permute-start | bytes 294920 | tf_op jit(solution)/shard_map/ppermute | solution.py:462
  69.3 4.1 %collective-permute-start.20 = (f32[24,8,128]{2,1,0:T(8,128)S(1)}, f32[24,8,128]{2,1,0:T(8,128)S(1)}, u32[]{:S(2)}, u32[]{:S(2)}) collective-permute-start(f32[24,8,128]{2,1,0:T(8,128)S(1)} %get-tuple-element.80), channel_id=1, source_target_pairs={{1,49},{33,0},{0,33},{32,4},{4,32},{36,5},{5,36},{37,9},{9,37},{41... | collective-permute-start | bytes 294920 | tf_op jit(solution)/shard_map/ppermute | solution.py:462
  69.4 4.0 %collective-permute-start.21 = (f32[24,8,128]{2,1,0:T(8,128)S(1)}, f32[24,8,128]{2,1,0:T(8,128)S(1)}, u32[]{:S(2)}, u32[]{:S(2)}) collective-permute-start(f32[24,8,128]{2,1,0:T(8,128)S(1)} %get-tuple-element.81), channel_id=1, source_target_pairs={{1,33},{33,1},{0,32},{32,0},{4,36},{36,4},{5,37},{37,5},{9,41},{41... | collective-permute-start | bytes 294920 | tf_op jit(solution)/shard_map/ppermute | solution.py:462
  74.7 5.2 %collective-permute-start.22 = (f32[48,8,128]{2,1,0:T(8,128)S(1)}, f32[48,8,128]{2,1,0:T(8,128)S(1)}, u32[]{:S(2)}, u32[]{:S(2)}) collective-permute-start(f32[48,8,128]{2,1,0:T(8,128)S(1)} %get-tuple-element.85), channel_id=1, source_target_pairs={{1,49},{33,0},{0,33},{32,4},{4,32},{36,5},{5,36},{37,9},{9,37},{41... | collective-permute-start | bytes 589832 | tf_op jit(solution)/shard_map/ppermute | solution.py:462
  74.8 5.1 %collective-permute-start.23 = (f32[48,8,128]{2,1,0:T(8,128)S(1)}, f32[48,8,128]{2,1,0:T(8,128)S(1)}, u32[]{:S(2)}, u32[]{:S(2)}) collective-permute-start(f32[48,8,128]{2,1,0:T(8,128)S(1)} %get-tuple-element.86), channel_id=1, source_target_pairs={{1,33},{33,1},{0,32},{32,0},{4,36},{36,4},{5,37},{37,5},{9,41},{41... | collective-permute-start | bytes 589832 | tf_op jit(solution)/shard_map/ppermute | solution.py:462
  80.8 10.2 %collective-permute-start.24 = (f32[48,8,128]{2,1,0:T(8,128)S(1)}, f32[48,8,128]{2,1,0:T(8,128)S(1)}, u32[]{:S(2)}, u32[]{:S(2)}) collective-permute-start(f32[48,8,128]{2,1,0:T(8,128)S(1)} %shard_map.82), channel_id=1, source_target_pairs={{1,0},{33,1},{0,2},{32,3},{4,4},{36,5},{5,6},{37,7},{9,8},{41,9},{... | collective-permute-start | bytes 589832 | tf_op jit(solution)/shard_map/ppermute | solution.py:558
  91.0 2.4 %collective-permute-start.25 = (f32[24,8,128]{2,1,0:T(8,128)S(1)}, f32[24,8,128]{2,1,0:T(8,128)S(1)}, u32[]{:S(2)}, u32[]{:S(2)}) collective-permute-start(f32[24,8,128]{2,1,0:T(8,128)S(1)} %shard_map.83), channel_id=1, source_target_pairs={{0,32},{1,33},{2,34},{3,35},{4,36},{5,37},{6,38},{7,39},{8,40},{9,... | collective-permute-start | bytes 294920 | tf_op jit(solution)/shard_map/ppermute | solution.py:560

commit v2 on v1

v2 whole, which is shorter than its diff:
```python
import functools

import jax
import jax.numpy as jnp
from jax import lax
from jax.experimental import pallas as pl
from jax.experimental.pallas import tpu as pltpu
from jax.sharding import PartitionSpec as P


LZ = 16
KINETIC = 1.0 / 6.0
QUARTIC = 1.0 / 216.0
SPIN_WEIGHT = 1.0 / 6.0
SMEAR_WEIGHT = 0.1
AXES = ("section", "space")
VMEM = pltpu.VMEM
PAIRS = 32
SLICES = 4


def chip(pair):
    at = min(pair, PAIRS - 1 - pair)
    y, x = divmod(at, 4)
    return (x if y % 2 == 0 else 3 - x), y, pair // 16


def place(half, core, pair):
    x, y, z = chip(pair % PAIRS)
    return (2 * half + core) * 32 + z * 16 + y * 4 + x


def natural(half, core, pair):
    return (2 * half + core) * 32 + pair


EVERY = [(half, core, pair) for half in range(2) for core in range(2) for pair in range(PAIRS)]
SPREAD = [(natural(h, c, j), place(h, c, j)) for h, c, j in EVERY]
COLLECT = [[(place(h, c, j), natural(h ^ way, c, j)) for h, c, j in EVERY] for way in range(2)]
UP = [(place(h, c, j), place(h, 1 - c, j + 1)) for h, c, j in EVERY]
DOWN = [(place(h, c, j), place(h, 1 - c, j - 1)) for h, c, j in EVERY]
SIBLING = [(place(h, c, j), place(h, 1 - c, j)) for h, c, j in EVERY]
FACING = [(place(h, c, j), place(1 - h, c, j)) for h, c, j in EVERY]


def rows_of(shape):
    return lax.broadcasted_iota(jnp.int32, shape, len(shape) - 2)


def lanes_of(shape):
    return lax.broadcasted_iota(jnp.int32, shape, len(shape) - 1)


def roll(value, by, axis):
    return pltpu.roll(value, by, value.ndim + axis)


def swap_planes(value):
    first = rows_of(value.shape) % 2 == 0
    return jnp.where(first, roll(value, 7, -2), roll(value, 1, -2))


def y_forward(value):
    moved = roll(value, 112, -1)
    return jnp.where(lanes_of(value.shape) < 112, moved, roll(moved, 6, -2))


def y_backward(value):
    moved = roll(value, 16, -1)
    return jnp.where(lanes_of(value.shape) >= 16, moved, roll(moved, 2, -2))


def z_forward(value):
    inside = lanes_of(value.shape) % LZ < LZ - 1
    return jnp.where(inside, roll(value, 127, -1), roll(value, LZ - 1, -1))


def z_backward(value):
    inside = lanes_of(value.shape) % LZ > 0
    return jnp.where(inside, roll(value, 1, -1), roll(value, 129 - LZ, -1))


def add(one, other):
    return [a + b for a, b in zip(one, other)]


def scaled(factor, field):
    return [factor * a for a in field]


def link_at(ref, base):
    def entry(row, column):
        return ref[base + 3 * row + column], ref[base + 9 + 3 * row + column]

    return entry


def product(entry, field, dagger, total=None):
    real, imag = [], []
    for out in range(3):
        sum_real = None if total is None else total[out]
        sum_imag = None if total is None else total[3 + out]
        for inner in range(3):
            link_real, link_imag = entry(inner, out) if dagger else entry(out, inner)
            field_real, field_imag = field[inner], field[3 + inner]
            cross_real, cross_imag = link_imag * field_imag, link_imag * field_real
            part_real, part_imag = link_real * field_real, link_real * field_imag
            if dagger:
                part_real, part_imag = part_real + cross_real, part_imag - cross_imag
            else:
                part_real, part_imag = part_real - cross_real, part_imag + cross_imag
            sum_real = part_real if sum_real is None else sum_real + part_real
            sum_imag = part_imag if sum_imag is None else sum_imag + part_imag
        real.append(sum_real)
        imag.append(sum_imag)
    return real + imag


ALONG_X, ALONG_Y, ALONG_Z = 0, 18, 36


def within(links, inner, field):
    total = scaled(-6.0, field)
    total = product(link_at(links, ALONG_Y), [y_forward(a) for a in field], False, total)
    back = product(link_at(links, ALONG_Y), field, True)
    total = add(total, [y_backward(a) for a in back])
    total = product(link_at(links, ALONG_Z), [z_forward(a) for a in field], False, total)
    back = product(link_at(links, ALONG_Z), field, True)
    total = add(total, [z_backward(a) for a in back])
    return product(link_at(inner, 0), [swap_planes(a) for a in field], False, total)


LADDER, LEVEL, TIME = 0, 18, 27


def level_entry(ref):
    def entry(row, column):
        if row == column:
            return ref[LEVEL + row], None
        slot = min(row, column) + max(row, column) - 1
        imag = ref[LEVEL + 6 + slot]
        return ref[LEVEL + 3 + slot], imag if row < column else -imag

    return entry


def hermitian_product(entry, field):
    real, imag = [], []
    for out in range(3):
        sum_real = sum_imag = None
        for inner in range(3):
            link_real, link_imag = entry(out, inner)
            part_real, part_imag = link_real * field[inner], link_real * field[3 + inner]
            if link_imag is not None:
                part_real = part_real - link_imag * field[3 + inner]
                part_imag = part_imag + link_imag * field[inner]
            sum_real = part_real if sum_real is None else sum_real + part_real
            sum_imag = part_imag if sum_imag is None else sum_imag + part_imag
        real.append(sum_real)
        imag.append(sum_imag)
    return real + imag


def spin_term(others, field):
    up, down = [a[0] for a in field], [a[1] for a in field]
    ladder, level = link_at(others, LADDER), level_entry(others)
    upper = add(hermitian_product(level, up), product(ladder, down, False))
    lower = product(ladder, up, True)
    lower = [a - b for a, b in zip(lower, hermitian_product(level, down))]
    return [jnp.stack([a, b]) for a, b in zip(upper, lower)]


def load(ref, column):
    return [ref[pl.ds(column * 12 + 2 * part, 2)] for part in range(6)]


def store(ref, column, field):
    for part in range(6):
        ref[pl.ds(column * 12 + 2 * part, 2)] = field[part]


def prepare(field, links, inner, lower, partial_ref, below_ref, above_ref, column):
    partial = within(links, inner, field)
    turned = [swap_planes(a) for a in partial]
    store(partial_ref, column, partial)
    store(below_ref, column, [jnp.where(lower, f, t) for f, t in zip(field, turned)])
    store(above_ref, column, [jnp.where(lower, t, f) for f, t in zip(field, turned)])


def two_laplacians(field, partial, from_below, from_above, links, inner, outer, lower):
    beyond = [
        swap_planes(jnp.where(lower, s, a)) for a, s in zip(from_below, from_above)
    ]
    rim = [jnp.where(lower, a, s) for a, s in zip(from_below, from_above)]
    single = product(link_at(outer, 0), beyond, False, partial)
    rim = product(link_at(outer, 0), field, True, rim)
    double = product(link_at(outer, 0), rim, False, within(links, inner, single))
    return single, double


def kernel_call(body, inputs, outputs, far=(), near=(), scratch=()):
    spec = pl.BlockSpec(memory_space=VMEM)
    spaces = [pltpu.HBM if at in far else pltpu.SMEM if at in near else VMEM for at in range(len(inputs))]
    inputs = [
        value if at in near else pltpu.with_memory_space_constraint(value, space)
        for at, (value, space) in enumerate(zip(inputs, spaces))
    ]
    shapes = [VMEM(shape, jnp.float32) for shape in outputs]
    return pl.pallas_call(
        body,
        in_specs=[pl.BlockSpec(memory_space=space) for space in spaces],
        out_specs=[spec] * len(outputs),
        out_shape=shapes,
        scratch_shapes=list(scratch),
        compiler_params=pltpu.CompilerParams(vmem_limit_bytes=32 * 1024 * 1024),
    )(*inputs)


FIELD = (12, 8, 128)
WITH_EDGE = (21, 8, 128)
WITH_RIM = (18, 8, 128)
CORE, HALF, TWIST = 0, 1, 2


def own_column(field, marks, message, base):
    half, twist = marks[HALF] > 0, marks[TWIST] > 0
    for part in range(6):
        for spin in range(2):
            low = jnp.where(twist, field[part, spin, 1], field[part, spin, 0])
            high = jnp.where(twist, field[part, spin, 3], field[part, spin, 2])
            message[base + part * 2 + spin] = jnp.where(half, high, low)


def pack_magnetic(magnetic, others):
    def raw(axis, imag, row, column):
        return magnetic[axis * 18 + imag * 9 + row * 3 + column]

    def real(axis, row, column):
        return 0.5 * (raw(axis, 0, row, column) + raw(axis, 0, column, row))

    def imag(axis, row, column):
        return 0.5 * (raw(axis, 1, row, column) - raw(axis, 1, column, row))

    for row in range(3):
        for column in range(3):
            at = LADDER + 3 * row + column
            others[at] = real(0, row, column) + imag(1, row, column)
            others[at + 9] = imag(0, row, column) - real(1, row, column)
        others[LEVEL + row] = real(2, row, row)
    for slot, (row, column) in enumerate(((0, 1), (0, 2), (1, 2))):
        others[LEVEL + 3 + slot] = real(2, row, column)
        others[LEVEL + 6 + slot] = imag(2, row, column)


def pack(space, time, magnetic, carried, own, field, raw, sems):
    copies = [
        pltpu.make_async_copy(source, target, sems.at[at])
        for at, (source, target) in enumerate(
            ((magnetic, raw), (space, own.at[pl.ds(0, 54)]), (time, own.at[pl.ds(54 + TIME, 18)]), (carried, field))
        )
    ]
    for copy in copies:
        copy.start()
    copies[0].wait()
    pack_magnetic(raw, own.at[pl.ds(54, 27)])
    for copy in copies[1:]:
        copy.wait()


def first_message(own, carried, marks, message):
    message[pl.ds(0, 54)] = own[pl.ds(0, 54)]
    own_column(carried, marks, message, 54)


def second_message(own, source, marks, message):
    message[pl.ds(0, 45)] = own[pl.ds(54, 45)]
    own_column(source, marks, message, 45)


def third_message(size, own, facing, message):
    message[pl.ds(0, size)] = own[pl.ds(0, size)]
    message[pl.ds(size, size)] = facing[...]


def pick(timeslice, own, facing, beside, marks, size, out):
    same_half = (marks[HALF] > 0) == (timeslice // 2 == 1)
    same_core = (marks[CORE] > 0) == (timeslice % 2 == 1)
    for at in range(size):
        mine = jnp.where(same_half, own[at], facing[at])
        theirs = jnp.where(same_half, beside[at], beside[size + at])
        out[at] = jnp.where(same_core, mine, theirs)


def arrange(links, inner, edge):
    first = rows_of((8, 128)) % 2 == 0
    turned = [swap_planes(links[at]) for at in range(18)]
    for row in range(3):
        for column in range(3):
            at, across = 3 * row + column, 3 * column + row
            inner[at] = jnp.where(first, links[at], turned[across])
            inner[at + 9] = jnp.where(first, links[at + 9], -turned[across + 9])
    for at in range(9):
        edge[at] = jnp.where(first, turned[at + 9], links[at])


def outgoing(from_below, links, outer):
    first = rows_of((8, 128)) % 2 == 0
    for row in range(3):
        for column in range(3):
            at, turned = 3 * row + column, 12 + 3 * column + row
            edge = from_below[turned]
            outer[at] = jnp.where(first, swap_planes(edge), links[at])
            outer[at + 9] = jnp.where(first, -edge, links[at + 9])


def begin(own, facing, beside, marks, field, links, inner, partial, to_below, to_above):
    pick(0, own, facing, beside, marks, 54, links)
    arrange(links, inner, to_above.at[pl.ds(12, 9)])
    lower = rows_of((8, 128)) % 2 == 0
    values = [own[pl.ds(54 + part * 2, 2)] for part in range(6)]
    store(field, 0, values)
    prepare(values, links, inner, lower, partial, to_below, to_above, 0)


def later_links(own, facing, beside, marks, *outs):
    for timeslice in range(1, SLICES):
        links, inner, edge = outs[3 * timeslice - 3 : 3 * timeslice]
        pick(timeslice, own, facing, beside, marks, 54, links)
        arrange(links, inner, edge)


def other_links(first, own, facing, beside, marks, *outs):
    for at, others in enumerate(outs):
        pick(first + at, own, facing, beside, marks, 45, others)


def step_a(field, partial, from_below, from_above, links, inner, outer, others, lower):
    single, double = two_laplacians(field, partial, from_below, from_above, links, inner, outer, lower)
    spin = spin_term(others, field)
    return [
        f + (0.5 * KINETIC) * s + (0.5 * QUARTIC) * d + (0.5 * SPIN_WEIGHT) * b
        for f, s, d, b in zip(field, single, double, spin)
    ]


def masked_sources(source_slice, others, marks, _, *outs):
    half, twist = marks[HALF] > 0, marks[TWIST] > 0
    for timeslice, out in enumerate(outs):
        on = [jnp.where(source_slice[column] == timeslice, 1.0, 0.0) for column in range(4)]
        weight = jnp.where(half, jnp.where(twist, on[3], on[2]), jnp.where(twist, on[1], on[0]))
        for at in range(12):
            out[at] = weight * others[45 + at]


def first_half(field, partial, from_below, from_above, links, inner, outer, others, *rest):
    rims, (turned_field, *messages) = rest[:-4], rest[-4:]
    lower = rows_of((8, 128)) % 2 == 0
    values = step_a(
        load(field, 0), load(partial, 0), load(from_below, 0), load(from_above, 0),
        links, inner, outer, others, lower,
    )
    values = product(link_at(others, TIME), values, True)
    store(turned_field, 0, values)
    prepare(values, links, inner, lower, *messages, 0)
    for rim, message in zip(rims, messages[1:]):
        message[pl.ds(12, 6)] = rim[...]


def second_half(field, partial, from_below, from_above, links, inner, outer, others, source, *rest):
    lower = rows_of((8, 128)) % 2 == 0
    values = step_a(
        load(field, 0), load(partial, 0), load(from_below, 0), load(from_above, 0),
        links, inner, outer, others, lower,
    )
    values = add(values, load(source, 0))
    if len(rest) == 4:
        result, *messages = rest
        store(result, 0, values)
        prepare(values, links, inner, lower, *messages, 0)
        return
    next_links, next_inner, next_edge, result, *messages = rest
    store(result, 0, values)
    prepare(values, next_links, next_inner, lower, *messages, 0)
    messages[2][pl.ds(12, 9)] = next_edge[...]


def smear_start(field, links, inner, partial_ref, rim_below, rim_above):
    first = rows_of((8, 128)) % 2 == 0
    partial = within(links, inner, load(field, 0))
    store(partial_ref, 0, partial)
    for part in range(6):
        up, down = partial[part][0], partial[part][1]
        rim_below[part] = jnp.where(first, up, swap_planes(down))
        rim_above[part] = jnp.where(first, swap_planes(up), down)


def smeared(field, partial, beyond, rim, links, inner, outer):
    single = product(link_at(outer, 0), beyond, False, partial)
    rim = product(link_at(outer, 0), field, True, rim)
    double = product(link_at(outer, 0), rim, False, within(links, inner, single))
    return [
        f + (2 * SMEAR_WEIGHT) * s + (SMEAR_WEIGHT * SMEAR_WEIGHT) * d
        for f, s, d in zip(field, single, double)
    ]


def smear_end(field, partial, from_below, from_above, rims_below, rims_above, links, inner, outer, out):
    lower = rows_of((8, 128)) % 2 == 0
    beyond = [
        swap_planes(jnp.where(lower, a, b)) for a, b in zip(load(from_above, 0), load(from_below, 0))
    ]
    rim = []
    for part in range(6):
        below, above = rims_below[12 + part], rims_above[12 + part]
        up = jnp.where(lower, below, swap_planes(above))
        down = jnp.where(lower, swap_planes(below), above)
        rim.append(jnp.stack([up, down]))
    store(out, 0, smeared(load(field, 0), load(partial, 0), beyond, rim, links, inner, outer))


def last_smear_end(field, partial, from_below, from_above, links, inner, outer, done_0, done_1, done_2, marks, mine, theirs):
    lower = rows_of((8, 128)) % 2 == 0
    core = marks[CORE] > 0
    below, above = load(from_below, 0), load(from_above, 0)
    beyond = [swap_planes(jnp.where(lower, a, b)) for a, b in zip(above, below)]
    rim = [jnp.where(lower, b, a) for a, b in zip(above, below)]
    last = smeared(load(field, 0), load(partial, 0), beyond, rim, links, inner, outer)
    for level, pair in enumerate(((load(done_0, 0), load(done_1, 0)), (load(done_2, 0), last))):
        store(mine, level, [jnp.where(core, b, a) for a, b in zip(*pair)])
        store(theirs, level, [jnp.where(core, a, b) for a, b in zip(*pair)])


def both_columns(way, mine, other, marks, *rest):
    half, twist = (marks[HALF] > 0) == (way == 0), marks[TWIST] > 0
    out = rest[-1]
    for at in range(12):
        own, beside = jnp.where(half, mine[12 + at], mine[at]), jnp.where(half, other[12 + at], other[at])
        out[at] = jnp.where(twist, beside, own)
        out[12 + at] = jnp.where(twist, own, beside)


def deliver(got0, got1, marks, out):
    half = marks[HALF] > 0
    for column in range(2):
        for part in range(6):
            for spin in range(2):
                at = column * 12 + part * 2 + spin
                out[part, spin, column] = jnp.where(half, got1[at], got0[at])
                out[part, spin, 2 + column] = jnp.where(half, got0[at], got1[at])


def registers(value, lead):
    rows = value.reshape(lead + (2, 4, 128))
    return jnp.swapaxes(rows, -3, -2).reshape(lead + (8, 128))


def exchange(to_below, to_above):
    return lax.ppermute(to_above, AXES, UP), lax.ppermute(to_below, AXES, DOWN)


def full(flag):
    return jnp.broadcast_to(flag.astype(jnp.float32), (8, 128))


def local(carried, source_field, source_slice, space_links, time_links, magnetic):
    section, space = lax.axis_index("section"), lax.axis_index("space")
    core, half = section % 2, section // 2
    x, y, z = space % 4, space // 4 % 4, space // 16
    twist_there = (core + x) % 2
    twist = (core + x + y + z) % 2
    marks_there = jnp.stack([full(core == 1), full(half == 1), full(twist_there == 1)])
    marks = jnp.stack([full(core == 1), full(half == 1), full(twist == 1)])

    carried = registers(carried, (6, 2, 4))
    source_field = registers(source_field, (6, 2, 4))
    space_links = registers(space_links, (54,))
    time_links = registers(time_links, (18,))
    magnetic = registers(magnetic, (54,))

    own, carried = kernel_call(
        pack,
        [space_links, time_links, magnetic, carried],
        [(99, 8, 128), (6, 2, 4, 8, 128)],
        far=range(4),
        scratch=[VMEM((54, 8, 128), jnp.float32), pltpu.SemaphoreType.DMA((4,))],
    )
    (message,) = kernel_call(first_message, [own, carried, marks_there], [(66, 8, 128)])
    links_own = lax.ppermute(message, AXES, SPREAD)
    (message,) = kernel_call(second_message, [own, source_field, marks_there], [(57, 8, 128)])
    others_own = lax.ppermute(message, AXES, SPREAD)
    links_facing = lax.ppermute(links_own[:54], AXES, FACING)
    others_facing = lax.ppermute(others_own[:45], AXES, FACING)
    (message,) = kernel_call(
        functools.partial(third_message, 54), [links_own, links_facing], [(108, 8, 128)]
    )
    links_beside = lax.ppermute(message, AXES, SIBLING)
    (message,) = kernel_call(
        functools.partial(third_message, 45), [others_own, others_facing], [(90, 8, 128)]
    )
    others_beside = lax.ppermute(message, AXES, SIBLING)

    field, links_0, inner_0, partial, to_below, to_above = kernel_call(
        begin,
        [links_own, links_facing, links_beside, marks],
        [FIELD, (54, 8, 128), (18, 8, 128), FIELD, FIELD, WITH_EDGE],
    )
    from_below, from_above = exchange(to_below, to_above)
    later = kernel_call(
        later_links,
        [links_own, links_facing, links_beside, marks],
        [(54, 8, 128), (18, 8, 128), (9, 8, 128)] * 3,
    )
    links, inner, edge = [links_0, *later[0::3]], [inner_0, *later[1::3]], [None, *later[2::3]]
    picked = [others_own, others_facing, others_beside, marks]
    others = kernel_call(functools.partial(other_links, 0), picked, [(45, 8, 128)])
    others += kernel_call(functools.partial(other_links, 1), picked, [(45, 8, 128)] * 3)

    sources = kernel_call(
        masked_sources, [source_slice, others_own, marks, to_below], [FIELD] * SLICES, near=(0,)
    )
    outer, done, rims = [], [], []
    for timeslice in range(SLICES):
        outer += kernel_call(outgoing, [from_below, links[timeslice]], [(18, 8, 128)])
        around = [links[timeslice], inner[timeslice], outer[timeslice], others[timeslice]]
        size = WITH_RIM if rims else FIELD
        before = [from_below, from_above]
        field, partial, to_below, to_above = kernel_call(
            first_half, [field, partial, *before, *around, *rims], [FIELD, FIELD, size, size]
        )
        from_below, from_above = exchange(to_below, to_above)
        if rims:
            at = timeslice - 1
            done += kernel_call(
                smear_end,
                [result, smear_partial, *before, from_below, from_above, links[at], inner[at], outer[at]],
                [FIELD],
            )
        inputs = [field, partial, from_below, from_above] + around + [sources[timeslice]]
        if timeslice + 1 < SLICES:
            after = [links[timeslice + 1], inner[timeslice + 1], edge[timeslice + 1]]
            field, partial, to_below, to_above = kernel_call(
                second_half, inputs + after, [FIELD, FIELD, FIELD, WITH_EDGE]
            )
            result = field
            smear_partial, *rims = kernel_call(
                smear_start, [field, links[timeslice], inner[timeslice]], [FIELD] + [(6, 8, 128)] * 2
            )
        else:
            field, partial, to_below, to_above = kernel_call(second_half, inputs, [FIELD] * 4)
        from_below, from_above = exchange(to_below, to_above)

    around = [links[-1], inner[-1], outer[-1]]
    mine, theirs = kernel_call(
        last_smear_end, [field, partial, from_below, from_above, *around, *done, marks], [(24, 8, 128)] * 2
    )
    other = lax.ppermute(theirs, AXES, SIBLING)
    (out1,) = kernel_call(functools.partial(both_columns, 1), [mine, other, marks], [(24, 8, 128)])
    got1 = lax.ppermute(out1, AXES, COLLECT[1])
    (out0,) = kernel_call(functools.partial(both_columns, 0), [mine, other, marks, out1], [(24, 8, 128)])
    got0 = lax.ppermute(out0, AXES, COLLECT[0])
    (out,) = kernel_call(deliver, [got0, got1, marks], [(6, 2, 4, 8, 128)])
    out = jnp.swapaxes(out.reshape(2, 3, 2, 4, 4, 2, 128), -3, -2)
    return out.reshape(1, 2, 3, 2, 4, 2, 512)


def solution(mesh):
    return jax.shard_map(
        local,
        mesh=mesh,
        in_specs=(
            P(None, None, None, None, "space", None),
            P(None, None, None, None, "space", None),
            P(),
            P("section", None, None, None, None, "space", None),
            P("section", None, None, None, "space", None),
            P("section", None, None, None, None, "space", None),
        ),
        out_specs=P("section", None, None, None, None, "space", None),
        check_vma=False,
    )
```

time: 95.6 us -> 91.1 us (0.953); the launches traced: 94.1 us -> 90.9 us
  starting transfers between devices: 37.3 us -> 42 us
  local copies, waits for them, and re-layouts: 4.52 us -> 0.86 us
  Pallas kernels: 9.43 us -> 7.36 us
  waiting for transfers between devices: 42.3 us -> 40.3 us
    ppermute x26 -> x27, starting transfers between devices: 37.3 us -> 42 us  [the longest x9 10.5 us: exchange(): lax.ppermute(to_below, AXES, DOWN)]
    unnamed x13 -> x5, local copies, waits for them, and re-layouts: 3.98 us -> 0.69 us
    pallas_call x21 -> x32, Pallas kernels: 9.43 us -> 7.36 us  [kernel_call(): pl.pallas_call(body, in_specs=[pl.BlockSpec(memory_space=space) for space...]
    ppermute x26 -> x27, waiting for transfers between devices: 42.3 us -> 40.3 us  [the longest x9 19.3 us: exchange(): lax.ppermute(to_above, AXES, UP)]
  transfers between devices with their start and end apart: 26 -> 27, of which waited for: 13 -> 21; matrix products, arithmetic and copies ran while one was open for 1% -> 0% of each run, Pallas kernels for 2% -> 3%
where the time goes in v2:
time: 91.1 us; the launch traced here: 90.9 us
  starting transfers between devices  42 us (46%)
  waiting for transfers between devices  40.3 us (44%)
  Pallas kernels  7.36 us (8%)
    ppermute x9, waiting for transfers between devices, exchange(): lax.ppermute(to_above, AXES, UP)  19.3 us
    ppermute x9, starting transfers between devices, exchange(): lax.ppermute(to_below, AXES, DOWN)  10.5 us
    pallas_call x32, Pallas kernels, kernel_call(): pl.pallas_call(body, in_specs=[pl.BlockSpec(memory_space=space) for space...  7.36 us
    ppermute x1, starting transfers between devices, local(): got0 = lax.ppermute(out0, AXES, COLLECT[0])  7.05 us
    ppermute x9, starting transfers between devices, exchange(): lax.ppermute(to_above, AXES, UP)  6 us
    ppermute x1, waiting for transfers between devices, local(): got1 = lax.ppermute(out1, AXES, COLLECT[1])  5.8 us
    ppermute x1, waiting for transfers between devices, local(): links_own = lax.ppermute(message, AXES, SPREAD)  5.26 us
    ppermute x1, starting transfers between devices, local(): links_own = lax.ppermute(message, AXES, SPREAD)  5.05 us
  transfers between devices with their start and end apart: 27, of which 21 were waited for; matrix products, arithmetic and copies ran while one was open for 0% of the time, Pallas kernels for 3%

profile of v2, /device:TPU:32, one launch (start us, length us, event | category | flops | bytes accessed | tf_op | source)
XLA Modules:
  0.0 90.9 jit_solution(10713504428366105820)
XLA Ops:
  0.1 1.2 %shard_map.64 = (f32[99,8,128]{2,1,0:T(8,128)S(1)}, f32[6,2,4,8,128]{4,3,2,1,0:T(8,128)S(1)}) custom-call(f32[54,8,128]{2,1,0:T(8,128)} %bitcast.36, f32[18,8,128]{2,1,0:T(8,128)} %bitcast.39, f32[54,8,128]{2,1,0:T(8,128)} %bitcast.37, f32[6,2,4,8,128]{4,3,2,1,0:T(8,128)} %bitcast.38), custom_call_target="tpu_custom_call" | custom-call | tf_op jit(solution)/shard_map/pallas_call | solution.py:209
  1.4 5.1 %collective-permute-start = (f32[66,8,128]{2,1,0:T(8,128)S(1)}, f32[66,8,128]{2,1,0:T(8,128)S(1)}, u32[]{:S(2)}, u32[]{:S(2)}) collective-permute-start(f32[66,8,128]{2,1,0:T(8,128)S(1)} %shard_map.65), channel_id=1, source_target_pairs={{0,0},{1,1},{2,2},{3,3},{4,7},{5,6},{6,5},{7,4},{8,8},{9,9},{10,10... | collective-permute-start | bytes 811016 | tf_op jit(solution)/shard_map/ppermute | solution.py:488
  6.5 4.3 %collective-permute-start.5 = (f32[57,8,128]{2,1,0:T(8,128)S(1)}, f32[57,8,128]{2,1,0:T(8,128)S(1)}, u32[]{:S(2)}, u32[]{:S(2)}) collective-permute-start(f32[57,8,128]{2,1,0:T(8,128)S(1)} %shard_map.69), channel_id=1, source_target_pairs={{0,0},{1,1},{2,2},{3,3},{4,7},{5,6},{6,5},{7,4},{8,8},{9,9},{10,10... | collective-permute-start | bytes 700424 | tf_op jit(solution)/shard_map/ppermute | solution.py:490
  10.8 5.3 %collective-permute-done.own = f32[66,8,128]{2,1,0:T(8,128)S(1)} collective-permute-done((f32[66,8,128]{2,1,0:T(8,128)S(1)}, f32[66,8,128]{2,1,0:T(8,128)S(1)}, u32[]{:S(2)}, u32[]{:S(2)}) %collective-permute-start) | collective-permute-done | bytes 270368 | tf_op jit(solution)/shard_map/ppermute | solution.py:488
  16.1 3.1 %collective-permute-start.1 = (f32[54,8,128]{2,1,0:T(8,128)S(1)}, f32[54,8,128]{2,1,0:T(8,128)S(1)}, u32[]{:S(2)}, u32[]{:S(2)}) collective-permute-start(f32[54,8,128]{2,1,0:T(8,128)S(1)} %slice.8), channel_id=1, source_target_pairs={{0,64},{1,65},{2,66},{3,67},{7,71},{6,70},{5,69},{4,68},{8,72},{9,... | collective-permute-start | bytes 663560 | tf_op jit(solution)/shard_map/ppermute | solution.py:491
  19.2 1.0 %collective-permute-done.5.own.others = f32[57,8,128]{2,1,0:T(8,128)S(1)} collective-permute-done((f32[57,8,128]{2,1,0:T(8,128)S(1)}, f32[57,8,128]{2,1,0:T(8,128)S(1)}, u32[]{:S(2)}, u32[]{:S(2)}) %collective-permute-start.5) | collective-permute-done | bytes 233504 | tf_op jit(solution)/shard_map/ppermute | solution.py:490
  20.1 3.1 %collective-permute-start.6 = (f32[45,8,128]{2,1,0:T(8,128)S(1)}, f32[45,8,128]{2,1,0:T(8,128)S(1)}, u32[]{:S(2)}, u32[]{:S(2)}) collective-permute-start(f32[45,8,128]{2,1,0:T(8,128)S(1)} %slice.9), channel_id=1, source_target_pairs={{0,64},{1,65},{2,66},{3,67},{7,71},{6,70},{5,69},{4,68},{8,72},{9,... | collective-permute-start | bytes 552968 | tf_op jit(solution)/shard_map/ppermute | solution.py:492
  23.2 0.5 collective-permute-done.1.facing
  23.9 3.7 %collective-permute-done.6.facing = f32[45,8,128]{2,1,0:T(8,128)S(1)} collective-permute-done((f32[45,8,128]{2,1,0:T(8,128)S(1)}, f32[45,8,128]{2,1,0:T(8,128)S(1)}, u32[]{:S(2)}, u32[]{:S(2)}) %collective-permute-start.6) | collective-permute-done | bytes 184352 | tf_op jit(solution)/shard_map/ppermute | solution.py:492
  28.2 1.7 %collective-permute-start.4 = (f32[12,8,128]{2,1,0:T(8,128)S(1)}, f32[12,8,128]{2,1,0:T(8,128)S(1)}, u32[]{:S(2)}, u32[]{:S(2)}) collective-permute-start(f32[12,8,128]{2,1,0:T(8,128)S(1)} %get-tuple-element.77._), channel_id=1, source_target_pairs={{0,48},{1,32},{2,33},{3,34},{7,35},{6,39},{5,38},{4,37},{8,36},{9,... | collective-permute-start | bytes 147464 | tf_op jit(solution)/shard_map/ppermute | solution.py:458
  30.0 2.5 %collective-permute-done.3.from_below = f32[21,8,128]{2,1,0:T(8,128)S(1)} collective-permute-done((f32[21,8,128]{2,1,0:T(8,128)S(1)}, f32[21,8,128]{2,1,0:T(8,128)S(1)}, u32[]{:S(2)}, u32[]{:S(2)}) %collective-permute-start.3) | collective-permute-done | bytes 86048 | tf_op jit(solution)/shard_map/ppermute | solution.py:458
  32.5 0.4 shard_map.72
  32.9 0.4 collective-permute-start.8
  33.3 1.4 %collective-permute-start.9 = (f32[12,8,128]{2,1,0:T(8,128)S(1)}, f32[12,8,128]{2,1,0:T(8,128)S(1)}, u32[]{:S(2)}, u32[]{:S(2)}) collective-permute-start(f32[12,8,128]{2,1,0:T(8,128)S(1)} %get-tuple-element.83), channel_id=1, source_target_pairs={{0,48},{1,32},{2,33},{3,34},{7,35},{6,39},{5,38},{4,37},{8,36},{9,... | collective-permute-start | bytes 147464 | tf_op jit(solution)/shard_map/ppermute | solution.py:458
  34.9 0.6 shard_map.73
  35.5 1.0 %collective-permute-done.8.from_below = f32[12,8,128]{2,1,0:T(8,128)S(1)} collective-permute-done((f32[12,8,128]{2,1,0:T(8,128)S(1)}, f32[12,8,128]{2,1,0:T(8,128)S(1)}, u32[]{:S(2)}, u32[]{:S(2)}) %collective-permute-start.8) | collective-permute-done | bytes 49184 | tf_op jit(solution)/shard_map/ppermute | solution.py:458
  37.7 1.4 %collective-permute-start.11 = (f32[12,8,128]{2,1,0:T(8,128)S(1)}, f32[12,8,128]{2,1,0:T(8,128)S(1)}, u32[]{:S(2)}, u32[]{:S(2)}) collective-permute-start(f32[12,8,128]{2,1,0:T(8,128)S(1)} %get-tuple-element.91), channel_id=1, source_target_pairs={{0,48},{1,32},{2,33},{3,34},{7,35},{6,39},{5,38},{4,37},{8,36},{9,... | collective-permute-start | bytes 147464 | tf_op jit(solution)/shard_map/ppermute | solution.py:458
  39.4 2.2 %collective-permute-done.10.from_below = f32[21,8,128]{2,1,0:T(8,128)S(1)} collective-permute-done((f32[21,8,128]{2,1,0:T(8,128)S(1)}, f32[21,8,128]{2,1,0:T(8,128)S(1)}, u32[]{:S(2)}, u32[]{:S(2)}) %collective-permute-start.10) | collective-permute-done | bytes 86048 | tf_op jit(solution)/shard_map/ppermute | solution.py:458
  41.6 0.4 shard_map.79
  42.1 0.7 collective-permute-start.12
  42.7 1.3 %collective-permute-start.13 = (f32[18,8,128]{2,1,0:T(8,128)S(1)}, f32[18,8,128]{2,1,0:T(8,128)S(1)}, u32[]{:S(2)}, u32[]{:S(2)}) collective-permute-start(f32[18,8,128]{2,1,0:T(8,128)S(1)} %get-tuple-element.98), channel_id=1, source_target_pairs={{0,48},{1,32},{2,33},{3,34},{7,35},{6,39},{5,38},{4,37},{8,36},{9,... | collective-permute-start | bytes 221192 | tf_op jit(solution)/shard_map/ppermute | solution.py:458
  44.1 2.3 %collective-permute-done.12.from_below.rims_below = f32[18,8,128]{2,1,0:T(8,128)S(1)} collective-permute-done((f32[18,8,128]{2,1,0:T(8,128)S(1)}, f32[18,8,128]{2,1,0:T(8,128)S(1)}, u32[]{:S(2)}, u32[]{:S(2)}) %collective-permute-start.12) | collective-permute-done | bytes 73760 | tf_op jit(solution)/shard_map/ppermute | solution.py:458
  46.4 0.5 collective-permute-done.13.from_above.rims_above
  47.3 1.6 %collective-permute-start.14 = (f32[21,8,128]{2,1,0:T(8,128)S(1)}, f32[21,8,128]{2,1,0:T(8,128)S(1)}, u32[]{:S(2)}, u32[]{:S(2)}) collective-permute-start(f32[21,8,128]{2,1,0:T(8,128)S(1)} %get-tuple-element.105), channel_id=1, source_target_pairs={{0,33},{1,34},{2,35},{3,39},{7,38},{6,37},{5,36},{4,40},{8,41},{9,... | collective-permute-start | bytes 258056 | tf_op jit(solution)/shard_map/ppermute | solution.py:458
  49.3 2.5 %collective-permute-done.14.from_below = f32[21,8,128]{2,1,0:T(8,128)S(1)} collective-permute-done((f32[21,8,128]{2,1,0:T(8,128)S(1)}, f32[21,8,128]{2,1,0:T(8,128)S(1)}, u32[]{:S(2)}, u32[]{:S(2)}) %collective-permute-start.14) | collective-permute-done | bytes 86048 | tf_op jit(solution)/shard_map/ppermute | solution.py:458
  51.8 0.8 collective-permute-done.15.from_above
  52.6 0.5 shard_map.83
  53.1 0.7 collective-permute-start.16
  53.8 1.1 %collective-permute-start.17 = (f32[18,8,128]{2,1,0:T(8,128)S(1)}, f32[18,8,128]{2,1,0:T(8,128)S(1)}, u32[]{:S(2)}, u32[]{:S(2)}) collective-permute-start(f32[18,8,128]{2,1,0:T(8,128)S(1)} %get-tuple-element.113), channel_id=1, source_target_pairs={{0,48},{1,32},{2,33},{3,34},{7,35},{6,39},{5,38},{4,37},{8,36},{9,... | collective-permute-start | bytes 221192 | tf_op jit(solution)/shard_map/ppermute | solution.py:458
  54.9 2.5 %collective-permute-done.16.from_below.rims_below = f32[18,8,128]{2,1,0:T(8,128)S(1)} collective-permute-done((f32[18,8,128]{2,1,0:T(8,128)S(1)}, f32[18,8,128]{2,1,0:T(8,128)S(1)}, u32[]{:S(2)}, u32[]{:S(2)}) %collective-permute-start.16) | collective-permute-done | bytes 73760 | tf_op jit(solution)/shard_map/ppermute | solution.py:458
  57.4 0.6 collective-permute-done.17.from_above.rims_above
  58.5 0.7 collective-permute-start.18
  59.2 1.1 %collective-permute-start.19 = (f32[12,8,128]{2,1,0:T(8,128)S(1)}, f32[12,8,128]{2,1,0:T(8,128)S(1)}, u32[]{:S(2)}, u32[]{:S(2)}) collective-permute-start(f32[12,8,128]{2,1,0:T(8,128)S(1)} %get-tuple-element.121), channel_id=1, source_target_pairs={{0,48},{1,32},{2,33},{3,34},{7,35},{6,39},{5,38},{4,37},{8,36},{9,... | collective-permute-start | bytes 147464 | tf_op jit(solution)/shard_map/ppermute | solution.py:458
  60.4 2.6 %collective-permute-done.18.from_below = f32[21,8,128]{2,1,0:T(8,128)S(1)} collective-permute-done((f32[21,8,128]{2,1,0:T(8,128)S(1)}, f32[21,8,128]{2,1,0:T(8,128)S(1)}, u32[]{:S(2)}, u32[]{:S(2)}) %collective-permute-start.18) | collective-permute-done | bytes 86048 | tf_op jit(solution)/shard_map/ppermute | solution.py:458
  63.1 0.5 shard_map.87
  63.5 0.6 collective-permute-start.20
  64.1 1.2 %collective-permute-start.21 = (f32[18,8,128]{2,1,0:T(8,128)S(1)}, f32[18,8,128]{2,1,0:T(8,128)S(1)}, u32[]{:S(2)}, u32[]{:S(2)}) collective-permute-start(f32[18,8,128]{2,1,0:T(8,128)S(1)} %get-tuple-element.128), channel_id=1, source_target_pairs={{0,48},{1,32},{2,33},{3,34},{7,35},{6,39},{5,38},{4,37},{8,36},{9,... | collective-permute-start | bytes 221192 | tf_op jit(solution)/shard_map/ppermute | solution.py:458
  65.4 2.5 %collective-permute-done.20.from_below.rims_below = f32[18,8,128]{2,1,0:T(8,128)S(1)} collective-permute-done((f32[18,8,128]{2,1,0:T(8,128)S(1)}, f32[18,8,128]{2,1,0:T(8,128)S(1)}, u32[]{:S(2)}, u32[]{:S(2)}) %collective-permute-start.20) | collective-permute-done | bytes 73760 | tf_op jit(solution)/shard_map/ppermute | solution.py:458
  68.3 0.4 shard_map.88
  68.7 0.8 collective-permute-start.22
  69.5 1.0 %collective-permute-start.23 = (f32[12,8,128]{2,1,0:T(8,128)S(1)}, f32[12,8,128]{2,1,0:T(8,128)S(1)}, u32[]{:S(2)}, u32[]{:S(2)}) collective-permute-start(f32[12,8,128]{2,1,0:T(8,128)S(1)} %get-tuple-element.133), channel_id=1, source_target_pairs={{0,48},{1,32},{2,33},{3,34},{7,35},{6,39},{5,38},{4,37},{8,36},{9,... | collective-permute-start | bytes 147464 | tf_op jit(solution)/shard_map/ppermute | solution.py:458
  71.2 1.3 %collective-permute-done.22.from_below = f32[12,8,128]{2,1,0:T(8,128)S(1)} collective-permute-done((f32[12,8,128]{2,1,0:T(8,128)S(1)}, f32[12,8,128]{2,1,0:T(8,128)S(1)}, u32[]{:S(2)}, u32[]{:S(2)}) %collective-permute-start.22) | collective-permute-done | bytes 49184 | tf_op jit(solution)/shard_map/ppermute | solution.py:458
  72.5 0.7 collective-permute-done.23.from_above
  73.7 1.2 %collective-permute-done.24.other = f32[24,8,128]{2,1,0:T(8,128)S(1)} collective-permute-done((f32[24,8,128]{2,1,0:T(8,128)S(1)}, f32[24,8,128]{2,1,0:T(8,128)S(1)}, u32[]{:S(2)}, u32[]{:S(2)}) %collective-permute-start.24) | collective-permute-done | bytes 98336 | tf_op jit(solution)/shard_map/ppermute | solution.py:556
  74.9 7.0 %collective-permute-start.25 = (f32[24,8,128]{2,1,0:T(8,128)S(1)}, f32[24,8,128]{2,1,0:T(8,128)S(1)}, u32[]{:S(2)}, u32[]{:S(2)}) collective-permute-start(f32[24,8,128]{2,1,0:T(8,128)S(1)} %shard_map.94), channel_id=1, source_target_pairs={{0,0},{1,1},{2,2},{3,3},{7,4},{6,5},{5,6},{4,7},{8,8},{9,9},{10,10... | collective-permute-start | bytes 294920 | tf_op jit(solution)/shard_map/ppermute | solution.py:560
  81.9 2.5 %collective-permute-start.26 = (f32[24,8,128]{2,1,0:T(8,128)S(1)}, f32[24,8,128]{2,1,0:T(8,128)S(1)}, u32[]{:S(2)}, u32[]{:S(2)}) collective-permute-start(f32[24,8,128]{2,1,0:T(8,128)S(1)} %shard_map.93.rest_0_), channel_id=1, source_target_pairs={{0,64},{1,65},{2,66},{3,67},{7,68},{6,69},{5,70},{4,71},{8,72},{9,... | collective-permute-start | bytes 294920 | tf_op jit(solution)/shard_map/ppermute | solution.py:558
  84.4 5.8 %collective-permute-done.26.got1 = f32[24,8,128]{2,1,0:T(8,128)S(1)} collective-permute-done((f32[24,8,128]{2,1,0:T(8,128)S(1)}, f32[24,8,128]{2,1,0:T(8,128)S(1)}, u32[]{:S(2)}, u32[]{:S(2)}) %collective-permute-start.26) | collective-permute-done | bytes 98336 | tf_op jit(solution)/shard_map/ppermute | solution.py:558
  90.3 0.7 copy.13
  (49 shorter events, 5.5 us)
Async XLA Ops:
  1.4 5.1 %copy-start = (f32[2,3,2,4,2,512]{5,4,3,2,1,0:T(2,128)S(1)}, f32[2,3,2,4,2,512]{5,4,3,2,1,0:T(2,128)}, u32[]{:S(2)}) copy-start(f32[2,3,2,4,2,512]{5,4,3,2,1,0:T(2,128)} %param.7) | copy-start | bytes 589828
  1.4 14.7 %collective-permute-start = (f32[66,8,128]{2,1,0:T(8,128)S(1)}, f32[66,8,128]{2,1,0:T(8,128)S(1)}, u32[]{:S(2)}, u32[]{:S(2)}) collective-permute-start(f32[66,8,128]{2,1,0:T(8,128)S(1)} %shard_map.65), channel_id=1, source_target_pairs={{0,0},{1,1},{2,2},{3,3},{4,7},{5,6},{6,5},{7,4},{8,8},{9,9},{10,10... | collective-permute-start | bytes 811016 | tf_op jit(solution)/shard_map/ppermute | solution.py:488
  6.5 13.6 %collective-permute-start.5 = (f32[57,8,128]{2,1,0:T(8,128)S(1)}, f32[57,8,128]{2,1,0:T(8,128)S(1)}, u32[]{:S(2)}, u32[]{:S(2)}) collective-permute-start(f32[57,8,128]{2,1,0:T(8,128)S(1)} %shard_map.69), channel_id=1, source_target_pairs={{0,0},{1,1},{2,2},{3,3},{4,7},{5,6},{6,5},{7,4},{8,8},{9,9},{10,10... | collective-permute-start | bytes 700424 | tf_op jit(solution)/shard_map/ppermute | solution.py:490
  16.1 7.6 %collective-permute-start.1 = (f32[54,8,128]{2,1,0:T(8,128)S(1)}, f32[54,8,128]{2,1,0:T(8,128)S(1)}, u32[]{:S(2)}, u32[]{:S(2)}) collective-permute-start(f32[54,8,128]{2,1,0:T(8,128)S(1)} %slice.8), channel_id=1, source_target_pairs={{0,64},{1,65},{2,66},{3,67},{7,71},{6,70},{5,69},{4,68},{8,72},{9,... | collective-permute-start | bytes 663560 | tf_op jit(solution)/shard_map/ppermute | solution.py:491
  20.1 7.4 %collective-permute-start.6 = (f32[45,8,128]{2,1,0:T(8,128)S(1)}, f32[45,8,128]{2,1,0:T(8,128)S(1)}, u32[]{:S(2)}, u32[]{:S(2)}) collective-permute-start(f32[45,8,128]{2,1,0:T(8,128)S(1)} %slice.9), channel_id=1, source_target_pairs={{0,64},{1,65},{2,66},{3,67},{7,71},{6,70},{5,69},{4,68},{8,72},{9,... | collective-permute-start | bytes 552968 | tf_op jit(solution)/shard_map/ppermute | solution.py:492
  23.8 4.1 %collective-permute-start.2 = (f32[108,8,128]{2,1,0:T(8,128)S(1)}, f32[108,8,128]{2,1,0:T(8,128)S(1)}, u32[]{:S(2)}, u32[]{:S(2)}) collective-permute-start(f32[108,8,128]{2,1,0:T(8,128)S(1)} %shard_map.66), channel_id=1, source_target_pairs={{0,32},{1,33},{2,34},{3,35},{7,39},{6,38},{5,37},{4,36},{8,40},{9,... | collective-permute-start | bytes 1327112 | tf_op jit(solution)/shard_map/ppermute | solution.py:496
  27.6 2.3 %collective-permute-start.7 = (f32[90,8,128]{2,1,0:T(8,128)S(1)}, f32[90,8,128]{2,1,0:T(8,128)S(1)}, u32[]{:S(2)}, u32[]{:S(2)}) collective-permute-start(f32[90,8,128]{2,1,0:T(8,128)S(1)} %shard_map.70), channel_id=1, source_target_pairs={{0,32},{1,33},{2,34},{3,35},{7,39},{6,38},{5,37},{4,36},{8,40},{9,... | collective-permute-start | bytes 1105928 | tf_op jit(solution)/shard_map/ppermute | solution.py:500
  28.1 4.3 %collective-permute-start.3 = (f32[21,8,128]{2,1,0:T(8,128)S(1)}, f32[21,8,128]{2,1,0:T(8,128)S(1)}, u32[]{:S(2)}, u32[]{:S(2)}) collective-permute-start(f32[21,8,128]{2,1,0:T(8,128)S(1)} %get-tuple-element.76), channel_id=1, source_target_pairs={{0,33},{1,34},{2,35},{3,39},{7,38},{6,37},{5,36},{4,40},{8,41},{9,... | collective-permute-start | bytes 258056 | tf_op jit(solution)/shard_map/ppermute | solution.py:458
  28.2 4.3 %collective-permute-start.4 = (f32[12,8,128]{2,1,0:T(8,128)S(1)}, f32[12,8,128]{2,1,0:T(8,128)S(1)}, u32[]{:S(2)}, u32[]{:S(2)}) collective-permute-start(f32[12,8,128]{2,1,0:T(8,128)S(1)} %get-tuple-element.77._), channel_id=1, source_target_pairs={{0,48},{1,32},{2,33},{3,34},{7,35},{6,39},{5,38},{4,37},{8,36},{9,... | collective-permute-start | bytes 147464 | tf_op jit(solution)/shard_map/ppermute | solution.py:458
  32.9 3.6 %collective-permute-start.8 = (f32[12,8,128]{2,1,0:T(8,128)S(1)}, f32[12,8,128]{2,1,0:T(8,128)S(1)}, u32[]{:S(2)}, u32[]{:S(2)}) collective-permute-start(f32[12,8,128]{2,1,0:T(8,128)S(1)} %get-tuple-element.82), channel_id=1, source_target_pairs={{0,33},{1,34},{2,35},{3,39},{7,38},{6,37},{5,36},{4,40},{8,41},{9,... | collective-permute-start | bytes 147464 | tf_op jit(solution)/shard_map/ppermute | solution.py:458
  33.3 1.6 %copy-start.1 = (s32[4]{0:T(128)S(1)}, s32[4]{0:T(128)}, u32[]{:S(2)}) copy-start(s32[4]{0:T(128)} %source_slice.1) | copy-start | bytes 52
  33.3 3.5 %collective-permute-start.9 = (f32[12,8,128]{2,1,0:T(8,128)S(1)}, f32[12,8,128]{2,1,0:T(8,128)S(1)}, u32[]{:S(2)}, u32[]{:S(2)}) collective-permute-start(f32[12,8,128]{2,1,0:T(8,128)S(1)} %get-tuple-element.83), channel_id=1, source_target_pairs={{0,48},{1,32},{2,33},{3,34},{7,35},{6,39},{5,38},{4,37},{8,36},{9,... | collective-permute-start | bytes 147464 | tf_op jit(solution)/shard_map/ppermute | solution.py:458
  37.3 4.3 %collective-permute-start.10 = (f32[21,8,128]{2,1,0:T(8,128)S(1)}, f32[21,8,128]{2,1,0:T(8,128)S(1)}, u32[]{:S(2)}, u32[]{:S(2)}) collective-permute-start(f32[21,8,128]{2,1,0:T(8,128)S(1)} %get-tuple-element.90), channel_id=1, source_target_pairs={{0,33},{1,34},{2,35},{3,39},{7,38},{6,37},{5,36},{4,40},{8,41},{9,... | collective-permute-start | bytes 258056 | tf_op jit(solution)/shard_map/ppermute | solution.py:458
  37.7 4.0 %collective-permute-start.11 = (f32[12,8,128]{2,1,0:T(8,128)S(1)}, f32[12,8,128]{2,1,0:T(8,128)S(1)}, u32[]{:S(2)}, u32[]{:S(2)}) collective-permute-start(f32[12,8,128]{2,1,0:T(8,128)S(1)} %get-tuple-element.91), channel_id=1, source_target_pairs={{0,48},{1,32},{2,33},{3,34},{7,35},{6,39},{5,38},{4,37},{8,36},{9,... | collective-permute-start | bytes 147464 | tf_op jit(solution)/shard_map/ppermute | solution.py:458
  42.1 4.3 %collective-permute-start.12 = (f32[18,8,128]{2,1,0:T(8,128)S(1)}, f32[18,8,128]{2,1,0:T(8,128)S(1)}, u32[]{:S(2)}, u32[]{:S(2)}) collective-permute-start(f32[18,8,128]{2,1,0:T(8,128)S(1)} %get-tuple-element.97), channel_id=1, source_target_pairs={{0,33},{1,34},{2,35},{3,39},{7,38},{6,37},{5,36},{4,40},{8,41},{9,... | collective-permute-start | bytes 221192 | tf_op jit(solution)/shard_map/ppermute | solution.py:458
  42.7 4.1 %collective-permute-start.13 = (f32[18,8,128]{2,1,0:T(8,128)S(1)}, f32[18,8,128]{2,1,0:T(8,128)S(1)}, u32[]{:S(2)}, u32[]{:S(2)}) collective-permute-start(f32[18,8,128]{2,1,0:T(8,128)S(1)} %get-tuple-element.98), channel_id=1, source_target_pairs={{0,48},{1,32},{2,33},{3,34},{7,35},{6,39},{5,38},{4,37},{8,36},{9,... | collective-permute-start | bytes 221192 | tf_op jit(solution)/shard_map/ppermute | solution.py:458
  47.3 4.5 %collective-permute-start.14 = (f32[21,8,128]{2,1,0:T(8,128)S(1)}, f32[21,8,128]{2,1,0:T(8,128)S(1)}, u32[]{:S(2)}, u32[]{:S(2)}) collective-permute-start(f32[21,8,128]{2,1,0:T(8,128)S(1)} %get-tuple-element.105), channel_id=1, source_target_pairs={{0,33},{1,34},{2,35},{3,39},{7,38},{6,37},{5,36},{4,40},{8,41},{9,... | collective-permute-start | bytes 258056 | tf_op jit(solution)/shard_map/ppermute | solution.py:458
  48.9 3.7 %collective-permute-start.15 = (f32[12,8,128]{2,1,0:T(8,128)S(1)}, f32[12,8,128]{2,1,0:T(8,128)S(1)}, u32[]{:S(2)}, u32[]{:S(2)}) collective-permute-start(f32[12,8,128]{2,1,0:T(8,128)S(1)} %get-tuple-element.106), channel_id=1, source_target_pairs={{0,48},{1,32},{2,33},{3,34},{7,35},{6,39},{5,38},{4,37},{8,36},{9,... | collective-permute-start | bytes 147464 | tf_op jit(solution)/shard_map/ppermute | solution.py:458
  53.1 4.3 %collective-permute-start.16 = (f32[18,8,128]{2,1,0:T(8,128)S(1)}, f32[18,8,128]{2,1,0:T(8,128)S(1)}, u32[]{:S(2)}, u32[]{:S(2)}) collective-permute-start(f32[18,8,128]{2,1,0:T(8,128)S(1)} %get-tuple-element.112), channel_id=1, source_target_pairs={{0,33},{1,34},{2,35},{3,39},{7,38},{6,37},{5,36},{4,40},{8,41},{9,... | collective-permute-start | bytes 221192 | tf_op jit(solution)/shard_map/ppermute | solution.py:458
  53.8 4.3 %collective-permute-start.17 = (f32[18,8,128]{2,1,0:T(8,128)S(1)}, f32[18,8,128]{2,1,0:T(8,128)S(1)}, u32[]{:S(2)}, u32[]{:S(2)}) collective-permute-start(f32[18,8,128]{2,1,0:T(8,128)S(1)} %get-tuple-element.113), channel_id=1, source_target_pairs={{0,48},{1,32},{2,33},{3,34},{7,35},{6,39},{5,38},{4,37},{8,36},{9,... | collective-permute-start | bytes 221192 | tf_op jit(solution)/shard_map/ppermute | solution.py:458
  58.5 4.6 %collective-permute-start.18 = (f32[21,8,128]{2,1,0:T(8,128)S(1)}, f32[21,8,128]{2,1,0:T(8,128)S(1)}, u32[]{:S(2)}, u32[]{:S(2)}) collective-permute-start(f32[21,8,128]{2,1,0:T(8,128)S(1)} %get-tuple-element.120), channel_id=1, source_target_pairs={{0,33},{1,34},{2,35},{3,39},{7,38},{6,37},{5,36},{4,40},{8,41},{9,... | collective-permute-start | bytes 258056 | tf_op jit(solution)/shard_map/ppermute | solution.py:458
  59.2 3.9 %collective-permute-start.19 = (f32[12,8,128]{2,1,0:T(8,128)S(1)}, f32[12,8,128]{2,1,0:T(8,128)S(1)}, u32[]{:S(2)}, u32[]{:S(2)}) collective-permute-start(f32[12,8,128]{2,1,0:T(8,128)S(1)} %get-tuple-element.121), channel_id=1, source_target_pairs={{0,48},{1,32},{2,33},{3,34},{7,35},{6,39},{5,38},{4,37},{8,36},{9,... | collective-permute-start | bytes 147464 | tf_op jit(solution)/shard_map/ppermute | solution.py:458
  63.5 4.3 %collective-permute-start.20 = (f32[18,8,128]{2,1,0:T(8,128)S(1)}, f32[18,8,128]{2,1,0:T(8,128)S(1)}, u32[]{:S(2)}, u32[]{:S(2)}) collective-permute-start(f32[18,8,128]{2,1,0:T(8,128)S(1)} %get-tuple-element.127), channel_id=1, source_target_pairs={{0,33},{1,34},{2,35},{3,39},{7,38},{6,37},{5,36},{4,40},{8,41},{9,... | collective-permute-start | bytes 221192 | tf_op jit(solution)/shard_map/ppermute | solution.py:458
  64.1 4.1 %collective-permute-start.21 = (f32[18,8,128]{2,1,0:T(8,128)S(1)}, f32[18,8,128]{2,1,0:T(8,128)S(1)}, u32[]{:S(2)}, u32[]{:S(2)}) collective-permute-start(f32[18,8,128]{2,1,0:T(8,128)S(1)} %get-tuple-element.128), channel_id=1, source_target_pairs={{0,48},{1,32},{2,33},{3,34},{7,35},{6,39},{5,38},{4,37},{8,36},{9,... | collective-permute-start | bytes 221192 | tf_op jit(solution)/shard_map/ppermute | solution.py:458
  68.7 3.8 %collective-permute-start.22 = (f32[12,8,128]{2,1,0:T(8,128)S(1)}, f32[12,8,128]{2,1,0:T(8,128)S(1)}, u32[]{:S(2)}, u32[]{:S(2)}) collective-permute-start(f32[12,8,128]{2,1,0:T(8,128)S(1)} %get-tuple-element.132), channel_id=1, source_target_pairs={{0,33},{1,34},{2,35},{3,39},{7,38},{6,37},{5,36},{4,40},{8,41},{9,... | collective-permute-start | bytes 147464 | tf_op jit(solution)/shard_map/ppermute | solution.py:458
  69.5 3.7 %collective-permute-start.23 = (f32[12,8,128]{2,1,0:T(8,128)S(1)}, f32[12,8,128]{2,1,0:T(8,128)S(1)}, u32[]{:S(2)}, u32[]{:S(2)}) collective-permute-start(f32[12,8,128]{2,1,0:T(8,128)S(1)} %get-tuple-element.133), channel_id=1, source_target_pairs={{0,48},{1,32},{2,33},{3,34},{7,35},{6,39},{5,38},{4,37},{8,36},{9,... | collective-permute-start | bytes 147464 | tf_op jit(solution)/shard_map/ppermute | solution.py:458
  73.5 1.4 %collective-permute-start.24 = (f32[24,8,128]{2,1,0:T(8,128)S(1)}, f32[24,8,128]{2,1,0:T(8,128)S(1)}, u32[]{:S(2)}, u32[]{:S(2)}) collective-permute-start(f32[24,8,128]{2,1,0:T(8,128)S(1)} %get-tuple-element.138), channel_id=1, source_target_pairs={{0,32},{1,33},{2,34},{3,35},{7,39},{6,38},{5,37},{4,36},{8,40},{9,... | collective-permute-start | bytes 294920 | tf_op jit(solution)/shard_map/ppermute | solution.py:556
  74.9 9.6 %collective-permute-start.25 = (f32[24,8,128]{2,1,0:T(8,128)S(1)}, f32[24,8,128]{2,1,0:T(8,128)S(1)}, u32[]{:S(2)}, u32[]{:S(2)}) collective-permute-start(f32[24,8,128]{2,1,0:T(8,128)S(1)} %shard_map.94), channel_id=1, source_target_pairs={{0,0},{1,1},{2,2},{3,3},{7,4},{6,5},{5,6},{4,7},{8,8},{9,9},{10,10... | collective-permute-start | bytes 294920 | tf_op jit(solution)/shard_map/ppermute | solution.py:560
  81.9 8.3 %collective-permute-start.26 = (f32[24,8,128]{2,1,0:T(8,128)S(1)}, f32[24,8,128]{2,1,0:T(8,128)S(1)}, u32[]{:S(2)}, u32[]{:S(2)}) collective-permute-start(f32[24,8,128]{2,1,0:T(8,128)S(1)} %shard_map.93.rest_0_), channel_id=1, source_target_pairs={{0,64},{1,65},{2,66},{3,67},{7,68},{6,69},{5,70},{4,71},{8,72},{9,... | collective-permute-start | bytes 294920 | tf_op jit(solution)/shard_map/ppermute | solution.py:558

commit v3 on v2

--- a/solution.py
+++ b/solution.py
@@ -187,15 +187,15 @@
     store(above_ref, column, [jnp.where(lower, t, f) for f, t in zip(field, turned)])
 
 
-def two_laplacians(field, partial, from_below, from_above, links, inner, outer, lower):
-    beyond = [
-        swap_planes(jnp.where(lower, s, a)) for a, s in zip(from_below, from_above)
-    ]
-    rim = [jnp.where(lower, a, s) for a, s in zip(from_below, from_above)]
+def two_laplacians(partial, beyond, rim, links, inner, outer):
     single = product(link_at(outer, 0), beyond, False, partial)
-    rim = product(link_at(outer, 0), field, True, rim)
-    double = product(link_at(outer, 0), rim, False, within(links, inner, single))
-    return single, double
+    return single, product(link_at(outer, 0), rim, False, within(links, inner, single))
+
+
+def arrived(from_below, from_above, lower):
+    below, above = load(from_below, 0), load(from_above, 0)
+    beyond = [swap_planes(jnp.where(lower, a, b)) for a, b in zip(above, below)]
+    return beyond, [jnp.where(lower, b, a) for a, b in zip(above, below)]
 
 
 def kernel_call(body, inputs, outputs, far=(), near=(), scratch=()):
@@ -334,12 +334,18 @@
         pick(first + at, own, facing, beside, marks, 45, others)
 
 
-def step_a(field, partial, from_below, from_above, links, inner, outer, others, lower):
-    single, double = two_laplacians(field, partial, from_below, from_above, links, inner, outer, lower)
-    spin = spin_term(others, field)
+def aside(field, outer, others, base, back):
+    values = load(field, 0)
+    spin = spin_term(others, values)
+    store(base, 0, [v + (0.5 * SPIN_WEIGHT) * b for v, b in zip(values, spin)])
+    store(back, 0, product(link_at(outer, 0), values, True))
+
+
+def step_a(base, back, partial, from_below, from_above, links, inner, outer, lower):
+    beyond, rim = arrived(from_below, from_above, lower)
+    single, double = two_laplacians(load(partial, 0), beyond, add(rim, load(back, 0)), links, inner, outer)
     return [
-        f + (0.5 * KINETIC) * s + (0.5 * QUARTIC) * d + (0.5 * SPIN_WEIGHT) * b
-        for f, s, d, b in zip(field, single, double, spin)
+        f + (0.5 * KINETIC) * s + (0.5 * QUARTIC) * d for f, s, d in zip(load(base, 0), single, double)
     ]
 
 
@@ -352,13 +358,10 @@
             out[at] = weight * others[45 + at]
 
 
-def first_half(field, partial, from_below, from_above, links, inner, outer, others, *rest):
+def first_half(base, back, partial, from_below, from_above, links, inner, outer, others, *rest):
     rims, (turned_field, *messages) = rest[:-4], rest[-4:]
     lower = rows_of((8, 128)) % 2 == 0
-    values = step_a(
-        load(field, 0), load(partial, 0), load(from_below, 0), load(from_above, 0),
-        links, inner, outer, others, lower,
-    )
+    values = step_a(base, back, partial, from_below, from_above, links, inner, outer, lower)
     values = product(link_at(others, TIME), values, True)
     store(turned_field, 0, values)
     prepare(values, links, inner, lower, *messages, 0)
@@ -366,12 +369,9 @@
         message[pl.ds(12, 6)] = rim[...]
 
 
-def second_half(field, partial, from_below, from_above, links, inner, outer, others, source, *rest):
+def second_half(base, back, partial, from_below, from_above, links, inner, outer, source, *rest):
     lower = rows_of((8, 128)) % 2 == 0
-    values = step_a(
-        load(field, 0), load(partial, 0), load(from_below, 0), load(from_above, 0),
-        links, inner, outer, others, lower,
-    )
+    values = step_a(base, back, partial, from_below, from_above, links, inner, outer, lower)
     values = add(values, load(source, 0))
     if len(rest) == 4:
         result, *messages = rest
@@ -395,9 +395,8 @@
 
 
 def smeared(field, partial, beyond, rim, links, inner, outer):
-    single = product(link_at(outer, 0), beyond, False, partial)
     rim = product(link_at(outer, 0), field, True, rim)
-    double = product(link_at(outer, 0), rim, False, within(links, inner, single))
+    single, double = two_laplacians(partial, beyond, rim, links, inner, outer)
     return [
         f + (2 * SMEAR_WEIGHT) * s + (SMEAR_WEIGHT * SMEAR_WEIGHT) * d
         for f, s, d in zip(field, single, double)
@@ -524,8 +523,9 @@
         around = [links[timeslice], inner[timeslice], outer[timeslice], others[timeslice]]
         size = WITH_RIM if rims else FIELD
         before = [from_below, from_above]
+        apart = kernel_call(aside, [field, outer[-1], others[timeslice]], [FIELD] * 2)
         field, partial, to_below, to_above = kernel_call(
-            first_half, [field, partial, *before, *around, *rims], [FIELD, FIELD, size, size]
+            first_half, [*apart, partial, *before, *around, *rims], [FIELD, FIELD, size, size]
         )
         from_below, from_above = exchange(to_below, to_above)
         if rims:
@@ -535,7 +535,8 @@
                 [result, smear_partial, *before, from_below, from_above, links[at], inner[at], outer[at]],
                 [FIELD],
             )
-        inputs = [field, partial, from_below, from_above] + around + [sources[timeslice]]
+        apart = kernel_call(aside, [field, outer[-1], others[timeslice]], [FIELD] * 2)
+        inputs = [*apart, partial, from_below, from_above, *around[:3], sources[timeslice]]
         if timeslice + 1 < SLICES:
             after = [links[timeslice + 1], inner[timeslice + 1], edge[timeslice + 1]]
             field, partial, to_below, to_above = kernel_call(

time: 91.1 us -> 90.7 us (level)
    pallas_call x32 -> x40, Pallas kernels: 7.36 us -> 7.38 us  [kernel_call(): pl.pallas_call(body, in_specs=[pl.BlockSpec(memory_space=space) for space...]
where the time goes in v3:
time: 90.7 us; the launch traced here: 90.5 us
  starting transfers between devices  41.7 us (46%)
  waiting for transfers between devices  40 us (44%)
  Pallas kernels  7.38 us (8%)
    ppermute x9, waiting for transfers between devices, exchange(): lax.ppermute(to_above, AXES, UP)  19.1 us
    ppermute x9, starting transfers between devices, exchange(): lax.ppermute(to_below, AXES, DOWN)  10.4 us
    pallas_call x40, Pallas kernels, kernel_call(): pl.pallas_call(body, in_specs=[pl.BlockSpec(memory_space=space) for space...  7.38 us
    ppermute x1, starting transfers between devices, local(): got0 = lax.ppermute(out0, AXES, COLLECT[0])  6.77 us
    ppermute x9, starting transfers between devices, exchange(): lax.ppermute(to_above, AXES, UP)  6.14 us
    ppermute x1, waiting for transfers between devices, local(): got1 = lax.ppermute(out1, AXES, COLLECT[1])  5.8 us
    ppermute x1, waiting for transfers between devices, local(): links_own = lax.ppermute(message, AXES, SPREAD)  5.26 us
    ppermute x1, starting transfers between devices, local(): links_own = lax.ppermute(message, AXES, SPREAD)  5.05 us
  transfers between devices with their start and end apart: 27, of which 21 were waited for; matrix products, arithmetic and copies ran while one was open for 0% of the time, Pallas kernels for 3%

profile of v3, /device:TPU:32, one launch (start us, length us, event | category | flops | bytes accessed | tf_op | source)
XLA Modules:
  0.0 90.5 jit_solution(3221490527518128807)
XLA Ops:
  0.1 1.2 %shard_map.64 = (f32[99,8,128]{2,1,0:T(8,128)S(1)}, f32[6,2,4,8,128]{4,3,2,1,0:T(8,128)S(1)}) custom-call(f32[54,8,128]{2,1,0:T(8,128)} %bitcast.36, f32[18,8,128]{2,1,0:T(8,128)} %bitcast.39, f32[54,8,128]{2,1,0:T(8,128)} %bitcast.37, f32[6,2,4,8,128]{4,3,2,1,0:T(8,128)} %bitcast.38), custom_call_target="tpu_custom_call" | custom-call | tf_op jit(solution)/shard_map/pallas_call | solution.py:209
  1.4 5.1 %collective-permute-start = (f32[66,8,128]{2,1,0:T(8,128)S(1)}, f32[66,8,128]{2,1,0:T(8,128)S(1)}, u32[]{:S(2)}, u32[]{:S(2)}) collective-permute-start(f32[66,8,128]{2,1,0:T(8,128)S(1)} %shard_map.65), channel_id=1, source_target_pairs={{0,0},{1,1},{2,2},{3,3},{4,7},{5,6},{6,5},{7,4},{8,8},{9,9},{10,10... | collective-permute-start | bytes 811016 | tf_op jit(solution)/shard_map/ppermute | solution.py:487
  6.5 4.3 %collective-permute-start.4 = (f32[57,8,128]{2,1,0:T(8,128)S(1)}, f32[57,8,128]{2,1,0:T(8,128)S(1)}, u32[]{:S(2)}, u32[]{:S(2)}) collective-permute-start(f32[57,8,128]{2,1,0:T(8,128)S(1)} %shard_map.69), channel_id=1, source_target_pairs={{0,0},{1,1},{2,2},{3,3},{4,7},{5,6},{6,5},{7,4},{8,8},{9,9},{10,10... | collective-permute-start | bytes 700424 | tf_op jit(solution)/shard_map/ppermute | solution.py:489
  10.8 5.3 %collective-permute-done.own = f32[66,8,128]{2,1,0:T(8,128)S(1)} collective-permute-done((f32[66,8,128]{2,1,0:T(8,128)S(1)}, f32[66,8,128]{2,1,0:T(8,128)S(1)}, u32[]{:S(2)}, u32[]{:S(2)}) %collective-permute-start) | collective-permute-done | bytes 270368 | tf_op jit(solution)/shard_map/ppermute | solution.py:487
  16.1 3.1 %collective-permute-start.1 = (f32[54,8,128]{2,1,0:T(8,128)S(1)}, f32[54,8,128]{2,1,0:T(8,128)S(1)}, u32[]{:S(2)}, u32[]{:S(2)}) collective-permute-start(f32[54,8,128]{2,1,0:T(8,128)S(1)} %slice.8), channel_id=1, source_target_pairs={{0,64},{1,65},{2,66},{3,67},{7,71},{6,70},{5,69},{4,68},{8,72},{9,... | collective-permute-start | bytes 663560 | tf_op jit(solution)/shard_map/ppermute | solution.py:490
  19.2 1.0 %collective-permute-done.4.own.others = f32[57,8,128]{2,1,0:T(8,128)S(1)} collective-permute-done((f32[57,8,128]{2,1,0:T(8,128)S(1)}, f32[57,8,128]{2,1,0:T(8,128)S(1)}, u32[]{:S(2)}, u32[]{:S(2)}) %collective-permute-start.4) | collective-permute-done | bytes 233504 | tf_op jit(solution)/shard_map/ppermute | solution.py:489
  20.1 3.1 %collective-permute-start.5 = (f32[45,8,128]{2,1,0:T(8,128)S(1)}, f32[45,8,128]{2,1,0:T(8,128)S(1)}, u32[]{:S(2)}, u32[]{:S(2)}) collective-permute-start(f32[45,8,128]{2,1,0:T(8,128)S(1)} %slice.9), channel_id=1, source_target_pairs={{0,64},{1,65},{2,66},{3,67},{7,71},{6,70},{5,69},{4,68},{8,72},{9,... | collective-permute-start | bytes 552968 | tf_op jit(solution)/shard_map/ppermute | solution.py:491
  23.2 0.5 collective-permute-done.1.facing
  23.9 3.7 %collective-permute-done.5.facing = f32[45,8,128]{2,1,0:T(8,128)S(1)} collective-permute-done((f32[45,8,128]{2,1,0:T(8,128)S(1)}, f32[45,8,128]{2,1,0:T(8,128)S(1)}, u32[]{:S(2)}, u32[]{:S(2)}) %collective-permute-start.5) | collective-permute-done | bytes 184352 | tf_op jit(solution)/shard_map/ppermute | solution.py:491
  28.2 1.7 %collective-permute-start.7 = (f32[12,8,128]{2,1,0:T(8,128)S(1)}, f32[12,8,128]{2,1,0:T(8,128)S(1)}, u32[]{:S(2)}, u32[]{:S(2)}) collective-permute-start(f32[12,8,128]{2,1,0:T(8,128)S(1)} %get-tuple-element.96._), channel_id=1, source_target_pairs={{0,48},{1,32},{2,33},{3,34},{7,35},{6,39},{5,38},{4,37},{8,36},{9,... | collective-permute-start | bytes 147464 | tf_op jit(solution)/shard_map/ppermute | solution.py:457
  30.0 2.4 %collective-permute-done.3.from_below = f32[21,8,128]{2,1,0:T(8,128)S(1)} collective-permute-done((f32[21,8,128]{2,1,0:T(8,128)S(1)}, f32[21,8,128]{2,1,0:T(8,128)S(1)}, u32[]{:S(2)}, u32[]{:S(2)}) %collective-permute-start.3) | collective-permute-done | bytes 86048 | tf_op jit(solution)/shard_map/ppermute | solution.py:457
  32.5 0.4 shard_map.73
  32.9 0.4 collective-permute-start.8
  33.4 1.4 %collective-permute-start.9 = (f32[12,8,128]{2,1,0:T(8,128)S(1)}, f32[12,8,128]{2,1,0:T(8,128)S(1)}, u32[]{:S(2)}, u32[]{:S(2)}) collective-permute-start(f32[12,8,128]{2,1,0:T(8,128)S(1)} %get-tuple-element.103), channel_id=1, source_target_pairs={{0,48},{1,32},{2,33},{3,34},{7,35},{6,39},{5,38},{4,37},{8,36},{9,... | collective-permute-start | bytes 147464 | tf_op jit(solution)/shard_map/ppermute | solution.py:457
  35.0 0.6 shard_map.75
  35.6 0.9 %collective-permute-done.8.from_below = f32[12,8,128]{2,1,0:T(8,128)S(1)} collective-permute-done((f32[12,8,128]{2,1,0:T(8,128)S(1)}, f32[12,8,128]{2,1,0:T(8,128)S(1)}, u32[]{:S(2)}, u32[]{:S(2)}) %collective-permute-start.8) | collective-permute-done | bytes 49184 | tf_op jit(solution)/shard_map/ppermute | solution.py:457
  37.2 0.4 collective-permute-start.10
  37.6 1.4 %collective-permute-start.11 = (f32[12,8,128]{2,1,0:T(8,128)S(1)}, f32[12,8,128]{2,1,0:T(8,128)S(1)}, u32[]{:S(2)}, u32[]{:S(2)}) collective-permute-start(f32[12,8,128]{2,1,0:T(8,128)S(1)} %get-tuple-element.114), channel_id=1, source_target_pairs={{0,48},{1,32},{2,33},{3,34},{7,35},{6,39},{5,38},{4,37},{8,36},{9,... | collective-permute-start | bytes 147464 | tf_op jit(solution)/shard_map/ppermute | solution.py:457
  39.4 2.2 %collective-permute-done.10.from_below = f32[21,8,128]{2,1,0:T(8,128)S(1)} collective-permute-done((f32[21,8,128]{2,1,0:T(8,128)S(1)}, f32[21,8,128]{2,1,0:T(8,128)S(1)}, u32[]{:S(2)}, u32[]{:S(2)}) %collective-permute-start.10) | collective-permute-done | bytes 86048 | tf_op jit(solution)/shard_map/ppermute | solution.py:457
  41.7 0.4 shard_map.82
  42.1 0.7 collective-permute-start.12
  42.7 1.3 %collective-permute-start.13 = (f32[18,8,128]{2,1,0:T(8,128)S(1)}, f32[18,8,128]{2,1,0:T(8,128)S(1)}, u32[]{:S(2)}, u32[]{:S(2)}) collective-permute-start(f32[18,8,128]{2,1,0:T(8,128)S(1)} %get-tuple-element.122), channel_id=1, source_target_pairs={{0,48},{1,32},{2,33},{3,34},{7,35},{6,39},{5,38},{4,37},{8,36},{9,... | collective-permute-start | bytes 221192 | tf_op jit(solution)/shard_map/ppermute | solution.py:457
  44.1 2.2 %collective-permute-done.12.from_below.rims_below = f32[18,8,128]{2,1,0:T(8,128)S(1)} collective-permute-done((f32[18,8,128]{2,1,0:T(8,128)S(1)}, f32[18,8,128]{2,1,0:T(8,128)S(1)}, u32[]{:S(2)}, u32[]{:S(2)}) %collective-permute-start.12) | collective-permute-done | bytes 73760 | tf_op jit(solution)/shard_map/ppermute | solution.py:457
  46.4 0.5 collective-permute-done.13.from_above.rims_above
  47.2 1.5 %collective-permute-start.14 = (f32[21,8,128]{2,1,0:T(8,128)S(1)}, f32[21,8,128]{2,1,0:T(8,128)S(1)}, u32[]{:S(2)}, u32[]{:S(2)}) collective-permute-start(f32[21,8,128]{2,1,0:T(8,128)S(1)} %get-tuple-element.128), channel_id=1, source_target_pairs={{0,33},{1,34},{2,35},{3,39},{7,38},{6,37},{5,36},{4,40},{8,41},{9,... | collective-permute-start | bytes 258056 | tf_op jit(solution)/shard_map/ppermute | solution.py:457
  49.2 2.5 %collective-permute-done.14.from_below = f32[21,8,128]{2,1,0:T(8,128)S(1)} collective-permute-done((f32[21,8,128]{2,1,0:T(8,128)S(1)}, f32[21,8,128]{2,1,0:T(8,128)S(1)}, u32[]{:S(2)}, u32[]{:S(2)}) %collective-permute-start.14) | collective-permute-done | bytes 86048 | tf_op jit(solution)/shard_map/ppermute | solution.py:457
  51.8 0.6 collective-permute-done.15.from_above
  52.8 0.8 collective-permute-start.16
  53.6 1.1 %collective-permute-start.17 = (f32[18,8,128]{2,1,0:T(8,128)S(1)}, f32[18,8,128]{2,1,0:T(8,128)S(1)}, u32[]{:S(2)}, u32[]{:S(2)}) collective-permute-start(f32[18,8,128]{2,1,0:T(8,128)S(1)} %get-tuple-element.141), channel_id=1, source_target_pairs={{0,48},{1,32},{2,33},{3,34},{7,35},{6,39},{5,38},{4,37},{8,36},{9,... | collective-permute-start | bytes 221192 | tf_op jit(solution)/shard_map/ppermute | solution.py:457
  54.7 2.4 %collective-permute-done.16.from_below.rims_below = f32[18,8,128]{2,1,0:T(8,128)S(1)} collective-permute-done((f32[18,8,128]{2,1,0:T(8,128)S(1)}, f32[18,8,128]{2,1,0:T(8,128)S(1)}, u32[]{:S(2)}, u32[]{:S(2)}) %collective-permute-start.16) | collective-permute-done | bytes 73760 | tf_op jit(solution)/shard_map/ppermute | solution.py:457
  57.1 0.7 collective-permute-done.17.from_above.rims_above
  58.2 0.8 collective-permute-start.18
  59.0 1.0 %collective-permute-start.19 = (f32[12,8,128]{2,1,0:T(8,128)S(1)}, f32[12,8,128]{2,1,0:T(8,128)S(1)}, u32[]{:S(2)}, u32[]{:S(2)}) collective-permute-start(f32[12,8,128]{2,1,0:T(8,128)S(1)} %get-tuple-element.152), channel_id=1, source_target_pairs={{0,48},{1,32},{2,33},{3,34},{7,35},{6,39},{5,38},{4,37},{8,36},{9,... | collective-permute-start | bytes 147464 | tf_op jit(solution)/shard_map/ppermute | solution.py:457
  60.2 2.6 %collective-permute-done.18.from_below = f32[21,8,128]{2,1,0:T(8,128)S(1)} collective-permute-done((f32[21,8,128]{2,1,0:T(8,128)S(1)}, f32[21,8,128]{2,1,0:T(8,128)S(1)}, u32[]{:S(2)}, u32[]{:S(2)}) %collective-permute-start.18) | collective-permute-done | bytes 86048 | tf_op jit(solution)/shard_map/ppermute | solution.py:457
  62.9 0.4 shard_map.94
  63.3 0.7 collective-permute-start.20
  64.0 1.1 %collective-permute-start.21 = (f32[18,8,128]{2,1,0:T(8,128)S(1)}, f32[18,8,128]{2,1,0:T(8,128)S(1)}, u32[]{:S(2)}, u32[]{:S(2)}) collective-permute-start(f32[18,8,128]{2,1,0:T(8,128)S(1)} %get-tuple-element.160), channel_id=1, source_target_pairs={{0,48},{1,32},{2,33},{3,34},{7,35},{6,39},{5,38},{4,37},{8,36},{9,... | collective-permute-start | bytes 221192 | tf_op jit(solution)/shard_map/ppermute | solution.py:457
  65.2 2.4 %collective-permute-done.20.from_below.rims_below = f32[18,8,128]{2,1,0:T(8,128)S(1)} collective-permute-done((f32[18,8,128]{2,1,0:T(8,128)S(1)}, f32[18,8,128]{2,1,0:T(8,128)S(1)}, u32[]{:S(2)}, u32[]{:S(2)}) %collective-permute-start.20) | collective-permute-done | bytes 73760 | tf_op jit(solution)/shard_map/ppermute | solution.py:457
  67.6 0.5 collective-permute-done.21.from_above.rims_above
  68.5 0.8 collective-permute-start.22
  69.3 1.0 %collective-permute-start.23 = (f32[12,8,128]{2,1,0:T(8,128)S(1)}, f32[12,8,128]{2,1,0:T(8,128)S(1)}, u32[]{:S(2)}, u32[]{:S(2)}) collective-permute-start(f32[12,8,128]{2,1,0:T(8,128)S(1)} %get-tuple-element.165), channel_id=1, source_target_pairs={{0,48},{1,32},{2,33},{3,34},{7,35},{6,39},{5,38},{4,37},{8,36},{9,... | collective-permute-start | bytes 147464 | tf_op jit(solution)/shard_map/ppermute | solution.py:457
  71.0 1.3 %collective-permute-done.22.from_below = f32[12,8,128]{2,1,0:T(8,128)S(1)} collective-permute-done((f32[12,8,128]{2,1,0:T(8,128)S(1)}, f32[12,8,128]{2,1,0:T(8,128)S(1)}, u32[]{:S(2)}, u32[]{:S(2)}) %collective-permute-start.22) | collective-permute-done | bytes 49184 | tf_op jit(solution)/shard_map/ppermute | solution.py:457
  72.2 0.8 collective-permute-done.23.from_above
  73.5 1.2 %collective-permute-done.24.other = f32[24,8,128]{2,1,0:T(8,128)S(1)} collective-permute-done((f32[24,8,128]{2,1,0:T(8,128)S(1)}, f32[24,8,128]{2,1,0:T(8,128)S(1)}, u32[]{:S(2)}, u32[]{:S(2)}) %collective-permute-start.24) | collective-permute-done | bytes 98336 | tf_op jit(solution)/shard_map/ppermute | solution.py:557
  74.7 6.8 %collective-permute-start.25 = (f32[24,8,128]{2,1,0:T(8,128)S(1)}, f32[24,8,128]{2,1,0:T(8,128)S(1)}, u32[]{:S(2)}, u32[]{:S(2)}) collective-permute-start(f32[24,8,128]{2,1,0:T(8,128)S(1)} %shard_map.102), channel_id=1, source_target_pairs={{0,0},{1,1},{2,2},{3,3},{7,4},{6,5},{5,6},{4,7},{8,8},{9,9},{10,10... | collective-permute-start | bytes 294920 | tf_op jit(solution)/shard_map/ppermute | solution.py:561
  81.5 2.5 %collective-permute-start.26 = (f32[24,8,128]{2,1,0:T(8,128)S(1)}, f32[24,8,128]{2,1,0:T(8,128)S(1)}, u32[]{:S(2)}, u32[]{:S(2)}) collective-permute-start(f32[24,8,128]{2,1,0:T(8,128)S(1)} %shard_map.101.rest_0_), channel_id=1, source_target_pairs={{0,64},{1,65},{2,66},{3,67},{7,68},{6,69},{5,70},{4,71},{8,72},{9,... | collective-permute-start | bytes 294920 | tf_op jit(solution)/shard_map/ppermute | solution.py:559
  84.0 5.8 %collective-permute-done.26.got1 = f32[24,8,128]{2,1,0:T(8,128)S(1)} collective-permute-done((f32[24,8,128]{2,1,0:T(8,128)S(1)}, f32[24,8,128]{2,1,0:T(8,128)S(1)}, u32[]{:S(2)}, u32[]{:S(2)}) %collective-permute-start.26) | collective-permute-done | bytes 98336 | tf_op jit(solution)/shard_map/ppermute | solution.py:559
  89.8 0.7 copy.13
  (57 shorter events, 5.9 us)
Async XLA Ops:
  1.4 5.1 %copy-start = (f32[2,3,2,4,2,512]{5,4,3,2,1,0:T(2,128)S(1)}, f32[2,3,2,4,2,512]{5,4,3,2,1,0:T(2,128)}, u32[]{:S(2)}) copy-start(f32[2,3,2,4,2,512]{5,4,3,2,1,0:T(2,128)} %param.7) | copy-start | bytes 589828
  1.4 14.7 %collective-permute-start = (f32[66,8,128]{2,1,0:T(8,128)S(1)}, f32[66,8,128]{2,1,0:T(8,128)S(1)}, u32[]{:S(2)}, u32[]{:S(2)}) collective-permute-start(f32[66,8,128]{2,1,0:T(8,128)S(1)} %shard_map.65), channel_id=1, source_target_pairs={{0,0},{1,1},{2,2},{3,3},{4,7},{5,6},{6,5},{7,4},{8,8},{9,9},{10,10... | collective-permute-start | bytes 811016 | tf_op jit(solution)/shard_map/ppermute | solution.py:487
  6.5 13.6 %collective-permute-start.4 = (f32[57,8,128]{2,1,0:T(8,128)S(1)}, f32[57,8,128]{2,1,0:T(8,128)S(1)}, u32[]{:S(2)}, u32[]{:S(2)}) collective-permute-start(f32[57,8,128]{2,1,0:T(8,128)S(1)} %shard_map.69), channel_id=1, source_target_pairs={{0,0},{1,1},{2,2},{3,3},{4,7},{5,6},{6,5},{7,4},{8,8},{9,9},{10,10... | collective-permute-start | bytes 700424 | tf_op jit(solution)/shard_map/ppermute | solution.py:489
  16.1 7.6 %collective-permute-start.1 = (f32[54,8,128]{2,1,0:T(8,128)S(1)}, f32[54,8,128]{2,1,0:T(8,128)S(1)}, u32[]{:S(2)}, u32[]{:S(2)}) collective-permute-start(f32[54,8,128]{2,1,0:T(8,128)S(1)} %slice.8), channel_id=1, source_target_pairs={{0,64},{1,65},{2,66},{3,67},{7,71},{6,70},{5,69},{4,68},{8,72},{9,... | collective-permute-start | bytes 663560 | tf_op jit(solution)/shard_map/ppermute | solution.py:490
  20.1 7.4 %collective-permute-start.5 = (f32[45,8,128]{2,1,0:T(8,128)S(1)}, f32[45,8,128]{2,1,0:T(8,128)S(1)}, u32[]{:S(2)}, u32[]{:S(2)}) collective-permute-start(f32[45,8,128]{2,1,0:T(8,128)S(1)} %slice.9), channel_id=1, source_target_pairs={{0,64},{1,65},{2,66},{3,67},{7,71},{6,70},{5,69},{4,68},{8,72},{9,... | collective-permute-start | bytes 552968 | tf_op jit(solution)/shard_map/ppermute | solution.py:491
  23.8 4.1 %collective-permute-start.2 = (f32[108,8,128]{2,1,0:T(8,128)S(1)}, f32[108,8,128]{2,1,0:T(8,128)S(1)}, u32[]{:S(2)}, u32[]{:S(2)}) collective-permute-start(f32[108,8,128]{2,1,0:T(8,128)S(1)} %shard_map.66), channel_id=1, source_target_pairs={{0,32},{1,33},{2,34},{3,35},{7,39},{6,38},{5,37},{4,36},{8,40},{9,... | collective-permute-start | bytes 1327112 | tf_op jit(solution)/shard_map/ppermute | solution.py:495
  27.6 2.3 %collective-permute-start.6 = (f32[90,8,128]{2,1,0:T(8,128)S(1)}, f32[90,8,128]{2,1,0:T(8,128)S(1)}, u32[]{:S(2)}, u32[]{:S(2)}) collective-permute-start(f32[90,8,128]{2,1,0:T(8,128)S(1)} %shard_map.70), channel_id=1, source_target_pairs={{0,32},{1,33},{2,34},{3,35},{7,39},{6,38},{5,37},{4,36},{8,40},{9,... | collective-permute-start | bytes 1105928 | tf_op jit(solution)/shard_map/ppermute | solution.py:499
  28.1 4.3 %collective-permute-start.3 = (f32[21,8,128]{2,1,0:T(8,128)S(1)}, f32[21,8,128]{2,1,0:T(8,128)S(1)}, u32[]{:S(2)}, u32[]{:S(2)}) collective-permute-start(f32[21,8,128]{2,1,0:T(8,128)S(1)} %get-tuple-element.91), channel_id=1, source_target_pairs={{0,33},{1,34},{2,35},{3,39},{7,38},{6,37},{5,36},{4,40},{8,41},{9,... | collective-permute-start | bytes 258056 | tf_op jit(solution)/shard_map/ppermute | solution.py:457
  28.2 4.3 %collective-permute-start.7 = (f32[12,8,128]{2,1,0:T(8,128)S(1)}, f32[12,8,128]{2,1,0:T(8,128)S(1)}, u32[]{:S(2)}, u32[]{:S(2)}) collective-permute-start(f32[12,8,128]{2,1,0:T(8,128)S(1)} %get-tuple-element.96._), channel_id=1, source_target_pairs={{0,48},{1,32},{2,33},{3,34},{7,35},{6,39},{5,38},{4,37},{8,36},{9,... | collective-permute-start | bytes 147464 | tf_op jit(solution)/shard_map/ppermute | solution.py:457
  32.9 3.6 %collective-permute-start.8 = (f32[12,8,128]{2,1,0:T(8,128)S(1)}, f32[12,8,128]{2,1,0:T(8,128)S(1)}, u32[]{:S(2)}, u32[]{:S(2)}) collective-permute-start(f32[12,8,128]{2,1,0:T(8,128)S(1)} %get-tuple-element.102), channel_id=1, source_target_pairs={{0,33},{1,34},{2,35},{3,39},{7,38},{6,37},{5,36},{4,40},{8,41},{9,... | collective-permute-start | bytes 147464 | tf_op jit(solution)/shard_map/ppermute | solution.py:457
  33.4 1.6 %copy-start.1 = (s32[4]{0:T(128)S(1)}, s32[4]{0:T(128)}, u32[]{:S(2)}) copy-start(s32[4]{0:T(128)} %source_slice.1) | copy-start | bytes 52
  33.4 3.5 %collective-permute-start.9 = (f32[12,8,128]{2,1,0:T(8,128)S(1)}, f32[12,8,128]{2,1,0:T(8,128)S(1)}, u32[]{:S(2)}, u32[]{:S(2)}) collective-permute-start(f32[12,8,128]{2,1,0:T(8,128)S(1)} %get-tuple-element.103), channel_id=1, source_target_pairs={{0,48},{1,32},{2,33},{3,34},{7,35},{6,39},{5,38},{4,37},{8,36},{9,... | collective-permute-start | bytes 147464 | tf_op jit(solution)/shard_map/ppermute | solution.py:457
  37.2 4.3 %collective-permute-start.10 = (f32[21,8,128]{2,1,0:T(8,128)S(1)}, f32[21,8,128]{2,1,0:T(8,128)S(1)}, u32[]{:S(2)}, u32[]{:S(2)}) collective-permute-start(f32[21,8,128]{2,1,0:T(8,128)S(1)} %get-tuple-element.109), channel_id=1, source_target_pairs={{0,33},{1,34},{2,35},{3,39},{7,38},{6,37},{5,36},{4,40},{8,41},{9,... | collective-permute-start | bytes 258056 | tf_op jit(solution)/shard_map/ppermute | solution.py:457
  37.6 4.0 %collective-permute-start.11 = (f32[12,8,128]{2,1,0:T(8,128)S(1)}, f32[12,8,128]{2,1,0:T(8,128)S(1)}, u32[]{:S(2)}, u32[]{:S(2)}) collective-permute-start(f32[12,8,128]{2,1,0:T(8,128)S(1)} %get-tuple-element.114), channel_id=1, source_target_pairs={{0,48},{1,32},{2,33},{3,34},{7,35},{6,39},{5,38},{4,37},{8,36},{9,... | collective-permute-start | bytes 147464 | tf_op jit(solution)/shard_map/ppermute | solution.py:457
  42.1 4.3 %collective-permute-start.12 = (f32[18,8,128]{2,1,0:T(8,128)S(1)}, f32[18,8,128]{2,1,0:T(8,128)S(1)}, u32[]{:S(2)}, u32[]{:S(2)}) collective-permute-start(f32[18,8,128]{2,1,0:T(8,128)S(1)} %get-tuple-element.121), channel_id=1, source_target_pairs={{0,33},{1,34},{2,35},{3,39},{7,38},{6,37},{5,36},{4,40},{8,41},{9,... | collective-permute-start | bytes 221192 | tf_op jit(solution)/shard_map/ppermute | solution.py:457
  42.7 4.1 %collective-permute-start.13 = (f32[18,8,128]{2,1,0:T(8,128)S(1)}, f32[18,8,128]{2,1,0:T(8,128)S(1)}, u32[]{:S(2)}, u32[]{:S(2)}) collective-permute-start(f32[18,8,128]{2,1,0:T(8,128)S(1)} %get-tuple-element.122), channel_id=1, source_target_pairs={{0,48},{1,32},{2,33},{3,34},{7,35},{6,39},{5,38},{4,37},{8,36},{9,... | collective-permute-start | bytes 221192 | tf_op jit(solution)/shard_map/ppermute | solution.py:457
  47.2 4.5 %collective-permute-start.14 = (f32[21,8,128]{2,1,0:T(8,128)S(1)}, f32[21,8,128]{2,1,0:T(8,128)S(1)}, u32[]{:S(2)}, u32[]{:S(2)}) collective-permute-start(f32[21,8,128]{2,1,0:T(8,128)S(1)} %get-tuple-element.128), channel_id=1, source_target_pairs={{0,33},{1,34},{2,35},{3,39},{7,38},{6,37},{5,36},{4,40},{8,41},{9,... | collective-permute-start | bytes 258056 | tf_op jit(solution)/shard_map/ppermute | solution.py:457
  48.7 3.7 %collective-permute-start.15 = (f32[12,8,128]{2,1,0:T(8,128)S(1)}, f32[12,8,128]{2,1,0:T(8,128)S(1)}, u32[]{:S(2)}, u32[]{:S(2)}) collective-permute-start(f32[12,8,128]{2,1,0:T(8,128)S(1)} %get-tuple-element.133), channel_id=1, source_target_pairs={{0,48},{1,32},{2,33},{3,34},{7,35},{6,39},{5,38},{4,37},{8,36},{9,... | collective-permute-start | bytes 147464 | tf_op jit(solution)/shard_map/ppermute | solution.py:457
  52.8 4.3 %collective-permute-start.16 = (f32[18,8,128]{2,1,0:T(8,128)S(1)}, f32[18,8,128]{2,1,0:T(8,128)S(1)}, u32[]{:S(2)}, u32[]{:S(2)}) collective-permute-start(f32[18,8,128]{2,1,0:T(8,128)S(1)} %get-tuple-element.140), channel_id=1, source_target_pairs={{0,33},{1,34},{2,35},{3,39},{7,38},{6,37},{5,36},{4,40},{8,41},{9,... | collective-permute-start | bytes 221192 | tf_op jit(solution)/shard_map/ppermute | solution.py:457
  53.6 4.3 %collective-permute-start.17 = (f32[18,8,128]{2,1,0:T(8,128)S(1)}, f32[18,8,128]{2,1,0:T(8,128)S(1)}, u32[]{:S(2)}, u32[]{:S(2)}) collective-permute-start(f32[18,8,128]{2,1,0:T(8,128)S(1)} %get-tuple-element.141), channel_id=1, source_target_pairs={{0,48},{1,32},{2,33},{3,34},{7,35},{6,39},{5,38},{4,37},{8,36},{9,... | collective-permute-start | bytes 221192 | tf_op jit(solution)/shard_map/ppermute | solution.py:457
  58.2 4.6 %collective-permute-start.18 = (f32[21,8,128]{2,1,0:T(8,128)S(1)}, f32[21,8,128]{2,1,0:T(8,128)S(1)}, u32[]{:S(2)}, u32[]{:S(2)}) collective-permute-start(f32[21,8,128]{2,1,0:T(8,128)S(1)} %get-tuple-element.147), channel_id=1, source_target_pairs={{0,33},{1,34},{2,35},{3,39},{7,38},{6,37},{5,36},{4,40},{8,41},{9,... | collective-permute-start | bytes 258056 | tf_op jit(solution)/shard_map/ppermute | solution.py:457
  59.0 3.9 %collective-permute-start.19 = (f32[12,8,128]{2,1,0:T(8,128)S(1)}, f32[12,8,128]{2,1,0:T(8,128)S(1)}, u32[]{:S(2)}, u32[]{:S(2)}) collective-permute-start(f32[12,8,128]{2,1,0:T(8,128)S(1)} %get-tuple-element.152), channel_id=1, source_target_pairs={{0,48},{1,32},{2,33},{3,34},{7,35},{6,39},{5,38},{4,37},{8,36},{9,... | collective-permute-start | bytes 147464 | tf_op jit(solution)/shard_map/ppermute | solution.py:457
  63.3 4.3 %collective-permute-start.20 = (f32[18,8,128]{2,1,0:T(8,128)S(1)}, f32[18,8,128]{2,1,0:T(8,128)S(1)}, u32[]{:S(2)}, u32[]{:S(2)}) collective-permute-start(f32[18,8,128]{2,1,0:T(8,128)S(1)} %get-tuple-element.159), channel_id=1, source_target_pairs={{0,33},{1,34},{2,35},{3,39},{7,38},{6,37},{5,36},{4,40},{8,41},{9,... | collective-permute-start | bytes 221192 | tf_op jit(solution)/shard_map/ppermute | solution.py:457
  64.0 4.1 %collective-permute-start.21 = (f32[18,8,128]{2,1,0:T(8,128)S(1)}, f32[18,8,128]{2,1,0:T(8,128)S(1)}, u32[]{:S(2)}, u32[]{:S(2)}) collective-permute-start(f32[18,8,128]{2,1,0:T(8,128)S(1)} %get-tuple-element.160), channel_id=1, source_target_pairs={{0,48},{1,32},{2,33},{3,34},{7,35},{6,39},{5,38},{4,37},{8,36},{9,... | collective-permute-start | bytes 221192 | tf_op jit(solution)/shard_map/ppermute | solution.py:457
  68.5 3.8 %collective-permute-start.22 = (f32[12,8,128]{2,1,0:T(8,128)S(1)}, f32[12,8,128]{2,1,0:T(8,128)S(1)}, u32[]{:S(2)}, u32[]{:S(2)}) collective-permute-start(f32[12,8,128]{2,1,0:T(8,128)S(1)} %get-tuple-element.164), channel_id=1, source_target_pairs={{0,33},{1,34},{2,35},{3,39},{7,38},{6,37},{5,36},{4,40},{8,41},{9,... | collective-permute-start | bytes 147464 | tf_op jit(solution)/shard_map/ppermute | solution.py:457
  69.3 3.7 %collective-permute-start.23 = (f32[12,8,128]{2,1,0:T(8,128)S(1)}, f32[12,8,128]{2,1,0:T(8,128)S(1)}, u32[]{:S(2)}, u32[]{:S(2)}) collective-permute-start(f32[12,8,128]{2,1,0:T(8,128)S(1)} %get-tuple-element.165), channel_id=1, source_target_pairs={{0,48},{1,32},{2,33},{3,34},{7,35},{6,39},{5,38},{4,37},{8,36},{9,... | collective-permute-start | bytes 147464 | tf_op jit(solution)/shard_map/ppermute | solution.py:457
  73.3 1.4 %collective-permute-start.24 = (f32[24,8,128]{2,1,0:T(8,128)S(1)}, f32[24,8,128]{2,1,0:T(8,128)S(1)}, u32[]{:S(2)}, u32[]{:S(2)}) collective-permute-start(f32[24,8,128]{2,1,0:T(8,128)S(1)} %get-tuple-element.170), channel_id=1, source_target_pairs={{0,32},{1,33},{2,34},{3,35},{7,39},{6,38},{5,37},{4,36},{8,40},{9,... | collective-permute-start | bytes 294920 | tf_op jit(solution)/shard_map/ppermute | solution.py:557
  74.7 9.3 %collective-permute-start.25 = (f32[24,8,128]{2,1,0:T(8,128)S(1)}, f32[24,8,128]{2,1,0:T(8,128)S(1)}, u32[]{:S(2)}, u32[]{:S(2)}) collective-permute-start(f32[24,8,128]{2,1,0:T(8,128)S(1)} %shard_map.102), channel_id=1, source_target_pairs={{0,0},{1,1},{2,2},{3,3},{7,4},{6,5},{5,6},{4,7},{8,8},{9,9},{10,10... | collective-permute-start | bytes 294920 | tf_op jit(solution)/shard_map/ppermute | solution.py:561
  81.5 8.3 %collective-permute-start.26 = (f32[24,8,128]{2,1,0:T(8,128)S(1)}, f32[24,8,128]{2,1,0:T(8,128)S(1)}, u32[]{:S(2)}, u32[]{:S(2)}) collective-permute-start(f32[24,8,128]{2,1,0:T(8,128)S(1)} %shard_map.101.rest_0_), channel_id=1, source_target_pairs={{0,64},{1,65},{2,66},{3,67},{7,68},{6,69},{5,70},{4,71},{8,72},{9,... | collective-permute-start | bytes 294920 | tf_op jit(solution)/shard_map/ppermute | solution.py:559

commit v4 on v3

--- a/solution.py
+++ b/solution.py
@@ -436,6 +436,8 @@
         own, beside = jnp.where(half, mine[12 + at], mine[at]), jnp.where(half, other[12 + at], other[at])
         out[at] = jnp.where(twist, beside, own)
         out[12 + at] = jnp.where(twist, own, beside)
+    if way == 1:
+        out[24] = marks[HALF]
 
 
 def deliver(got0, got1, marks, out):
@@ -555,7 +557,7 @@
         last_smear_end, [field, partial, from_below, from_above, *around, *done, marks], [(24, 8, 128)] * 2
     )
     other = lax.ppermute(theirs, AXES, SIBLING)
-    (out1,) = kernel_call(functools.partial(both_columns, 1), [mine, other, marks], [(24, 8, 128)])
+    (out1,) = kernel_call(functools.partial(both_columns, 1), [mine, other, marks], [(25, 8, 128)])
     got1 = lax.ppermute(out1, AXES, COLLECT[1])
     (out0,) = kernel_call(functools.partial(both_columns, 0), [mine, other, marks, out1], [(24, 8, 128)])
     got0 = lax.ppermute(out0, AXES, COLLECT[0])

time: 90.7 us -> 90.6 us (level)
    ppermute x1, waiting for transfers between devices: 5.8 us -> 0.01 us  [local(): got1 = lax.ppermute(out1, AXES, COLLECT[1])]
    ppermute x1, waiting for transfers between devices: 0.01 us -> 5.79 us  [local(): got0 = lax.ppermute(out0, AXES, COLLECT[0])]
    ppermute x1, starting transfers between devices: 6.77 us -> 1.92 us  [local(): got0 = lax.ppermute(out0, AXES, COLLECT[0])]
    ppermute x1, starting transfers between devices: 2.49 us -> 7.34 us  [local(): got1 = lax.ppermute(out1, AXES, COLLECT[1])]
where the time goes in v4:
time: 90.6 us; the launch traced here: 90.5 us
  starting transfers between devices  41.7 us (46%)
  waiting for transfers between devices  40 us (44%)
  Pallas kernels  7.38 us (8%)
    ppermute x9, waiting for transfers between devices, exchange(): lax.ppermute(to_above, AXES, UP)  19.1 us
    ppermute x9, starting transfers between devices, exchange(): lax.ppermute(to_below, AXES, DOWN)  10.4 us
    pallas_call x40, Pallas kernels, kernel_call(): pl.pallas_call(body, in_specs=[pl.BlockSpec(memory_space=space) for space...  7.38 us
    ppermute x1, starting transfers between devices, local(): got1 = lax.ppermute(out1, AXES, COLLECT[1])  7.34 us
    ppermute x9, starting transfers between devices, exchange(): lax.ppermute(to_above, AXES, UP)  6.14 us
    ppermute x1, waiting for transfers between devices, local(): got0 = lax.ppermute(out0, AXES, COLLECT[0])  5.79 us
    ppermute x1, waiting for transfers between devices, local(): links_own = lax.ppermute(message, AXES, SPREAD)  5.26 us
    ppermute x1, starting transfers between devices, local(): links_own = lax.ppermute(message, AXES, SPREAD)  5.05 us
  transfers between devices with their start and end apart: 27, of which 21 were waited for; matrix products, arithmetic and copies ran while one was open for 0% of the time, Pallas kernels for 3%

profile of v4, /device:TPU:32, one launch (start us, length us, event | category | flops | bytes accessed | tf_op | source)
XLA Modules:
  0.0 90.5 jit_solution(5930951752097008533)
XLA Ops:
  0.1 1.2 %shard_map.64 = (f32[99,8,128]{2,1,0:T(8,128)S(1)}, f32[6,2,4,8,128]{4,3,2,1,0:T(8,128)S(1)}) custom-call(f32[54,8,128]{2,1,0:T(8,128)} %bitcast.36, f32[18,8,128]{2,1,0:T(8,128)} %bitcast.39, f32[54,8,128]{2,1,0:T(8,128)} %bitcast.37, f32[6,2,4,8,128]{4,3,2,1,0:T(8,128)} %bitcast.38), custom_call_target="tpu_custom_call" | custom-call | tf_op jit(solution)/shard_map/pallas_call | solution.py:209
  1.4 5.1 %collective-permute-start = (f32[66,8,128]{2,1,0:T(8,128)S(1)}, f32[66,8,128]{2,1,0:T(8,128)S(1)}, u32[]{:S(2)}, u32[]{:S(2)}) collective-permute-start(f32[66,8,128]{2,1,0:T(8,128)S(1)} %shard_map.65), channel_id=1, source_target_pairs={{0,0},{1,1},{2,2},{3,3},{4,7},{5,6},{6,5},{7,4},{8,8},{9,9},{10,10... | collective-permute-start | bytes 811016 | tf_op jit(solution)/shard_map/ppermute | solution.py:489
  6.5 4.3 %collective-permute-start.4 = (f32[57,8,128]{2,1,0:T(8,128)S(1)}, f32[57,8,128]{2,1,0:T(8,128)S(1)}, u32[]{:S(2)}, u32[]{:S(2)}) collective-permute-start(f32[57,8,128]{2,1,0:T(8,128)S(1)} %shard_map.69), channel_id=1, source_target_pairs={{0,0},{1,1},{2,2},{3,3},{4,7},{5,6},{6,5},{7,4},{8,8},{9,9},{10,10... | collective-permute-start | bytes 700424 | tf_op jit(solution)/shard_map/ppermute | solution.py:491
  10.8 5.3 %collective-permute-done.own = f32[66,8,128]{2,1,0:T(8,128)S(1)} collective-permute-done((f32[66,8,128]{2,1,0:T(8,128)S(1)}, f32[66,8,128]{2,1,0:T(8,128)S(1)}, u32[]{:S(2)}, u32[]{:S(2)}) %collective-permute-start) | collective-permute-done | bytes 270368 | tf_op jit(solution)/shard_map/ppermute | solution.py:489
  16.1 3.1 %collective-permute-start.1 = (f32[54,8,128]{2,1,0:T(8,128)S(1)}, f32[54,8,128]{2,1,0:T(8,128)S(1)}, u32[]{:S(2)}, u32[]{:S(2)}) collective-permute-start(f32[54,8,128]{2,1,0:T(8,128)S(1)} %slice.8), channel_id=1, source_target_pairs={{0,64},{1,65},{2,66},{3,67},{7,71},{6,70},{5,69},{4,68},{8,72},{9,... | collective-permute-start | bytes 663560 | tf_op jit(solution)/shard_map/ppermute | solution.py:492
  19.2 1.0 %collective-permute-done.4.own.others = f32[57,8,128]{2,1,0:T(8,128)S(1)} collective-permute-done((f32[57,8,128]{2,1,0:T(8,128)S(1)}, f32[57,8,128]{2,1,0:T(8,128)S(1)}, u32[]{:S(2)}, u32[]{:S(2)}) %collective-permute-start.4) | collective-permute-done | bytes 233504 | tf_op jit(solution)/shard_map/ppermute | solution.py:491
  20.1 3.1 %collective-permute-start.5 = (f32[45,8,128]{2,1,0:T(8,128)S(1)}, f32[45,8,128]{2,1,0:T(8,128)S(1)}, u32[]{:S(2)}, u32[]{:S(2)}) collective-permute-start(f32[45,8,128]{2,1,0:T(8,128)S(1)} %slice.9), channel_id=1, source_target_pairs={{0,64},{1,65},{2,66},{3,67},{7,71},{6,70},{5,69},{4,68},{8,72},{9,... | collective-permute-start | bytes 552968 | tf_op jit(solution)/shard_map/ppermute | solution.py:493
  23.2 0.5 collective-permute-done.1.facing
  23.9 3.7 %collective-permute-done.5.facing = f32[45,8,128]{2,1,0:T(8,128)S(1)} collective-permute-done((f32[45,8,128]{2,1,0:T(8,128)S(1)}, f32[45,8,128]{2,1,0:T(8,128)S(1)}, u32[]{:S(2)}, u32[]{:S(2)}) %collective-permute-start.5) | collective-permute-done | bytes 184352 | tf_op jit(solution)/shard_map/ppermute | solution.py:493
  28.2 1.7 %collective-permute-start.7 = (f32[12,8,128]{2,1,0:T(8,128)S(1)}, f32[12,8,128]{2,1,0:T(8,128)S(1)}, u32[]{:S(2)}, u32[]{:S(2)}) collective-permute-start(f32[12,8,128]{2,1,0:T(8,128)S(1)} %get-tuple-element.96._), channel_id=1, source_target_pairs={{0,48},{1,32},{2,33},{3,34},{7,35},{6,39},{5,38},{4,37},{8,36},{9,... | collective-permute-start | bytes 147464 | tf_op jit(solution)/shard_map/ppermute | solution.py:459
  30.0 2.4 %collective-permute-done.3.from_below = f32[21,8,128]{2,1,0:T(8,128)S(1)} collective-permute-done((f32[21,8,128]{2,1,0:T(8,128)S(1)}, f32[21,8,128]{2,1,0:T(8,128)S(1)}, u32[]{:S(2)}, u32[]{:S(2)}) %collective-permute-start.3) | collective-permute-done | bytes 86048 | tf_op jit(solution)/shard_map/ppermute | solution.py:459
  32.5 0.4 shard_map.73
  32.9 0.4 collective-permute-start.8
  33.4 1.4 %collective-permute-start.9 = (f32[12,8,128]{2,1,0:T(8,128)S(1)}, f32[12,8,128]{2,1,0:T(8,128)S(1)}, u32[]{:S(2)}, u32[]{:S(2)}) collective-permute-start(f32[12,8,128]{2,1,0:T(8,128)S(1)} %get-tuple-element.103), channel_id=1, source_target_pairs={{0,48},{1,32},{2,33},{3,34},{7,35},{6,39},{5,38},{4,37},{8,36},{9,... | collective-permute-start | bytes 147464 | tf_op jit(solution)/shard_map/ppermute | solution.py:459
  35.0 0.6 shard_map.75
  35.6 0.9 %collective-permute-done.8.from_below = f32[12,8,128]{2,1,0:T(8,128)S(1)} collective-permute-done((f32[12,8,128]{2,1,0:T(8,128)S(1)}, f32[12,8,128]{2,1,0:T(8,128)S(1)}, u32[]{:S(2)}, u32[]{:S(2)}) %collective-permute-start.8) | collective-permute-done | bytes 49184 | tf_op jit(solution)/shard_map/ppermute | solution.py:459
  37.2 0.4 collective-permute-start.10
  37.6 1.4 %collective-permute-start.11 = (f32[12,8,128]{2,1,0:T(8,128)S(1)}, f32[12,8,128]{2,1,0:T(8,128)S(1)}, u32[]{:S(2)}, u32[]{:S(2)}) collective-permute-start(f32[12,8,128]{2,1,0:T(8,128)S(1)} %get-tuple-element.114), channel_id=1, source_target_pairs={{0,48},{1,32},{2,33},{3,34},{7,35},{6,39},{5,38},{4,37},{8,36},{9,... | collective-permute-start | bytes 147464 | tf_op jit(solution)/shard_map/ppermute | solution.py:459
  39.4 2.2 %collective-permute-done.10.from_below = f32[21,8,128]{2,1,0:T(8,128)S(1)} collective-permute-done((f32[21,8,128]{2,1,0:T(8,128)S(1)}, f32[21,8,128]{2,1,0:T(8,128)S(1)}, u32[]{:S(2)}, u32[]{:S(2)}) %collective-permute-start.10) | collective-permute-done | bytes 86048 | tf_op jit(solution)/shard_map/ppermute | solution.py:459
  41.7 0.4 shard_map.82
  42.1 0.7 collective-permute-start.12
  42.7 1.3 %collective-permute-start.13 = (f32[18,8,128]{2,1,0:T(8,128)S(1)}, f32[18,8,128]{2,1,0:T(8,128)S(1)}, u32[]{:S(2)}, u32[]{:S(2)}) collective-permute-start(f32[18,8,128]{2,1,0:T(8,128)S(1)} %get-tuple-element.122), channel_id=1, source_target_pairs={{0,48},{1,32},{2,33},{3,34},{7,35},{6,39},{5,38},{4,37},{8,36},{9,... | collective-permute-start | bytes 221192 | tf_op jit(solution)/shard_map/ppermute | solution.py:459
  44.1 2.2 %collective-permute-done.12.from_below.rims_below = f32[18,8,128]{2,1,0:T(8,128)S(1)} collective-permute-done((f32[18,8,128]{2,1,0:T(8,128)S(1)}, f32[18,8,128]{2,1,0:T(8,128)S(1)}, u32[]{:S(2)}, u32[]{:S(2)}) %collective-permute-start.12) | collective-permute-done | bytes 73760 | tf_op jit(solution)/shard_map/ppermute | solution.py:459
  46.4 0.5 collective-permute-done.13.from_above.rims_above
  47.2 1.5 %collective-permute-start.14 = (f32[21,8,128]{2,1,0:T(8,128)S(1)}, f32[21,8,128]{2,1,0:T(8,128)S(1)}, u32[]{:S(2)}, u32[]{:S(2)}) collective-permute-start(f32[21,8,128]{2,1,0:T(8,128)S(1)} %get-tuple-element.128), channel_id=1, source_target_pairs={{0,33},{1,34},{2,35},{3,39},{7,38},{6,37},{5,36},{4,40},{8,41},{9,... | collective-permute-start | bytes 258056 | tf_op jit(solution)/shard_map/ppermute | solution.py:459
  49.2 2.5 %collective-permute-done.14.from_below = f32[21,8,128]{2,1,0:T(8,128)S(1)} collective-permute-done((f32[21,8,128]{2,1,0:T(8,128)S(1)}, f32[21,8,128]{2,1,0:T(8,128)S(1)}, u32[]{:S(2)}, u32[]{:S(2)}) %collective-permute-start.14) | collective-permute-done | bytes 86048 | tf_op jit(solution)/shard_map/ppermute | solution.py:459
  51.8 0.6 collective-permute-done.15.from_above
  52.8 0.8 collective-permute-start.16
  53.6 1.1 %collective-permute-start.17 = (f32[18,8,128]{2,1,0:T(8,128)S(1)}, f32[18,8,128]{2,1,0:T(8,128)S(1)}, u32[]{:S(2)}, u32[]{:S(2)}) collective-permute-start(f32[18,8,128]{2,1,0:T(8,128)S(1)} %get-tuple-element.141), channel_id=1, source_target_pairs={{0,48},{1,32},{2,33},{3,34},{7,35},{6,39},{5,38},{4,37},{8,36},{9,... | collective-permute-start | bytes 221192 | tf_op jit(solution)/shard_map/ppermute | solution.py:459
  54.7 2.4 %collective-permute-done.16.from_below.rims_below = f32[18,8,128]{2,1,0:T(8,128)S(1)} collective-permute-done((f32[18,8,128]{2,1,0:T(8,128)S(1)}, f32[18,8,128]{2,1,0:T(8,128)S(1)}, u32[]{:S(2)}, u32[]{:S(2)}) %collective-permute-start.16) | collective-permute-done | bytes 73760 | tf_op jit(solution)/shard_map/ppermute | solution.py:459
  57.1 0.7 collective-permute-done.17.from_above.rims_above
  58.2 0.8 collective-permute-start.18
  59.0 1.0 %collective-permute-start.19 = (f32[12,8,128]{2,1,0:T(8,128)S(1)}, f32[12,8,128]{2,1,0:T(8,128)S(1)}, u32[]{:S(2)}, u32[]{:S(2)}) collective-permute-start(f32[12,8,128]{2,1,0:T(8,128)S(1)} %get-tuple-element.152), channel_id=1, source_target_pairs={{0,48},{1,32},{2,33},{3,34},{7,35},{6,39},{5,38},{4,37},{8,36},{9,... | collective-permute-start | bytes 147464 | tf_op jit(solution)/shard_map/ppermute | solution.py:459
  60.2 2.6 %collective-permute-done.18.from_below = f32[21,8,128]{2,1,0:T(8,128)S(1)} collective-permute-done((f32[21,8,128]{2,1,0:T(8,128)S(1)}, f32[21,8,128]{2,1,0:T(8,128)S(1)}, u32[]{:S(2)}, u32[]{:S(2)}) %collective-permute-start.18) | collective-permute-done | bytes 86048 | tf_op jit(solution)/shard_map/ppermute | solution.py:459
  62.9 0.4 shard_map.94
  63.3 0.7 collective-permute-start.20
  64.0 1.1 %collective-permute-start.21 = (f32[18,8,128]{2,1,0:T(8,128)S(1)}, f32[18,8,128]{2,1,0:T(8,128)S(1)}, u32[]{:S(2)}, u32[]{:S(2)}) collective-permute-start(f32[18,8,128]{2,1,0:T(8,128)S(1)} %get-tuple-element.160), channel_id=1, source_target_pairs={{0,48},{1,32},{2,33},{3,34},{7,35},{6,39},{5,38},{4,37},{8,36},{9,... | collective-permute-start | bytes 221192 | tf_op jit(solution)/shard_map/ppermute | solution.py:459
  65.2 2.4 %collective-permute-done.20.from_below.rims_below = f32[18,8,128]{2,1,0:T(8,128)S(1)} collective-permute-done((f32[18,8,128]{2,1,0:T(8,128)S(1)}, f32[18,8,128]{2,1,0:T(8,128)S(1)}, u32[]{:S(2)}, u32[]{:S(2)}) %collective-permute-start.20) | collective-permute-done | bytes 73760 | tf_op jit(solution)/shard_map/ppermute | solution.py:459
  67.6 0.5 collective-permute-done.21.from_above.rims_above
  68.5 0.8 collective-permute-start.22
  69.3 1.0 %collective-permute-start.23 = (f32[12,8,128]{2,1,0:T(8,128)S(1)}, f32[12,8,128]{2,1,0:T(8,128)S(1)}, u32[]{:S(2)}, u32[]{:S(2)}) collective-permute-start(f32[12,8,128]{2,1,0:T(8,128)S(1)} %get-tuple-element.165), channel_id=1, source_target_pairs={{0,48},{1,32},{2,33},{3,34},{7,35},{6,39},{5,38},{4,37},{8,36},{9,... | collective-permute-start | bytes 147464 | tf_op jit(solution)/shard_map/ppermute | solution.py:459
  71.0 1.3 %collective-permute-done.22.from_below = f32[12,8,128]{2,1,0:T(8,128)S(1)} collective-permute-done((f32[12,8,128]{2,1,0:T(8,128)S(1)}, f32[12,8,128]{2,1,0:T(8,128)S(1)}, u32[]{:S(2)}, u32[]{:S(2)}) %collective-permute-start.22) | collective-permute-done | bytes 49184 | tf_op jit(solution)/shard_map/ppermute | solution.py:459
  72.2 0.8 collective-permute-done.23.from_above
  73.5 1.2 %collective-permute-done.24.other = f32[24,8,128]{2,1,0:T(8,128)S(1)} collective-permute-done((f32[24,8,128]{2,1,0:T(8,128)S(1)}, f32[24,8,128]{2,1,0:T(8,128)S(1)}, u32[]{:S(2)}, u32[]{:S(2)}) %collective-permute-start.24) | collective-permute-done | bytes 98336 | tf_op jit(solution)/shard_map/ppermute | solution.py:559
  74.7 7.3 %collective-permute-start.26 = (f32[25,8,128]{2,1,0:T(8,128)S(1)}, f32[25,8,128]{2,1,0:T(8,128)S(1)}, u32[]{:S(2)}, u32[]{:S(2)}) collective-permute-start(f32[25,8,128]{2,1,0:T(8,128)S(1)} %shard_map.101.rest_0_), channel_id=1, source_target_pairs={{0,64},{1,65},{2,66},{3,67},{7,68},{6,69},{5,70},{4,71},{8,72},{9,... | collective-permute-start | bytes 307208 | tf_op jit(solution)/shard_map/ppermute | solution.py:561
  82.0 1.9 %collective-permute-start.25 = (f32[24,8,128]{2,1,0:T(8,128)S(1)}, f32[24,8,128]{2,1,0:T(8,128)S(1)}, u32[]{:S(2)}, u32[]{:S(2)}) collective-permute-start(f32[24,8,128]{2,1,0:T(8,128)S(1)} %shard_map.102), channel_id=1, source_target_pairs={{0,0},{1,1},{2,2},{3,3},{7,4},{6,5},{5,6},{4,7},{8,8},{9,9},{10,10... | collective-permute-start | bytes 294920 | tf_op jit(solution)/shard_map/ppermute | solution.py:563
  84.0 5.8 %collective-permute-done.25.got0 = f32[24,8,128]{2,1,0:T(8,128)S(1)} collective-permute-done((f32[24,8,128]{2,1,0:T(8,128)S(1)}, f32[24,8,128]{2,1,0:T(8,128)S(1)}, u32[]{:S(2)}, u32[]{:S(2)}) %collective-permute-start.25) | collective-permute-done | bytes 98336 | tf_op jit(solution)/shard_map/ppermute | solution.py:563
  89.8 0.7 copy.13
  (57 shorter events, 5.9 us)
Async XLA Ops:
  1.4 5.1 %copy-start = (f32[2,3,2,4,2,512]{5,4,3,2,1,0:T(2,128)S(1)}, f32[2,3,2,4,2,512]{5,4,3,2,1,0:T(2,128)}, u32[]{:S(2)}) copy-start(f32[2,3,2,4,2,512]{5,4,3,2,1,0:T(2,128)} %param.7) | copy-start | bytes 589828
  1.4 14.7 %collective-permute-start = (f32[66,8,128]{2,1,0:T(8,128)S(1)}, f32[66,8,128]{2,1,0:T(8,128)S(1)}, u32[]{:S(2)}, u32[]{:S(2)}) collective-permute-start(f32[66,8,128]{2,1,0:T(8,128)S(1)} %shard_map.65), channel_id=1, source_target_pairs={{0,0},{1,1},{2,2},{3,3},{4,7},{5,6},{6,5},{7,4},{8,8},{9,9},{10,10... | collective-permute-start | bytes 811016 | tf_op jit(solution)/shard_map/ppermute | solution.py:489
  6.5 13.6 %collective-permute-start.4 = (f32[57,8,128]{2,1,0:T(8,128)S(1)}, f32[57,8,128]{2,1,0:T(8,128)S(1)}, u32[]{:S(2)}, u32[]{:S(2)}) collective-permute-start(f32[57,8,128]{2,1,0:T(8,128)S(1)} %shard_map.69), channel_id=1, source_target_pairs={{0,0},{1,1},{2,2},{3,3},{4,7},{5,6},{6,5},{7,4},{8,8},{9,9},{10,10... | collective-permute-start | bytes 700424 | tf_op jit(solution)/shard_map/ppermute | solution.py:491
  16.1 7.6 %collective-permute-start.1 = (f32[54,8,128]{2,1,0:T(8,128)S(1)}, f32[54,8,128]{2,1,0:T(8,128)S(1)}, u32[]{:S(2)}, u32[]{:S(2)}) collective-permute-start(f32[54,8,128]{2,1,0:T(8,128)S(1)} %slice.8), channel_id=1, source_target_pairs={{0,64},{1,65},{2,66},{3,67},{7,71},{6,70},{5,69},{4,68},{8,72},{9,... | collective-permute-start | bytes 663560 | tf_op jit(solution)/shard_map/ppermute | solution.py:492
  20.1 7.4 %collective-permute-start.5 = (f32[45,8,128]{2,1,0:T(8,128)S(1)}, f32[45,8,128]{2,1,0:T(8,128)S(1)}, u32[]{:S(2)}, u32[]{:S(2)}) collective-permute-start(f32[45,8,128]{2,1,0:T(8,128)S(1)} %slice.9), channel_id=1, source_target_pairs={{0,64},{1,65},{2,66},{3,67},{7,71},{6,70},{5,69},{4,68},{8,72},{9,... | collective-permute-start | bytes 552968 | tf_op jit(solution)/shard_map/ppermute | solution.py:493
  23.8 4.1 %collective-permute-start.2 = (f32[108,8,128]{2,1,0:T(8,128)S(1)}, f32[108,8,128]{2,1,0:T(8,128)S(1)}, u32[]{:S(2)}, u32[]{:S(2)}) collective-permute-start(f32[108,8,128]{2,1,0:T(8,128)S(1)} %shard_map.66), channel_id=1, source_target_pairs={{0,32},{1,33},{2,34},{3,35},{7,39},{6,38},{5,37},{4,36},{8,40},{9,... | collective-permute-start | bytes 1327112 | tf_op jit(solution)/shard_map/ppermute | solution.py:497
  27.6 2.3 %collective-permute-start.6 = (f32[90,8,128]{2,1,0:T(8,128)S(1)}, f32[90,8,128]{2,1,0:T(8,128)S(1)}, u32[]{:S(2)}, u32[]{:S(2)}) collective-permute-start(f32[90,8,128]{2,1,0:T(8,128)S(1)} %shard_map.70), channel_id=1, source_target_pairs={{0,32},{1,33},{2,34},{3,35},{7,39},{6,38},{5,37},{4,36},{8,40},{9,... | collective-permute-start | bytes 1105928 | tf_op jit(solution)/shard_map/ppermute | solution.py:501
  28.1 4.3 %collective-permute-start.3 = (f32[21,8,128]{2,1,0:T(8,128)S(1)}, f32[21,8,128]{2,1,0:T(8,128)S(1)}, u32[]{:S(2)}, u32[]{:S(2)}) collective-permute-start(f32[21,8,128]{2,1,0:T(8,128)S(1)} %get-tuple-element.91), channel_id=1, source_target_pairs={{0,33},{1,34},{2,35},{3,39},{7,38},{6,37},{5,36},{4,40},{8,41},{9,... | collective-permute-start | bytes 258056 | tf_op jit(solution)/shard_map/ppermute | solution.py:459
  28.2 4.3 %collective-permute-start.7 = (f32[12,8,128]{2,1,0:T(8,128)S(1)}, f32[12,8,128]{2,1,0:T(8,128)S(1)}, u32[]{:S(2)}, u32[]{:S(2)}) collective-permute-start(f32[12,8,128]{2,1,0:T(8,128)S(1)} %get-tuple-element.96._), channel_id=1, source_target_pairs={{0,48},{1,32},{2,33},{3,34},{7,35},{6,39},{5,38},{4,37},{8,36},{9,... | collective-permute-start | bytes 147464 | tf_op jit(solution)/shard_map/ppermute | solution.py:459
  32.9 3.6 %collective-permute-start.8 = (f32[12,8,128]{2,1,0:T(8,128)S(1)}, f32[12,8,128]{2,1,0:T(8,128)S(1)}, u32[]{:S(2)}, u32[]{:S(2)}) collective-permute-start(f32[12,8,128]{2,1,0:T(8,128)S(1)} %get-tuple-element.102), channel_id=1, source_target_pairs={{0,33},{1,34},{2,35},{3,39},{7,38},{6,37},{5,36},{4,40},{8,41},{9,... | collective-permute-start | bytes 147464 | tf_op jit(solution)/shard_map/ppermute | solution.py:459
  33.4 1.6 %copy-start.1 = (s32[4]{0:T(128)S(1)}, s32[4]{0:T(128)}, u32[]{:S(2)}) copy-start(s32[4]{0:T(128)} %source_slice.1) | copy-start | bytes 52
  33.4 3.5 %collective-permute-start.9 = (f32[12,8,128]{2,1,0:T(8,128)S(1)}, f32[12,8,128]{2,1,0:T(8,128)S(1)}, u32[]{:S(2)}, u32[]{:S(2)}) collective-permute-start(f32[12,8,128]{2,1,0:T(8,128)S(1)} %get-tuple-element.103), channel_id=1, source_target_pairs={{0,48},{1,32},{2,33},{3,34},{7,35},{6,39},{5,38},{4,37},{8,36},{9,... | collective-permute-start | bytes 147464 | tf_op jit(solution)/shard_map/ppermute | solution.py:459
  37.2 4.3 %collective-permute-start.10 = (f32[21,8,128]{2,1,0:T(8,128)S(1)}, f32[21,8,128]{2,1,0:T(8,128)S(1)}, u32[]{:S(2)}, u32[]{:S(2)}) collective-permute-start(f32[21,8,128]{2,1,0:T(8,128)S(1)} %get-tuple-element.109), channel_id=1, source_target_pairs={{0,33},{1,34},{2,35},{3,39},{7,38},{6,37},{5,36},{4,40},{8,41},{9,... | collective-permute-start | bytes 258056 | tf_op jit(solution)/shard_map/ppermute | solution.py:459
  37.6 4.0 %collective-permute-start.11 = (f32[12,8,128]{2,1,0:T(8,128)S(1)}, f32[12,8,128]{2,1,0:T(8,128)S(1)}, u32[]{:S(2)}, u32[]{:S(2)}) collective-permute-start(f32[12,8,128]{2,1,0:T(8,128)S(1)} %get-tuple-element.114), channel_id=1, source_target_pairs={{0,48},{1,32},{2,33},{3,34},{7,35},{6,39},{5,38},{4,37},{8,36},{9,... | collective-permute-start | bytes 147464 | tf_op jit(solution)/shard_map/ppermute | solution.py:459
  42.1 4.3 %collective-permute-start.12 = (f32[18,8,128]{2,1,0:T(8,128)S(1)}, f32[18,8,128]{2,1,0:T(8,128)S(1)}, u32[]{:S(2)}, u32[]{:S(2)}) collective-permute-start(f32[18,8,128]{2,1,0:T(8,128)S(1)} %get-tuple-element.121), channel_id=1, source_target_pairs={{0,33},{1,34},{2,35},{3,39},{7,38},{6,37},{5,36},{4,40},{8,41},{9,... | collective-permute-start | bytes 221192 | tf_op jit(solution)/shard_map/ppermute | solution.py:459
  42.7 4.1 %collective-permute-start.13 = (f32[18,8,128]{2,1,0:T(8,128)S(1)}, f32[18,8,128]{2,1,0:T(8,128)S(1)}, u32[]{:S(2)}, u32[]{:S(2)}) collective-permute-start(f32[18,8,128]{2,1,0:T(8,128)S(1)} %get-tuple-element.122), channel_id=1, source_target_pairs={{0,48},{1,32},{2,33},{3,34},{7,35},{6,39},{5,38},{4,37},{8,36},{9,... | collective-permute-start | bytes 221192 | tf_op jit(solution)/shard_map/ppermute | solution.py:459
  47.2 4.5 %collective-permute-start.14 = (f32[21,8,128]{2,1,0:T(8,128)S(1)}, f32[21,8,128]{2,1,0:T(8,128)S(1)}, u32[]{:S(2)}, u32[]{:S(2)}) collective-permute-start(f32[21,8,128]{2,1,0:T(8,128)S(1)} %get-tuple-element.128), channel_id=1, source_target_pairs={{0,33},{1,34},{2,35},{3,39},{7,38},{6,37},{5,36},{4,40},{8,41},{9,... | collective-permute-start | bytes 258056 | tf_op jit(solution)/shard_map/ppermute | solution.py:459
  48.7 3.7 %collective-permute-start.15 = (f32[12,8,128]{2,1,0:T(8,128)S(1)}, f32[12,8,128]{2,1,0:T(8,128)S(1)}, u32[]{:S(2)}, u32[]{:S(2)}) collective-permute-start(f32[12,8,128]{2,1,0:T(8,128)S(1)} %get-tuple-element.133), channel_id=1, source_target_pairs={{0,48},{1,32},{2,33},{3,34},{7,35},{6,39},{5,38},{4,37},{8,36},{9,... | collective-permute-start | bytes 147464 | tf_op jit(solution)/shard_map/ppermute | solution.py:459
  52.8 4.3 %collective-permute-start.16 = (f32[18,8,128]{2,1,0:T(8,128)S(1)}, f32[18,8,128]{2,1,0:T(8,128)S(1)}, u32[]{:S(2)}, u32[]{:S(2)}) collective-permute-start(f32[18,8,128]{2,1,0:T(8,128)S(1)} %get-tuple-element.140), channel_id=1, source_target_pairs={{0,33},{1,34},{2,35},{3,39},{7,38},{6,37},{5,36},{4,40},{8,41},{9,... | collective-permute-start | bytes 221192 | tf_op jit(solution)/shard_map/ppermute | solution.py:459
  53.6 4.3 %collective-permute-start.17 = (f32[18,8,128]{2,1,0:T(8,128)S(1)}, f32[18,8,128]{2,1,0:T(8,128)S(1)}, u32[]{:S(2)}, u32[]{:S(2)}) collective-permute-start(f32[18,8,128]{2,1,0:T(8,128)S(1)} %get-tuple-element.141), channel_id=1, source_target_pairs={{0,48},{1,32},{2,33},{3,34},{7,35},{6,39},{5,38},{4,37},{8,36},{9,... | collective-permute-start | bytes 221192 | tf_op jit(solution)/shard_map/ppermute | solution.py:459
  58.2 4.6 %collective-permute-start.18 = (f32[21,8,128]{2,1,0:T(8,128)S(1)}, f32[21,8,128]{2,1,0:T(8,128)S(1)}, u32[]{:S(2)}, u32[]{:S(2)}) collective-permute-start(f32[21,8,128]{2,1,0:T(8,128)S(1)} %get-tuple-element.147), channel_id=1, source_target_pairs={{0,33},{1,34},{2,35},{3,39},{7,38},{6,37},{5,36},{4,40},{8,41},{9,... | collective-permute-start | bytes 258056 | tf_op jit(solution)/shard_map/ppermute | solution.py:459
  59.0 3.9 %collective-permute-start.19 = (f32[12,8,128]{2,1,0:T(8,128)S(1)}, f32[12,8,128]{2,1,0:T(8,128)S(1)}, u32[]{:S(2)}, u32[]{:S(2)}) collective-permute-start(f32[12,8,128]{2,1,0:T(8,128)S(1)} %get-tuple-element.152), channel_id=1, source_target_pairs={{0,48},{1,32},{2,33},{3,34},{7,35},{6,39},{5,38},{4,37},{8,36},{9,... | collective-permute-start | bytes 147464 | tf_op jit(solution)/shard_map/ppermute | solution.py:459
  63.3 4.3 %collective-permute-start.20 = (f32[18,8,128]{2,1,0:T(8,128)S(1)}, f32[18,8,128]{2,1,0:T(8,128)S(1)}, u32[]{:S(2)}, u32[]{:S(2)}) collective-permute-start(f32[18,8,128]{2,1,0:T(8,128)S(1)} %get-tuple-element.159), channel_id=1, source_target_pairs={{0,33},{1,34},{2,35},{3,39},{7,38},{6,37},{5,36},{4,40},{8,41},{9,... | collective-permute-start | bytes 221192 | tf_op jit(solution)/shard_map/ppermute | solution.py:459
  64.0 4.1 %collective-permute-start.21 = (f32[18,8,128]{2,1,0:T(8,128)S(1)}, f32[18,8,128]{2,1,0:T(8,128)S(1)}, u32[]{:S(2)}, u32[]{:S(2)}) collective-permute-start(f32[18,8,128]{2,1,0:T(8,128)S(1)} %get-tuple-element.160), channel_id=1, source_target_pairs={{0,48},{1,32},{2,33},{3,34},{7,35},{6,39},{5,38},{4,37},{8,36},{9,... | collective-permute-start | bytes 221192 | tf_op jit(solution)/shard_map/ppermute | solution.py:459
  68.5 3.8 %collective-permute-start.22 = (f32[12,8,128]{2,1,0:T(8,128)S(1)}, f32[12,8,128]{2,1,0:T(8,128)S(1)}, u32[]{:S(2)}, u32[]{:S(2)}) collective-permute-start(f32[12,8,128]{2,1,0:T(8,128)S(1)} %get-tuple-element.164), channel_id=1, source_target_pairs={{0,33},{1,34},{2,35},{3,39},{7,38},{6,37},{5,36},{4,40},{8,41},{9,... | collective-permute-start | bytes 147464 | tf_op jit(solution)/shard_map/ppermute | solution.py:459
  69.3 3.7 %collective-permute-start.23 = (f32[12,8,128]{2,1,0:T(8,128)S(1)}, f32[12,8,128]{2,1,0:T(8,128)S(1)}, u32[]{:S(2)}, u32[]{:S(2)}) collective-permute-start(f32[12,8,128]{2,1,0:T(8,128)S(1)} %get-tuple-element.165), channel_id=1, source_target_pairs={{0,48},{1,32},{2,33},{3,34},{7,35},{6,39},{5,38},{4,37},{8,36},{9,... | collective-permute-start | bytes 147464 | tf_op jit(solution)/shard_map/ppermute | solution.py:459
  73.3 1.4 %collective-permute-start.24 = (f32[24,8,128]{2,1,0:T(8,128)S(1)}, f32[24,8,128]{2,1,0:T(8,128)S(1)}, u32[]{:S(2)}, u32[]{:S(2)}) collective-permute-start(f32[24,8,128]{2,1,0:T(8,128)S(1)} %get-tuple-element.170), channel_id=1, source_target_pairs={{0,32},{1,33},{2,34},{3,35},{7,39},{6,38},{5,37},{4,36},{8,40},{9,... | collective-permute-start | bytes 294920 | tf_op jit(solution)/shard_map/ppermute | solution.py:559
  74.7 15.1 %collective-permute-start.26 = (f32[25,8,128]{2,1,0:T(8,128)S(1)}, f32[25,8,128]{2,1,0:T(8,128)S(1)}, u32[]{:S(2)}, u32[]{:S(2)}) collective-permute-start(f32[25,8,128]{2,1,0:T(8,128)S(1)} %shard_map.101.rest_0_), channel_id=1, source_target_pairs={{0,64},{1,65},{2,66},{3,67},{7,68},{6,69},{5,70},{4,71},{8,72},{9,... | collective-permute-start | bytes 307208 | tf_op jit(solution)/shard_map/ppermute | solution.py:561
  82.0 7.7 %collective-permute-start.25 = (f32[24,8,128]{2,1,0:T(8,128)S(1)}, f32[24,8,128]{2,1,0:T(8,128)S(1)}, u32[]{:S(2)}, u32[]{:S(2)}) collective-permute-start(f32[24,8,128]{2,1,0:T(8,128)S(1)} %shard_map.102), channel_id=1, source_target_pairs={{0,0},{1,1},{2,2},{3,3},{7,4},{6,5},{5,6},{4,7},{8,8},{9,9},{10,10... | collective-permute-start | bytes 294920 | tf_op jit(solution)/shard_map/ppermute | solution.py:563

commit v5 on v4

--- a/solution.py
+++ b/solution.py
@@ -198,14 +198,14 @@
     return beyond, [jnp.where(lower, b, a) for a, b in zip(above, below)]
 
 
-def kernel_call(body, inputs, outputs, far=(), near=(), scratch=()):
-    spec = pl.BlockSpec(memory_space=VMEM)
+def kernel_call(body, inputs, outputs, far=(), near=(), scratch=(), target=VMEM):
+    spec = pl.BlockSpec(memory_space=target)
     spaces = [pltpu.HBM if at in far else pltpu.SMEM if at in near else VMEM for at in range(len(inputs))]
     inputs = [
         value if at in near else pltpu.with_memory_space_constraint(value, space)
         for at, (value, space) in enumerate(zip(inputs, spaces))
     ]
-    shapes = [VMEM(shape, jnp.float32) for shape in outputs]
+    shapes = [target(shape, jnp.float32) for shape in outputs]
     return pl.pallas_call(
         body,
         in_specs=[pl.BlockSpec(memory_space=space) for space in spaces],
@@ -440,14 +440,19 @@
         out[24] = marks[HALF]
 
 
-def deliver(got0, got1, marks, out):
+def deliver(got0, got1, marks, out, held, sems):
     half = marks[HALF] > 0
-    for column in range(2):
-        for part in range(6):
+    copies = []
+    for part in range(6):
+        for column in range(2):
             for spin in range(2):
                 at = column * 12 + part * 2 + spin
-                out[part, spin, column] = jnp.where(half, got1[at], got0[at])
-                out[part, spin, 2 + column] = jnp.where(half, got0[at], got1[at])
+                held[part, spin, column] = jnp.where(half, got1[at], got0[at])
+                held[part, spin, 2 + column] = jnp.where(half, got0[at], got1[at])
+        copies.append(pltpu.make_async_copy(held.at[part], out.at[part], sems.at[part]))
+        copies[-1].start()
+    for copy in copies:
+        copy.wait()
 
 
 def registers(value, lead):
@@ -561,7 +566,14 @@
     got1 = lax.ppermute(out1, AXES, COLLECT[1])
     (out0,) = kernel_call(functools.partial(both_columns, 0), [mine, other, marks, out1], [(24, 8, 128)])
     got0 = lax.ppermute(out0, AXES, COLLECT[0])
-    (out,) = kernel_call(deliver, [got0, got1, marks], [(6, 2, 4, 8, 128)])
+    whole = (6, 2, 4, 8, 128)
+    (out,) = kernel_call(
+        deliver,
+        [got0, got1, marks],
+        [whole],
+        scratch=[VMEM(whole, jnp.float32), pltpu.SemaphoreType.DMA((6,))],
+        target=pltpu.HBM,
+    )
     out = jnp.swapaxes(out.reshape(2, 3, 2, 4, 4, 2, 128), -3, -2)
     return out.reshape(1, 2, 3, 2, 4, 2, 512)
 

time: 90.6 us -> 90.8 us (level)
  no operation moved by 1% of the time
where the time goes in v5:
time: 90.8 us; the launch traced here: 90.6 us
  starting transfers between devices  41.7 us (46%)
  waiting for transfers between devices  40 us (44%)
  Pallas kernels  8.09 us (9%)
    ppermute x9, waiting for transfers between devices, exchange(): lax.ppermute(to_above, AXES, UP)  19.1 us
    ppermute x9, starting transfers between devices, exchange(): lax.ppermute(to_below, AXES, DOWN)  10.4 us
    pallas_call x40, Pallas kernels, kernel_call(): pl.pallas_call(body, in_specs=[pl.BlockSpec(memory_space=space) for space...  8.09 us
    ppermute x1, starting transfers between devices, local(): got1 = lax.ppermute(out1, AXES, COLLECT[1])  7.34 us
    ppermute x9, starting transfers between devices, exchange(): lax.ppermute(to_above, AXES, UP)  6.14 us
    ppermute x1, waiting for transfers between devices, local(): got0 = lax.ppermute(out0, AXES, COLLECT[0])  5.79 us
    ppermute x1, waiting for transfers between devices, local(): links_own = lax.ppermute(message, AXES, SPREAD)  5.26 us
    ppermute x1, starting transfers between devices, local(): links_own = lax.ppermute(message, AXES, SPREAD)  5.05 us
  transfers between devices with their start and end apart: 27, of which 21 were waited for; matrix products, arithmetic and copies ran while one was open for 0% of the time, Pallas kernels for 3%

profile of v5, /device:TPU:32, one launch (start us, length us, event | category | flops | bytes accessed | tf_op | source)
XLA Modules:
  0.0 90.6 jit_solution(16311757725368996639)
XLA Ops:
  0.1 1.2 %shard_map.64 = (f32[99,8,128]{2,1,0:T(8,128)S(1)}, f32[6,2,4,8,128]{4,3,2,1,0:T(8,128)S(1)}) custom-call(f32[54,8,128]{2,1,0:T(8,128)} %bitcast.35, f32[18,8,128]{2,1,0:T(8,128)} %bitcast.38, f32[54,8,128]{2,1,0:T(8,128)} %bitcast.36, f32[6,2,4,8,128]{4,3,2,1,0:T(8,128)} %bitcast.37), custom_call_target="tpu_custom_call" | custom-call | tf_op jit(solution)/shard_map/pallas_call | solution.py:209
  1.4 5.1 %collective-permute-start = (f32[66,8,128]{2,1,0:T(8,128)S(1)}, f32[66,8,128]{2,1,0:T(8,128)S(1)}, u32[]{:S(2)}, u32[]{:S(2)}) collective-permute-start(f32[66,8,128]{2,1,0:T(8,128)S(1)} %shard_map.65), channel_id=1, source_target_pairs={{0,0},{1,1},{2,2},{3,3},{4,7},{5,6},{6,5},{7,4},{8,8},{9,9},{10,10... | collective-permute-start | bytes 811016 | tf_op jit(solution)/shard_map/ppermute | solution.py:494
  6.5 4.3 %collective-permute-start.4 = (f32[57,8,128]{2,1,0:T(8,128)S(1)}, f32[57,8,128]{2,1,0:T(8,128)S(1)}, u32[]{:S(2)}, u32[]{:S(2)}) collective-permute-start(f32[57,8,128]{2,1,0:T(8,128)S(1)} %shard_map.69), channel_id=1, source_target_pairs={{0,0},{1,1},{2,2},{3,3},{4,7},{5,6},{6,5},{7,4},{8,8},{9,9},{10,10... | collective-permute-start | bytes 700424 | tf_op jit(solution)/shard_map/ppermute | solution.py:496
  10.8 5.3 %collective-permute-done.own = f32[66,8,128]{2,1,0:T(8,128)S(1)} collective-permute-done((f32[66,8,128]{2,1,0:T(8,128)S(1)}, f32[66,8,128]{2,1,0:T(8,128)S(1)}, u32[]{:S(2)}, u32[]{:S(2)}) %collective-permute-start) | collective-permute-done | bytes 270368 | tf_op jit(solution)/shard_map/ppermute | solution.py:494
  16.1 3.1 %collective-permute-start.1 = (f32[54,8,128]{2,1,0:T(8,128)S(1)}, f32[54,8,128]{2,1,0:T(8,128)S(1)}, u32[]{:S(2)}, u32[]{:S(2)}) collective-permute-start(f32[54,8,128]{2,1,0:T(8,128)S(1)} %slice.8), channel_id=1, source_target_pairs={{0,64},{1,65},{2,66},{3,67},{7,71},{6,70},{5,69},{4,68},{8,72},{9,... | collective-permute-start | bytes 663560 | tf_op jit(solution)/shard_map/ppermute | solution.py:497
  19.2 1.0 %collective-permute-done.4.own.others = f32[57,8,128]{2,1,0:T(8,128)S(1)} collective-permute-done((f32[57,8,128]{2,1,0:T(8,128)S(1)}, f32[57,8,128]{2,1,0:T(8,128)S(1)}, u32[]{:S(2)}, u32[]{:S(2)}) %collective-permute-start.4) | collective-permute-done | bytes 233504 | tf_op jit(solution)/shard_map/ppermute | solution.py:496
  20.1 3.1 %collective-permute-start.5 = (f32[45,8,128]{2,1,0:T(8,128)S(1)}, f32[45,8,128]{2,1,0:T(8,128)S(1)}, u32[]{:S(2)}, u32[]{:S(2)}) collective-permute-start(f32[45,8,128]{2,1,0:T(8,128)S(1)} %slice.9), channel_id=1, source_target_pairs={{0,64},{1,65},{2,66},{3,67},{7,71},{6,70},{5,69},{4,68},{8,72},{9,... | collective-permute-start | bytes 552968 | tf_op jit(solution)/shard_map/ppermute | solution.py:498
  23.2 0.5 collective-permute-done.1.facing
  23.9 3.7 %collective-permute-done.5.facing = f32[45,8,128]{2,1,0:T(8,128)S(1)} collective-permute-done((f32[45,8,128]{2,1,0:T(8,128)S(1)}, f32[45,8,128]{2,1,0:T(8,128)S(1)}, u32[]{:S(2)}, u32[]{:S(2)}) %collective-permute-start.5) | collective-permute-done | bytes 184352 | tf_op jit(solution)/shard_map/ppermute | solution.py:498
  28.2 1.7 %collective-permute-start.7 = (f32[12,8,128]{2,1,0:T(8,128)S(1)}, f32[12,8,128]{2,1,0:T(8,128)S(1)}, u32[]{:S(2)}, u32[]{:S(2)}) collective-permute-start(f32[12,8,128]{2,1,0:T(8,128)S(1)} %get-tuple-element.96._), channel_id=1, source_target_pairs={{0,48},{1,32},{2,33},{3,34},{7,35},{6,39},{5,38},{4,37},{8,36},{9,... | collective-permute-start | bytes 147464 | tf_op jit(solution)/shard_map/ppermute | solution.py:464
  30.0 2.4 %collective-permute-done.3.from_below = f32[21,8,128]{2,1,0:T(8,128)S(1)} collective-permute-done((f32[21,8,128]{2,1,0:T(8,128)S(1)}, f32[21,8,128]{2,1,0:T(8,128)S(1)}, u32[]{:S(2)}, u32[]{:S(2)}) %collective-permute-start.3) | collective-permute-done | bytes 86048 | tf_op jit(solution)/shard_map/ppermute | solution.py:464
  32.5 0.4 shard_map.73
  32.9 0.4 collective-permute-start.8
  33.4 1.4 %collective-permute-start.9 = (f32[12,8,128]{2,1,0:T(8,128)S(1)}, f32[12,8,128]{2,1,0:T(8,128)S(1)}, u32[]{:S(2)}, u32[]{:S(2)}) collective-permute-start(f32[12,8,128]{2,1,0:T(8,128)S(1)} %get-tuple-element.103), channel_id=1, source_target_pairs={{0,48},{1,32},{2,33},{3,34},{7,35},{6,39},{5,38},{4,37},{8,36},{9,... | collective-permute-start | bytes 147464 | tf_op jit(solution)/shard_map/ppermute | solution.py:464
  35.0 0.6 shard_map.75
  35.6 0.9 %collective-permute-done.8.from_below = f32[12,8,128]{2,1,0:T(8,128)S(1)} collective-permute-done((f32[12,8,128]{2,1,0:T(8,128)S(1)}, f32[12,8,128]{2,1,0:T(8,128)S(1)}, u32[]{:S(2)}, u32[]{:S(2)}) %collective-permute-start.8) | collective-permute-done | bytes 49184 | tf_op jit(solution)/shard_map/ppermute | solution.py:464
  37.2 0.4 collective-permute-start.10
  37.6 1.4 %collective-permute-start.11 = (f32[12,8,128]{2,1,0:T(8,128)S(1)}, f32[12,8,128]{2,1,0:T(8,128)S(1)}, u32[]{:S(2)}, u32[]{:S(2)}) collective-permute-start(f32[12,8,128]{2,1,0:T(8,128)S(1)} %get-tuple-element.114), channel_id=1, source_target_pairs={{0,48},{1,32},{2,33},{3,34},{7,35},{6,39},{5,38},{4,37},{8,36},{9,... | collective-permute-start | bytes 147464 | tf_op jit(solution)/shard_map/ppermute | solution.py:464
  39.4 2.2 %collective-permute-done.10.from_below = f32[21,8,128]{2,1,0:T(8,128)S(1)} collective-permute-done((f32[21,8,128]{2,1,0:T(8,128)S(1)}, f32[21,8,128]{2,1,0:T(8,128)S(1)}, u32[]{:S(2)}, u32[]{:S(2)}) %collective-permute-start.10) | collective-permute-done | bytes 86048 | tf_op jit(solution)/shard_map/ppermute | solution.py:464
  41.7 0.4 shard_map.82
  42.1 0.7 collective-permute-start.12
  42.7 1.3 %collective-permute-start.13 = (f32[18,8,128]{2,1,0:T(8,128)S(1)}, f32[18,8,128]{2,1,0:T(8,128)S(1)}, u32[]{:S(2)}, u32[]{:S(2)}) collective-permute-start(f32[18,8,128]{2,1,0:T(8,128)S(1)} %get-tuple-element.122), channel_id=1, source_target_pairs={{0,48},{1,32},{2,33},{3,34},{7,35},{6,39},{5,38},{4,37},{8,36},{9,... | collective-permute-start | bytes 221192 | tf_op jit(solution)/shard_map/ppermute | solution.py:464
  44.1 2.2 %collective-permute-done.12.from_below.rims_below = f32[18,8,128]{2,1,0:T(8,128)S(1)} collective-permute-done((f32[18,8,128]{2,1,0:T(8,128)S(1)}, f32[18,8,128]{2,1,0:T(8,128)S(1)}, u32[]{:S(2)}, u32[]{:S(2)}) %collective-permute-start.12) | collective-permute-done | bytes 73760 | tf_op jit(solution)/shard_map/ppermute | solution.py:464
  46.4 0.5 collective-permute-done.13.from_above.rims_above
  47.2 1.5 %collective-permute-start.14 = (f32[21,8,128]{2,1,0:T(8,128)S(1)}, f32[21,8,128]{2,1,0:T(8,128)S(1)}, u32[]{:S(2)}, u32[]{:S(2)}) collective-permute-start(f32[21,8,128]{2,1,0:T(8,128)S(1)} %get-tuple-element.128), channel_id=1, source_target_pairs={{0,33},{1,34},{2,35},{3,39},{7,38},{6,37},{5,36},{4,40},{8,41},{9,... | collective-permute-start | bytes 258056 | tf_op jit(solution)/shard_map/ppermute | solution.py:464
  49.2 2.5 %collective-permute-done.14.from_below = f32[21,8,128]{2,1,0:T(8,128)S(1)} collective-permute-done((f32[21,8,128]{2,1,0:T(8,128)S(1)}, f32[21,8,128]{2,1,0:T(8,128)S(1)}, u32[]{:S(2)}, u32[]{:S(2)}) %collective-permute-start.14) | collective-permute-done | bytes 86048 | tf_op jit(solution)/shard_map/ppermute | solution.py:464
  51.8 0.6 collective-permute-done.15.from_above
  52.8 0.8 collective-permute-start.16
  53.6 1.1 %collective-permute-start.17 = (f32[18,8,128]{2,1,0:T(8,128)S(1)}, f32[18,8,128]{2,1,0:T(8,128)S(1)}, u32[]{:S(2)}, u32[]{:S(2)}) collective-permute-start(f32[18,8,128]{2,1,0:T(8,128)S(1)} %get-tuple-element.141), channel_id=1, source_target_pairs={{0,48},{1,32},{2,33},{3,34},{7,35},{6,39},{5,38},{4,37},{8,36},{9,... | collective-permute-start | bytes 221192 | tf_op jit(solution)/shard_map/ppermute | solution.py:464
  54.7 2.4 %collective-permute-done.16.from_below.rims_below = f32[18,8,128]{2,1,0:T(8,128)S(1)} collective-permute-done((f32[18,8,128]{2,1,0:T(8,128)S(1)}, f32[18,8,128]{2,1,0:T(8,128)S(1)}, u32[]{:S(2)}, u32[]{:S(2)}) %collective-permute-start.16) | collective-permute-done | bytes 73760 | tf_op jit(solution)/shard_map/ppermute | solution.py:464
  57.1 0.7 collective-permute-done.17.from_above.rims_above
  58.2 0.8 collective-permute-start.18
  59.0 1.0 %collective-permute-start.19 = (f32[12,8,128]{2,1,0:T(8,128)S(1)}, f32[12,8,128]{2,1,0:T(8,128)S(1)}, u32[]{:S(2)}, u32[]{:S(2)}) collective-permute-start(f32[12,8,128]{2,1,0:T(8,128)S(1)} %get-tuple-element.152), channel_id=1, source_target_pairs={{0,48},{1,32},{2,33},{3,34},{7,35},{6,39},{5,38},{4,37},{8,36},{9,... | collective-permute-start | bytes 147464 | tf_op jit(solution)/shard_map/ppermute | solution.py:464
  60.2 2.6 %collective-permute-done.18.from_below = f32[21,8,128]{2,1,0:T(8,128)S(1)} collective-permute-done((f32[21,8,128]{2,1,0:T(8,128)S(1)}, f32[21,8,128]{2,1,0:T(8,128)S(1)}, u32[]{:S(2)}, u32[]{:S(2)}) %collective-permute-start.18) | collective-permute-done | bytes 86048 | tf_op jit(solution)/shard_map/ppermute | solution.py:464
  62.9 0.4 shard_map.94
  63.3 0.7 collective-permute-start.20
  64.0 1.1 %collective-permute-start.21 = (f32[18,8,128]{2,1,0:T(8,128)S(1)}, f32[18,8,128]{2,1,0:T(8,128)S(1)}, u32[]{:S(2)}, u32[]{:S(2)}) collective-permute-start(f32[18,8,128]{2,1,0:T(8,128)S(1)} %get-tuple-element.160), channel_id=1, source_target_pairs={{0,48},{1,32},{2,33},{3,34},{7,35},{6,39},{5,38},{4,37},{8,36},{9,... | collective-permute-start | bytes 221192 | tf_op jit(solution)/shard_map/ppermute | solution.py:464
  65.2 2.4 %collective-permute-done.20.from_below.rims_below = f32[18,8,128]{2,1,0:T(8,128)S(1)} collective-permute-done((f32[18,8,128]{2,1,0:T(8,128)S(1)}, f32[18,8,128]{2,1,0:T(8,128)S(1)}, u32[]{:S(2)}, u32[]{:S(2)}) %collective-permute-start.20) | collective-permute-done | bytes 73760 | tf_op jit(solution)/shard_map/ppermute | solution.py:464
  67.6 0.5 collective-permute-done.21.from_above.rims_above
  68.5 0.8 collective-permute-start.22
  69.3 1.0 %collective-permute-start.23 = (f32[12,8,128]{2,1,0:T(8,128)S(1)}, f32[12,8,128]{2,1,0:T(8,128)S(1)}, u32[]{:S(2)}, u32[]{:S(2)}) collective-permute-start(f32[12,8,128]{2,1,0:T(8,128)S(1)} %get-tuple-element.165), channel_id=1, source_target_pairs={{0,48},{1,32},{2,33},{3,34},{7,35},{6,39},{5,38},{4,37},{8,36},{9,... | collective-permute-start | bytes 147464 | tf_op jit(solution)/shard_map/ppermute | solution.py:464
  71.0 1.3 %collective-permute-done.22.from_below = f32[12,8,128]{2,1,0:T(8,128)S(1)} collective-permute-done((f32[12,8,128]{2,1,0:T(8,128)S(1)}, f32[12,8,128]{2,1,0:T(8,128)S(1)}, u32[]{:S(2)}, u32[]{:S(2)}) %collective-permute-start.22) | collective-permute-done | bytes 49184 | tf_op jit(solution)/shard_map/ppermute | solution.py:464
  72.2 0.8 collective-permute-done.23.from_above
  73.5 1.2 %collective-permute-done.24.other = f32[24,8,128]{2,1,0:T(8,128)S(1)} collective-permute-done((f32[24,8,128]{2,1,0:T(8,128)S(1)}, f32[24,8,128]{2,1,0:T(8,128)S(1)}, u32[]{:S(2)}, u32[]{:S(2)}) %collective-permute-start.24) | collective-permute-done | bytes 98336 | tf_op jit(solution)/shard_map/ppermute | solution.py:564
  74.7 7.3 %collective-permute-start.26 = (f32[25,8,128]{2,1,0:T(8,128)S(1)}, f32[25,8,128]{2,1,0:T(8,128)S(1)}, u32[]{:S(2)}, u32[]{:S(2)}) collective-permute-start(f32[25,8,128]{2,1,0:T(8,128)S(1)} %shard_map.101.rest_0_), channel_id=1, source_target_pairs={{0,64},{1,65},{2,66},{3,67},{7,68},{6,69},{5,70},{4,71},{8,72},{9,... | collective-permute-start | bytes 307208 | tf_op jit(solution)/shard_map/ppermute | solution.py:566
  82.0 1.9 %collective-permute-start.25 = (f32[24,8,128]{2,1,0:T(8,128)S(1)}, f32[24,8,128]{2,1,0:T(8,128)S(1)}, u32[]{:S(2)}, u32[]{:S(2)}) collective-permute-start(f32[24,8,128]{2,1,0:T(8,128)S(1)} %shard_map.102), channel_id=1, source_target_pairs={{0,0},{1,1},{2,2},{3,3},{7,4},{6,5},{5,6},{4,7},{8,8},{9,9},{10,10... | collective-permute-start | bytes 294920 | tf_op jit(solution)/shard_map/ppermute | solution.py:568
  84.0 5.8 %collective-permute-done.25.got0 = f32[24,8,128]{2,1,0:T(8,128)S(1)} collective-permute-done((f32[24,8,128]{2,1,0:T(8,128)S(1)}, f32[24,8,128]{2,1,0:T(8,128)S(1)}, u32[]{:S(2)}, u32[]{:S(2)}) %collective-permute-start.25) | collective-permute-done | bytes 98336 | tf_op jit(solution)/shard_map/ppermute | solution.py:568
  89.8 0.7 shard_map.103
  (56 shorter events, 5.9 us)
Async XLA Ops:
  1.4 5.1 %copy-start = (f32[2,3,2,4,2,512]{5,4,3,2,1,0:T(2,128)S(1)}, f32[2,3,2,4,2,512]{5,4,3,2,1,0:T(2,128)}, u32[]{:S(2)}) copy-start(f32[2,3,2,4,2,512]{5,4,3,2,1,0:T(2,128)} %param.7) | copy-start | bytes 589828
  1.4 14.7 %collective-permute-start = (f32[66,8,128]{2,1,0:T(8,128)S(1)}, f32[66,8,128]{2,1,0:T(8,128)S(1)}, u32[]{:S(2)}, u32[]{:S(2)}) collective-permute-start(f32[66,8,128]{2,1,0:T(8,128)S(1)} %shard_map.65), channel_id=1, source_target_pairs={{0,0},{1,1},{2,2},{3,3},{4,7},{5,6},{6,5},{7,4},{8,8},{9,9},{10,10... | collective-permute-start | bytes 811016 | tf_op jit(solution)/shard_map/ppermute | solution.py:494
  6.5 13.6 %collective-permute-start.4 = (f32[57,8,128]{2,1,0:T(8,128)S(1)}, f32[57,8,128]{2,1,0:T(8,128)S(1)}, u32[]{:S(2)}, u32[]{:S(2)}) collective-permute-start(f32[57,8,128]{2,1,0:T(8,128)S(1)} %shard_map.69), channel_id=1, source_target_pairs={{0,0},{1,1},{2,2},{3,3},{4,7},{5,6},{6,5},{7,4},{8,8},{9,9},{10,10... | collective-permute-start | bytes 700424 | tf_op jit(solution)/shard_map/ppermute | solution.py:496
  16.1 7.6 %collective-permute-start.1 = (f32[54,8,128]{2,1,0:T(8,128)S(1)}, f32[54,8,128]{2,1,0:T(8,128)S(1)}, u32[]{:S(2)}, u32[]{:S(2)}) collective-permute-start(f32[54,8,128]{2,1,0:T(8,128)S(1)} %slice.8), channel_id=1, source_target_pairs={{0,64},{1,65},{2,66},{3,67},{7,71},{6,70},{5,69},{4,68},{8,72},{9,... | collective-permute-start | bytes 663560 | tf_op jit(solution)/shard_map/ppermute | solution.py:497
  20.1 7.4 %collective-permute-start.5 = (f32[45,8,128]{2,1,0:T(8,128)S(1)}, f32[45,8,128]{2,1,0:T(8,128)S(1)}, u32[]{:S(2)}, u32[]{:S(2)}) collective-permute-start(f32[45,8,128]{2,1,0:T(8,128)S(1)} %slice.9), channel_id=1, source_target_pairs={{0,64},{1,65},{2,66},{3,67},{7,71},{6,70},{5,69},{4,68},{8,72},{9,... | collective-permute-start | bytes 552968 | tf_op jit(solution)/shard_map/ppermute | solution.py:498
  23.8 4.1 %collective-permute-start.2 = (f32[108,8,128]{2,1,0:T(8,128)S(1)}, f32[108,8,128]{2,1,0:T(8,128)S(1)}, u32[]{:S(2)}, u32[]{:S(2)}) collective-permute-start(f32[108,8,128]{2,1,0:T(8,128)S(1)} %shard_map.66), channel_id=1, source_target_pairs={{0,32},{1,33},{2,34},{3,35},{7,39},{6,38},{5,37},{4,36},{8,40},{9,... | collective-permute-start | bytes 1327112 | tf_op jit(solution)/shard_map/ppermute | solution.py:502
  27.6 2.3 %collective-permute-start.6 = (f32[90,8,128]{2,1,0:T(8,128)S(1)}, f32[90,8,128]{2,1,0:T(8,128)S(1)}, u32[]{:S(2)}, u32[]{:S(2)}) collective-permute-start(f32[90,8,128]{2,1,0:T(8,128)S(1)} %shard_map.70), channel_id=1, source_target_pairs={{0,32},{1,33},{2,34},{3,35},{7,39},{6,38},{5,37},{4,36},{8,40},{9,... | collective-permute-start | bytes 1105928 | tf_op jit(solution)/shard_map/ppermute | solution.py:506
  28.1 4.3 %collective-permute-start.3 = (f32[21,8,128]{2,1,0:T(8,128)S(1)}, f32[21,8,128]{2,1,0:T(8,128)S(1)}, u32[]{:S(2)}, u32[]{:S(2)}) collective-permute-start(f32[21,8,128]{2,1,0:T(8,128)S(1)} %get-tuple-element.91), channel_id=1, source_target_pairs={{0,33},{1,34},{2,35},{3,39},{7,38},{6,37},{5,36},{4,40},{8,41},{9,... | collective-permute-start | bytes 258056 | tf_op jit(solution)/shard_map/ppermute | solution.py:464
  28.2 4.3 %collective-permute-start.7 = (f32[12,8,128]{2,1,0:T(8,128)S(1)}, f32[12,8,128]{2,1,0:T(8,128)S(1)}, u32[]{:S(2)}, u32[]{:S(2)}) collective-permute-start(f32[12,8,128]{2,1,0:T(8,128)S(1)} %get-tuple-element.96._), channel_id=1, source_target_pairs={{0,48},{1,32},{2,33},{3,34},{7,35},{6,39},{5,38},{4,37},{8,36},{9,... | collective-permute-start | bytes 147464 | tf_op jit(solution)/shard_map/ppermute | solution.py:464
  32.9 3.6 %collective-permute-start.8 = (f32[12,8,128]{2,1,0:T(8,128)S(1)}, f32[12,8,128]{2,1,0:T(8,128)S(1)}, u32[]{:S(2)}, u32[]{:S(2)}) collective-permute-start(f32[12,8,128]{2,1,0:T(8,128)S(1)} %get-tuple-element.102), channel_id=1, source_target_pairs={{0,33},{1,34},{2,35},{3,39},{7,38},{6,37},{5,36},{4,40},{8,41},{9,... | collective-permute-start | bytes 147464 | tf_op jit(solution)/shard_map/ppermute | solution.py:464
  33.4 1.6 %copy-start.1 = (s32[4]{0:T(128)S(1)}, s32[4]{0:T(128)}, u32[]{:S(2)}) copy-start(s32[4]{0:T(128)} %source_slice.1) | copy-start | bytes 52
  33.4 3.5 %collective-permute-start.9 = (f32[12,8,128]{2,1,0:T(8,128)S(1)}, f32[12,8,128]{2,1,0:T(8,128)S(1)}, u32[]{:S(2)}, u32[]{:S(2)}) collective-permute-start(f32[12,8,128]{2,1,0:T(8,128)S(1)} %get-tuple-element.103), channel_id=1, source_target_pairs={{0,48},{1,32},{2,33},{3,34},{7,35},{6,39},{5,38},{4,37},{8,36},{9,... | collective-permute-start | bytes 147464 | tf_op jit(solution)/shard_map/ppermute | solution.py:464
  37.2 4.3 %collective-permute-start.10 = (f32[21,8,128]{2,1,0:T(8,128)S(1)}, f32[21,8,128]{2,1,0:T(8,128)S(1)}, u32[]{:S(2)}, u32[]{:S(2)}) collective-permute-start(f32[21,8,128]{2,1,0:T(8,128)S(1)} %get-tuple-element.109), channel_id=1, source_target_pairs={{0,33},{1,34},{2,35},{3,39},{7,38},{6,37},{5,36},{4,40},{8,41},{9,... | collective-permute-start | bytes 258056 | tf_op jit(solution)/shard_map/ppermute | solution.py:464
  37.6 4.0 %collective-permute-start.11 = (f32[12,8,128]{2,1,0:T(8,128)S(1)}, f32[12,8,128]{2,1,0:T(8,128)S(1)}, u32[]{:S(2)}, u32[]{:S(2)}) collective-permute-start(f32[12,8,128]{2,1,0:T(8,128)S(1)} %get-tuple-element.114), channel_id=1, source_target_pairs={{0,48},{1,32},{2,33},{3,34},{7,35},{6,39},{5,38},{4,37},{8,36},{9,... | collective-permute-start | bytes 147464 | tf_op jit(solution)/shard_map/ppermute | solution.py:464
  42.1 4.3 %collective-permute-start.12 = (f32[18,8,128]{2,1,0:T(8,128)S(1)}, f32[18,8,128]{2,1,0:T(8,128)S(1)}, u32[]{:S(2)}, u32[]{:S(2)}) collective-permute-start(f32[18,8,128]{2,1,0:T(8,128)S(1)} %get-tuple-element.121), channel_id=1, source_target_pairs={{0,33},{1,34},{2,35},{3,39},{7,38},{6,37},{5,36},{4,40},{8,41},{9,... | collective-permute-start | bytes 221192 | tf_op jit(solution)/shard_map/ppermute | solution.py:464
  42.7 4.1 %collective-permute-start.13 = (f32[18,8,128]{2,1,0:T(8,128)S(1)}, f32[18,8,128]{2,1,0:T(8,128)S(1)}, u32[]{:S(2)}, u32[]{:S(2)}) collective-permute-start(f32[18,8,128]{2,1,0:T(8,128)S(1)} %get-tuple-element.122), channel_id=1, source_target_pairs={{0,48},{1,32},{2,33},{3,34},{7,35},{6,39},{5,38},{4,37},{8,36},{9,... | collective-permute-start | bytes 221192 | tf_op jit(solution)/shard_map/ppermute | solution.py:464
  47.2 4.5 %collective-permute-start.14 = (f32[21,8,128]{2,1,0:T(8,128)S(1)}, f32[21,8,128]{2,1,0:T(8,128)S(1)}, u32[]{:S(2)}, u32[]{:S(2)}) collective-permute-start(f32[21,8,128]{2,1,0:T(8,128)S(1)} %get-tuple-element.128), channel_id=1, source_target_pairs={{0,33},{1,34},{2,35},{3,39},{7,38},{6,37},{5,36},{4,40},{8,41},{9,... | collective-permute-start | bytes 258056 | tf_op jit(solution)/shard_map/ppermute | solution.py:464
  48.7 3.7 %collective-permute-start.15 = (f32[12,8,128]{2,1,0:T(8,128)S(1)}, f32[12,8,128]{2,1,0:T(8,128)S(1)}, u32[]{:S(2)}, u32[]{:S(2)}) collective-permute-start(f32[12,8,128]{2,1,0:T(8,128)S(1)} %get-tuple-element.133), channel_id=1, source_target_pairs={{0,48},{1,32},{2,33},{3,34},{7,35},{6,39},{5,38},{4,37},{8,36},{9,... | collective-permute-start | bytes 147464 | tf_op jit(solution)/shard_map/ppermute | solution.py:464
  52.8 4.3 %collective-permute-start.16 = (f32[18,8,128]{2,1,0:T(8,128)S(1)}, f32[18,8,128]{2,1,0:T(8,128)S(1)}, u32[]{:S(2)}, u32[]{:S(2)}) collective-permute-start(f32[18,8,128]{2,1,0:T(8,128)S(1)} %get-tuple-element.140), channel_id=1, source_target_pairs={{0,33},{1,34},{2,35},{3,39},{7,38},{6,37},{5,36},{4,40},{8,41},{9,... | collective-permute-start | bytes 221192 | tf_op jit(solution)/shard_map/ppermute | solution.py:464
  53.6 4.3 %collective-permute-start.17 = (f32[18,8,128]{2,1,0:T(8,128)S(1)}, f32[18,8,128]{2,1,0:T(8,128)S(1)}, u32[]{:S(2)}, u32[]{:S(2)}) collective-permute-start(f32[18,8,128]{2,1,0:T(8,128)S(1)} %get-tuple-element.141), channel_id=1, source_target_pairs={{0,48},{1,32},{2,33},{3,34},{7,35},{6,39},{5,38},{4,37},{8,36},{9,... | collective-permute-start | bytes 221192 | tf_op jit(solution)/shard_map/ppermute | solution.py:464
  58.2 4.6 %collective-permute-start.18 = (f32[21,8,128]{2,1,0:T(8,128)S(1)}, f32[21,8,128]{2,1,0:T(8,128)S(1)}, u32[]{:S(2)}, u32[]{:S(2)}) collective-permute-start(f32[21,8,128]{2,1,0:T(8,128)S(1)} %get-tuple-element.147), channel_id=1, source_target_pairs={{0,33},{1,34},{2,35},{3,39},{7,38},{6,37},{5,36},{4,40},{8,41},{9,... | collective-permute-start | bytes 258056 | tf_op jit(solution)/shard_map/ppermute | solution.py:464
  59.0 3.9 %collective-permute-start.19 = (f32[12,8,128]{2,1,0:T(8,128)S(1)}, f32[12,8,128]{2,1,0:T(8,128)S(1)}, u32[]{:S(2)}, u32[]{:S(2)}) collective-permute-start(f32[12,8,128]{2,1,0:T(8,128)S(1)} %get-tuple-element.152), channel_id=1, source_target_pairs={{0,48},{1,32},{2,33},{3,34},{7,35},{6,39},{5,38},{4,37},{8,36},{9,... | collective-permute-start | bytes 147464 | tf_op jit(solution)/shard_map/ppermute | solution.py:464
  63.3 4.3 %collective-permute-start.20 = (f32[18,8,128]{2,1,0:T(8,128)S(1)}, f32[18,8,128]{2,1,0:T(8,128)S(1)}, u32[]{:S(2)}, u32[]{:S(2)}) collective-permute-start(f32[18,8,128]{2,1,0:T(8,128)S(1)} %get-tuple-element.159), channel_id=1, source_target_pairs={{0,33},{1,34},{2,35},{3,39},{7,38},{6,37},{5,36},{4,40},{8,41},{9,... | collective-permute-start | bytes 221192 | tf_op jit(solution)/shard_map/ppermute | solution.py:464
  64.0 4.1 %collective-permute-start.21 = (f32[18,8,128]{2,1,0:T(8,128)S(1)}, f32[18,8,128]{2,1,0:T(8,128)S(1)}, u32[]{:S(2)}, u32[]{:S(2)}) collective-permute-start(f32[18,8,128]{2,1,0:T(8,128)S(1)} %get-tuple-element.160), channel_id=1, source_target_pairs={{0,48},{1,32},{2,33},{3,34},{7,35},{6,39},{5,38},{4,37},{8,36},{9,... | collective-permute-start | bytes 221192 | tf_op jit(solution)/shard_map/ppermute | solution.py:464
  68.5 3.8 %collective-permute-start.22 = (f32[12,8,128]{2,1,0:T(8,128)S(1)}, f32[12,8,128]{2,1,0:T(8,128)S(1)}, u32[]{:S(2)}, u32[]{:S(2)}) collective-permute-start(f32[12,8,128]{2,1,0:T(8,128)S(1)} %get-tuple-element.164), channel_id=1, source_target_pairs={{0,33},{1,34},{2,35},{3,39},{7,38},{6,37},{5,36},{4,40},{8,41},{9,... | collective-permute-start | bytes 147464 | tf_op jit(solution)/shard_map/ppermute | solution.py:464
  69.3 3.7 %collective-permute-start.23 = (f32[12,8,128]{2,1,0:T(8,128)S(1)}, f32[12,8,128]{2,1,0:T(8,128)S(1)}, u32[]{:S(2)}, u32[]{:S(2)}) collective-permute-start(f32[12,8,128]{2,1,0:T(8,128)S(1)} %get-tuple-element.165), channel_id=1, source_target_pairs={{0,48},{1,32},{2,33},{3,34},{7,35},{6,39},{5,38},{4,37},{8,36},{9,... | collective-permute-start | bytes 147464 | tf_op jit(solution)/shard_map/ppermute | solution.py:464
  73.3 1.4 %collective-permute-start.24 = (f32[24,8,128]{2,1,0:T(8,128)S(1)}, f32[24,8,128]{2,1,0:T(8,128)S(1)}, u32[]{:S(2)}, u32[]{:S(2)}) collective-permute-start(f32[24,8,128]{2,1,0:T(8,128)S(1)} %get-tuple-element.170), channel_id=1, source_target_pairs={{0,32},{1,33},{2,34},{3,35},{7,39},{6,38},{5,37},{4,36},{8,40},{9,... | collective-permute-start | bytes 294920 | tf_op jit(solution)/shard_map/ppermute | solution.py:564
  74.7 15.1 %collective-permute-start.26 = (f32[25,8,128]{2,1,0:T(8,128)S(1)}, f32[25,8,128]{2,1,0:T(8,128)S(1)}, u32[]{:S(2)}, u32[]{:S(2)}) collective-permute-start(f32[25,8,128]{2,1,0:T(8,128)S(1)} %shard_map.101.rest_0_), channel_id=1, source_target_pairs={{0,64},{1,65},{2,66},{3,67},{7,68},{6,69},{5,70},{4,71},{8,72},{9,... | collective-permute-start | bytes 307208 | tf_op jit(solution)/shard_map/ppermute | solution.py:566
  82.0 7.7 %collective-permute-start.25 = (f32[24,8,128]{2,1,0:T(8,128)S(1)}, f32[24,8,128]{2,1,0:T(8,128)S(1)}, u32[]{:S(2)}, u32[]{:S(2)}) collective-permute-start(f32[24,8,128]{2,1,0:T(8,128)S(1)} %shard_map.102), channel_id=1, source_target_pairs={{0,0},{1,1},{2,2},{3,3},{7,4},{6,5},{5,6},{4,7},{8,8},{9,9},{10,10... | collective-permute-start | bytes 294920 | tf_op jit(solution)/shard_map/ppermute | solution.py:568
